TPU v7x, 256 devices: a whole 4x4x8 slice. The times are simulated.
256 devices in a mesh: band: 16 (over x, y), patch: 8 (over z), rep: 2 (over core).
Axes of the slice: x: 4, y: 4, z: 8, core: 2. Of those that a mesh axis runs over, the one named last changes fastest.
Arguments:
- grid_latents: bfloat16 [2, 65536, 512], P('rep', ('band', 'patch')), may hold values from -6 to 6
- mesh_latents: bfloat16 [2, 32768, 512], P('rep', ('band', 'patch')), may hold values from -6 to 6
- weights: bfloat16 [7, 512, 512], replicated, may hold values from -0.25 to 0.25
- target_band: int32 [512, 1], P(('band', 'patch')), may hold values from 0 to 15; in each aligned block of 4 rows (0 to 3, 4 to 7, ...) at most 2 rows name the same one
- target_block: int32 [512], P(('band', 'patch')), may hold values from 0 to 1
- node_slot: int32 [65536], P(('band', 'patch')), may hold values from 0 to 127
- neighbours: int32 [32768, 6], P(('band', 'patch')), may hold values from 0 to 32767, as said below
- mesh_cotangent: bfloat16 [2, 32768, 512], P('rep', ('band', 'patch')), may hold values from -6 to 6
Outputs:
- grid_grad: bfloat16 [2, 65536, 512], P('rep', ('band', 'patch'))
- mesh_grad: bfloat16 [2, 32768, 512], P('rep', ('band', 'patch'))
- weight_grads: float32 [7, 512, 512], P(None, 'band')
Inputs may be any that keep to these rules, and one draw needn't show every extreme that they name: `target_band`: of the 4 grid blocks on one device, at most 2 name the same band, and that many do for some band on some device in every draw. `neighbours`: every neighbour of a mesh node is owned by the node's own device or by one of the two devices next to it in band-then-patch order, wrapping around.
All inputs are finite; a program needn't handle non-finite values.
Results may differ from a plain program's by a relative error of at most 0.022.
Values may be sent and summed in bfloat16 or wider, within the bound.
No kernel may reach another device: no remote copies, remote signals or barrier semaphores. Data moves between devices by JAX's collectives and lax.ppermute only.
A program may use at most 128 MiB of HBM per device.

v0:
```python
import math

import jax
import jax.numpy as jnp
from jax import lax
from jax.sharding import PartitionSpec as P


def with_halo(cells, sides, width):
    for axis, dim in sides:
        count = lax.axis_size(axis)
        head = lax.slice_in_dim(cells, 0, width, axis=dim)
        tail = lax.slice_in_dim(cells, cells.shape[dim] - width, cells.shape[dim], axis=dim)
        cells = jnp.concatenate(
            [
                lax.ppermute(tail, axis, [(i, (i + 1) % count) for i in range(count)]),
                cells,
                lax.ppermute(head, axis, [((i + 1) % count, i) for i in range(count)]),
            ],
            axis=dim,
        )
    return cells


def silu_slope(value):
    sigma = jax.nn.sigmoid(value)
    return sigma * (1.0 + value * (1.0 - sigma))


def matmul(left, right):
    return jnp.dot(left, right, preferred_element_type=jnp.float32)


def body(
    grid_latents,
    mesh_latents,
    weights,
    target_band,
    target_block,
    node_slot,
    neighbours,
    mesh_cotangent,
):
    block_rows = 128
    features = weights.shape[2]
    grid_rows = grid_latents.shape[1]
    blocks = grid_rows // block_rows
    mesh_rows = mesh_latents.shape[1]
    band_count = lax.axis_size("band")
    patches = lax.axis_size("patch")
    replicas = lax.axis_size("rep")
    cycle_size = band_count * patches
    capacity = max(2, 2 * ((blocks + band_count - 1) // band_count))
    slot_count = band_count * capacity
    grid_scale = 1.0 / math.sqrt(replicas * grid_rows * cycle_size)
    mesh_scale = 1.0 / math.sqrt(replicas * mesh_rows * cycle_size)
    inputs = grid_latents[0]
    first_pre = matmul(inputs, weights[0])
    hidden = jax.nn.silu(first_pre).astype(jnp.bfloat16)
    message = matmul(hidden, weights[1]).astype(jnp.bfloat16)
    band_of = target_band[:, 0]
    band_hits = (band_of[:, None] == jnp.arange(band_count, dtype=jnp.int32)[None, :]).astype(
        jnp.int32
    )
    earlier = jnp.cumsum(band_hits, axis=0) - band_hits
    rank_in = jnp.sum(earlier * band_hits, axis=1)
    slot_index = band_of * capacity + rank_in
    send_rows = (
        jnp.zeros((slot_count, block_rows, features), jnp.bfloat16)
        .at[slot_index]
        .set(message.reshape(blocks, block_rows, features))
    )
    node_ids = target_block[:, None] * block_rows + node_slot.reshape(blocks, block_rows)
    send_ids = jnp.full((slot_count, block_rows), mesh_rows, jnp.int32).at[slot_index].set(node_ids)
    got_rows, got_ids = (
        lax.all_to_all(send_rows, "band", split_axis=0, concat_axis=0, tiled=True),
        lax.all_to_all(send_ids, "band", split_axis=0, concat_axis=0, tiled=True),
    )
    flat_ids = got_ids.reshape(slot_count * block_rows)
    selector = (jnp.arange(mesh_rows, dtype=jnp.int32)[:, None] == flat_ids[None, :]).astype(
        jnp.bfloat16
    )
    aggregate = matmul(selector, got_rows.reshape(slot_count * block_rows, features))
    aggregate_b = aggregate.astype(jnp.bfloat16)
    second = matmul(aggregate_b, weights[2])
    squashed = jax.nn.silu(second).astype(jnp.bfloat16)
    latent = mesh_latents[0].astype(jnp.float32) + matmul(squashed, weights[3])
    latent_b = latent.astype(jnp.bfloat16)
    position = lax.axis_index("band") * patches + lax.axis_index("patch")
    owner_dev = neighbours // mesh_rows
    offset = jnp.mod(owner_dev - position + 1, cycle_size)
    local_rows = offset * mesh_rows + jnp.mod(neighbours, mesh_rows)
    padded = with_halo(latent_b, ((("band", "patch"), 0),), mesh_rows)
    sender = matmul(padded, weights[4])
    receiver = matmul(latent_b, weights[5])
    degree = neighbours.shape[1]
    summed = jnp.zeros((mesh_rows, features), jnp.float32)
    for column in range(degree):
        pre_act = jnp.take(sender, local_rows[:, column], axis=0) + receiver
        summed = summed + jax.nn.silu(pre_act)
    summed_b = summed.astype(jnp.bfloat16)
    cotangent = mesh_cotangent[0]
    grad_out_w = matmul(summed_b.T, cotangent)
    grad_summed = matmul(cotangent, weights[6].T)
    grad_recv = jnp.zeros((mesh_rows, features), jnp.float32)
    grad_pad = jnp.zeros((3 * mesh_rows, features), jnp.float32)
    for column in range(degree):
        edge_rows = local_rows[:, column]
        pre_act = jnp.take(sender, edge_rows, axis=0) + receiver
        edge_grad = lax.optimization_barrier(
            (grad_summed * silu_slope(pre_act)).astype(jnp.bfloat16)
        ).astype(jnp.float32)
        grad_recv = grad_recv + edge_grad
        grad_pad = grad_pad + jax.ops.segment_sum(edge_grad, edge_rows, num_segments=3 * mesh_rows)
    outer_grads = jnp.concatenate([grad_pad[:mesh_rows], grad_pad[2 * mesh_rows :]], axis=0)
    returned = with_halo(outer_grads, ((("band", "patch"), 0),), mesh_rows)
    grad_send = (
        grad_pad[mesh_rows : 2 * mesh_rows] + returned[:mesh_rows] + returned[3 * mesh_rows :]
    )
    grad_send_b = grad_send.astype(jnp.bfloat16)
    grad_recv_b = grad_recv.astype(jnp.bfloat16)
    grad_ws = matmul(latent_b.T, grad_send_b)
    grad_wr = matmul(latent_b.T, grad_recv_b)
    grad_latent = (
        cotangent.astype(jnp.float32)
        + matmul(grad_send_b, weights[4].T)
        + matmul(grad_recv_b, weights[5].T)
    )
    grad_latent_b = grad_latent.astype(jnp.bfloat16)
    grad_wo = matmul(squashed.T, grad_latent_b)
    grad_squashed = matmul(grad_latent_b, weights[3].T)
    grad_second = (grad_squashed * silu_slope(second)).astype(jnp.bfloat16)
    grad_wa = matmul(aggregate_b.T, grad_second)
    grad_aggregate = matmul(grad_second, weights[2].T).astype(jnp.bfloat16)
    outgoing = jnp.take(grad_aggregate, got_ids, axis=0, mode="fill", fill_value=0)
    incoming = lax.all_to_all(outgoing, "band", split_axis=0, concat_axis=0, tiled=True)
    grad_message = jnp.take(incoming, slot_index, axis=0).reshape(grid_rows, features)
    grad_w2 = matmul(hidden.T, grad_message)
    grad_hidden = matmul(grad_message, weights[1].T)
    grad_first = (grad_hidden * silu_slope(first_pre)).astype(jnp.bfloat16)
    grad_w1 = matmul(inputs.T, grad_first)
    grid_grad = matmul(grad_first, weights[0].T).astype(jnp.bfloat16)
    partials = jnp.stack(
        [
            grad_w1 * grid_scale,
            grad_w2 * grid_scale,
            grad_wa * mesh_scale,
            grad_wo * mesh_scale,
            grad_ws * mesh_scale,
            grad_wr * mesh_scale,
            grad_out_w * mesh_scale,
        ]
    )
    summed_grads = lax.psum(partials, ("band", "patch", "rep"))
    share = features // band_count
    weight_part = lax.dynamic_slice_in_dim(summed_grads, lax.axis_index("band") * share, share, 1)
    return (grid_grad[None], grad_latent_b[None], weight_part)


def solution(mesh):
    return jax.shard_map(
        body,
        mesh=mesh,
        in_specs=(
            P("rep", ("band", "patch"), None),
            P("rep", ("band", "patch"), None),
            P(),
            P(("band", "patch"), None),
            P(("band", "patch")),
            P(("band", "patch")),
            P(("band", "patch"), None),
            P("rep", ("band", "patch"), None),
        ),
        out_specs=(
            P("rep", ("band", "patch"), None),
            P("rep", ("band", "patch"), None),
            P(None, "band", None),
        ),
        check_vma=False,
    )
```

profile of v0, /device:TPU:1, one launch (start us, length us, event | category | flops | bytes accessed | tf_op | source)
XLA Modules:
  0.0 547.7 jit_solution(8683566623285331115)
XLA Ops:
  11.5 7.6 %all-to-all-start = ((s32[16,2,128]{2,1,0:T(2,128)}), s32[16,2,128]{2,1,0:T(2,128)S(1)}, u32[]{:S(2)}, u32[]{:S(2)}) async-start(s32[16,2,128]{2,1,0:T(2,128)} %bitcast.5), calls=%async_computation | async-start | bytes 32768 | tf_op jit(solution)/shard_map/all_to_all | solution.py:77
  23.1 2.5 broadcast_in_dim.57
  25.6 2.5 scatter_fusion
  28.1 6.8 %all-to-all-start.1 = ((bf16[32,128,512]{2,1,0:T(8,128)(2,1)}), bf16[32,128,512]{2,1,0:T(8,128)(2,1)}, u32[]{:S(2)}, u32[]{:S(2)}) async-start(bf16[32,128,512]{2,1,0:T(8,128)(2,1)} %scatter_fusion), calls=%async_computation.1 | async-start | bytes 8388608 | tf_op jit(solution)/shard_map/all_to_all | solution.py:76
  35.2 51.6 %all-to-all-done.1 = bf16[32,128,512]{2,1,0:T(8,128)(2,1)} async-done(((bf16[32,128,512]{2,1,0:T(8,128)(2,1)}), bf16[32,128,512]{2,1,0:T(8,128)(2,1)}, u32[]{:S(2)}, u32[]{:S(2)}) %all-to-all-start.1) | async-done | bytes 4194336 | tf_op jit(solution)/shard_map/all_to_all | solution.py:76
  86.8 3.6 fusion.22
  91.1 7.9 %collective-permute-start.1 = (bf16[256,512]{1,0:T(8,128)(2,1)S(1)}, bf16[256,512]{1,0:T(8,128)(2,1)S(1)}, u32[]{:S(2)}, u32[]{:S(2)}) collective-permute-start(bf16[256,512]{1,0:T(8,128)(2,1)S(1)} %fusion.20), channel_id=1, source_target_pairs={{2,0},{4,2},{6,4},{8,6},{10,8},{12,10},{14,12},{16,14},{18,16},{20... | collective-permute-start | bytes 786440 | tf_op jit(solution)/shard_map/ppermute | solution.py:18
  100.1 2.2 collective-permute-done.1
  102.3 7.3 %collective-permute-done = bf16[256,512]{1,0:T(8,128)(2,1)S(1)} collective-permute-done((bf16[256,512]{1,0:T(8,128)(2,1)S(1)}, bf16[256,512]{1,0:T(8,128)(2,1)S(1)}, u32[]{:S(2)}, u32[]{:S(2)}) %collective-permute-start) | collective-permute-done | bytes 262176 | tf_op jit(solution)/shard_map/ppermute | solution.py:16
  112.1 1.8 gather_fusion.5
  113.9 1.8 gather_fusion.4
  115.7 1.8 gather_fusion.3
  117.5 1.8 gather_fusion.2
  119.2 3.2 multiply_convert_fusion.6
  125.0 3.3 scatter_custom_fusion.3
  128.3 3.3 scatter_custom_fusion.5
  131.7 4.0 scatter_custom_fusion.2
  135.7 3.0 add.251
  138.7 6.3 %scatter_custom_fusion.4 = f32[768,512]{1,0:T(8,128)} fusion(f32[768,512]{1,0:T(8,128)} %add.251, s32[512]{0:T(512)S(1)} %bitcast.166, f32[256,512]{1,0:T(8,128)S(1)} %copy-done.3, f32[]{:T(128)} %constant.137, f32[256,512]{1,0:T(8,128)S(1)} %copy-done.2), kind=kCustom, calls=%fused_computation.57 | custom fusion | flops 524288 | bytes 2621952 | tf_op jit(solution)/shard_map/add | solution.py:114
  145.1 1.9 add.262
  147.2 6.9 %collective-permute-start.3 = (f32[256,512]{1,0:T(8,128)S(1)}, f32[256,512]{1,0:T(8,128)S(1)}, u32[]{:S(2)}, u32[]{:S(2)}) collective-permute-start(f32[256,512]{1,0:T(8,128)S(1)} %get-tuple-element.13), channel_id=1, source_target_pairs={{2,0},{4,2},{6,4},{8,6},{10,8},{12,10},{14,12},{16,14},{18,16},{20... | collective-permute-start | bytes 1572872 | tf_op jit(solution)/shard_map/ppermute | solution.py:18
  154.7 6.3 %collective-permute-done.2 = f32[256,512]{1,0:T(8,128)S(1)} collective-permute-done((f32[256,512]{1,0:T(8,128)S(1)}, f32[256,512]{1,0:T(8,128)S(1)}, u32[]{:S(2)}, u32[]{:S(2)}) %collective-permute-start.2) | collective-permute-done | bytes 524320 | tf_op jit(solution)/shard_map/ppermute | solution.py:16
  162.6 17.3 %gather_fusion = bf16[4096,512]{1,0:T(8,128)(2,1)} fusion(bf16[256,512]{1,0:T(8,128)(2,1)S(1)} %convolution_convert_fusion.2, s32[4096]{0:T(1024)S(1)} %fusion.86), kind=kCustom, calls=%fused_computation.6 | custom fusion | bytes 8404992 | tf_op jit(solution)/shard_map/jit(_take)/gather | solution.py:135
  179.9 3.9 broadcast_select_fusion
  183.8 9.2 %all-to-all-start.2 = ((bf16[32,128,512]{2,1,0:T(8,128)(2,1)}), bf16[32,128,512]{2,1,0:T(8,128)(2,1)}, u32[]{:S(2)}, u32[]{:S(2)}) async-start(bf16[32,128,512]{2,1,0:T(8,128)(2,1)} %broadcast_select_fusion), calls=%async_computation.2 | async-start | bytes 8388608 | tf_op jit(solution)/shard_map/all_to_all | solution.py:136
  193.2 46.7 %all-to-all-done.2 = bf16[32,128,512]{2,1,0:T(8,128)(2,1)} async-done(((bf16[32,128,512]{2,1,0:T(8,128)(2,1)}), bf16[32,128,512]{2,1,0:T(8,128)(2,1)}, u32[]{:S(2)}, u32[]{:S(2)}) %all-to-all-start.2) | async-done | bytes 4194336 | tf_op jit(solution)/shard_map/all_to_all | solution.py:136
  239.9 2.8 gather_fusion.1
  242.9 1.7 fusion.16
  253.3 2.3 fusion.7
  255.6 2.3 fusion.17
  257.9 279.6 %all-reduce.2.cloned.1.call-done = f32[7,512,512]{1,2,0:T(8,128)} async-done(((f32[7,512,512]{1,2,0:T(8,128)}), f32[7,512,512]{1,2,0:T(8,128)}) %all-reduce.2.cloned.1.call-update) | async-done | bytes 7340048 | tf_op jit(solution)/shard_map/psum | solution.py:154
  537.5 2.0 constant_dynamic-slice_fusion
  (143 shorter events, 27.7 us)
Async XLA Ops:
  7.2 12.0 %copy-start = (bf16[1,512,512]{2,1,0:T(8,128)(2,1)S(1)}, bf16[1,512,512]{2,1,0:T(8,128)(2,1)}, u32[]{:S(2)}) copy-start(bf16[1,512,512]{2,1,0:T(8,128)(2,1)} %param.10) | copy-start | bytes 1572868
  11.5 16.6 %all-to-all-start = ((s32[16,2,128]{2,1,0:T(2,128)}), s32[16,2,128]{2,1,0:T(2,128)S(1)}, u32[]{:S(2)}, u32[]{:S(2)}) async-start(s32[16,2,128]{2,1,0:T(2,128)} %bitcast.5), calls=%async_computation | async-start | bytes 32768 | tf_op jit(solution)/shard_map/all_to_all | solution.py:77
  28.1 6.8 %copy-start.40 = (s32[256,6]{0,1:T(8,128)S(1)}, s32[256,6]{0,1:T(8,128)}, u32[]{:S(2)}) copy-start(s32[256,6]{0,1:T(8,128)} %param.16) | copy-start | bytes 18436
  28.1 58.7 %all-to-all-start.1 = ((bf16[32,128,512]{2,1,0:T(8,128)(2,1)}), bf16[32,128,512]{2,1,0:T(8,128)(2,1)}, u32[]{:S(2)}, u32[]{:S(2)}) async-start(bf16[32,128,512]{2,1,0:T(8,128)(2,1)} %scatter_fusion), calls=%async_computation.1 | async-start | bytes 8388608 | tf_op jit(solution)/shard_map/all_to_all | solution.py:76
  90.4 19.8 %copy-start.16 = (bf16[256,512]{1,0:T(8,128)(2,1)}, bf16[256,512]{1,0:T(8,128)(2,1)S(1)}, u32[]{:S(2)}) copy-start(bf16[256,512]{1,0:T(8,128)(2,1)S(1)} %fusion.22) | copy-start | bytes 786436
  90.7 11.6 %copy-start.31 = (f32[256,512]{1,0:T(8,128)}, f32[256,512]{1,0:T(8,128)S(1)}, u32[]{:S(2)}) copy-start(f32[256,512]{1,0:T(8,128)S(1)} %fusion.58) | copy-start | bytes 1572868
  91.1 11.2 %collective-permute-start.1 = (bf16[256,512]{1,0:T(8,128)(2,1)S(1)}, bf16[256,512]{1,0:T(8,128)(2,1)S(1)}, u32[]{:S(2)}, u32[]{:S(2)}) collective-permute-start(bf16[256,512]{1,0:T(8,128)(2,1)S(1)} %fusion.20), channel_id=1, source_target_pairs={{2,0},{4,2},{6,4},{8,6},{10,8},{12,10},{14,12},{16,14},{18,16},{20... | collective-permute-start | bytes 786440 | tf_op jit(solution)/shard_map/ppermute | solution.py:18
  98.9 10.7 %collective-permute-start = (bf16[256,512]{1,0:T(8,128)(2,1)S(1)}, bf16[256,512]{1,0:T(8,128)(2,1)S(1)}, u32[]{:S(2)}, u32[]{:S(2)}) collective-permute-start(bf16[256,512]{1,0:T(8,128)(2,1)S(1)} %fusion.20), channel_id=1, source_target_pairs={{0,2},{2,4},{4,6},{6,8},{8,10},{10,12},{12,14},{14,16},{16,18},{18... | collective-permute-start | bytes 786440 | tf_op jit(solution)/shard_map/ppermute | solution.py:16
  111.1 8.1 %copy-start.22 = (f32[256,512]{1,0:T(8,128)}, f32[256,512]{1,0:T(8,128)S(1)}, u32[]{:S(2)}) copy-start(f32[256,512]{1,0:T(8,128)S(1)} %gather_fusion.7) | copy-start | bytes 1572868
  112.1 7.1 %copy-start.24 = (f32[256,512]{1,0:T(8,128)}, f32[256,512]{1,0:T(8,128)S(1)}, u32[]{:S(2)}) copy-start(f32[256,512]{1,0:T(8,128)S(1)} %gather_fusion.6) | copy-start | bytes 1572868
  122.5 9.2 %copy-start.18 = (bf16[256,512]{1,0:T(8,128)(2,1)}, bf16[256,512]{1,0:T(8,128)(2,1)S(1)}, u32[]{:S(2)}) copy-start(bf16[256,512]{1,0:T(8,128)(2,1)S(1)} %get-tuple-element.15) | copy-start | bytes 786436
  122.5 9.2 %copy-start.20 = (bf16[256,512]{1,0:T(8,128)(2,1)}, bf16[256,512]{1,0:T(8,128)(2,1)S(1)}, u32[]{:S(2)}) copy-start(bf16[256,512]{1,0:T(8,128)(2,1)S(1)} %get-tuple-element.18) | copy-start | bytes 786436
  138.7 6.3 %copy-start.1 = (f32[768,512]{1,0:T(8,128)S(1)}, f32[768,512]{1,0:T(8,128)}, u32[]{:S(2)}) copy-start(f32[768,512]{1,0:T(8,128)} %scatter_custom_fusion.5) | copy-start | bytes 4718596
  145.0 9.1 %copy-start.7 = (bf16[256,512]{1,0:T(8,128)(2,1)S(1)}, bf16[256,512]{1,0:T(8,128)(2,1)}, u32[]{:S(2)}) copy-start(bf16[256,512]{1,0:T(8,128)(2,1)} %copy-done.6) | copy-start | bytes 786436
  145.0 9.1 %copy-start.9 = (bf16[256,512]{1,0:T(8,128)(2,1)S(1)}, bf16[256,512]{1,0:T(8,128)(2,1)}, u32[]{:S(2)}) copy-start(bf16[256,512]{1,0:T(8,128)(2,1)} %copy-done.8) | copy-start | bytes 786436
  145.0 9.1 %copy-start.11 = (bf16[256,512]{1,0:T(8,128)(2,1)S(1)}, bf16[256,512]{1,0:T(8,128)(2,1)}, u32[]{:S(2)}) copy-start(bf16[256,512]{1,0:T(8,128)(2,1)} %copy-done.10) | copy-start | bytes 786436
  145.0 9.0 %copy-start.13 = (bf16[256,512]{1,0:T(8,128)(2,1)S(1)}, bf16[256,512]{1,0:T(8,128)(2,1)}, u32[]{:S(2)}) copy-start(bf16[256,512]{1,0:T(8,128)(2,1)} %copy-done.12) | copy-start | bytes 786436
  145.0 9.0 %copy-start.19 = (bf16[256,512]{1,0:T(8,128)(2,1)S(1)}, bf16[256,512]{1,0:T(8,128)(2,1)}, u32[]{:S(2)}) copy-start(bf16[256,512]{1,0:T(8,128)(2,1)} %copy-done.18) | copy-start | bytes 786436
  145.1 9.0 %copy-start.21 = (bf16[256,512]{1,0:T(8,128)(2,1)S(1)}, bf16[256,512]{1,0:T(8,128)(2,1)}, u32[]{:S(2)}) copy-start(bf16[256,512]{1,0:T(8,128)(2,1)} %copy-done.20) | copy-start | bytes 786436
  145.1 9.3 %copy-start.5 = (bf16[7,512,512]{2,1,0:T(8,128)(2,1)S(1)}, bf16[7,512,512]{2,1,0:T(8,128)(2,1)}, u32[]{:S(2)}) copy-start(bf16[7,512,512]{2,1,0:T(8,128)(2,1)} %param.12) | copy-start | bytes 11010052
  147.0 14.2 %copy-start.34 = (bf16[1,256,512]{2,1,0:T(8,128)(2,1)S(1)}, bf16[1,256,512]{2,1,0:T(8,128)(2,1)}, u32[]{:S(2)}) copy-start(bf16[1,256,512]{2,1,0:T(8,128)(2,1)} %param.17) | copy-start | bytes 786436
  147.1 14.5 %copy-start.32 = (f32[256,512]{1,0:T(8,128)S(1)}, f32[256,512]{1,0:T(8,128)}, u32[]{:S(2)}) copy-start(f32[256,512]{1,0:T(8,128)} %copy-done.31) | copy-start | bytes 1572868
  147.1 13.9 %collective-permute-start.2 = (f32[256,512]{1,0:T(8,128)S(1)}, f32[256,512]{1,0:T(8,128)S(1)}, u32[]{:S(2)}, u32[]{:S(2)}) collective-permute-start(f32[256,512]{1,0:T(8,128)S(1)} %get-tuple-element.12), channel_id=1, source_target_pairs={{0,2},{2,4},{4,6},{6,8},{8,10},{10,12},{12,14},{14,16},{16,18},{18... | collective-permute-start | bytes 1572872 | tf_op jit(solution)/shard_map/ppermute | solution.py:16
  147.2 13.8 %collective-permute-start.3 = (f32[256,512]{1,0:T(8,128)S(1)}, f32[256,512]{1,0:T(8,128)S(1)}, u32[]{:S(2)}, u32[]{:S(2)}) collective-permute-start(f32[256,512]{1,0:T(8,128)S(1)} %get-tuple-element.13), channel_id=1, source_target_pairs={{2,0},{4,2},{6,4},{8,6},{10,8},{12,10},{14,12},{16,14},{18,16},{20... | collective-permute-start | bytes 1572872 | tf_op jit(solution)/shard_map/ppermute | solution.py:18
  162.3 17.7 %copy-start.38 = (bf16[256,512]{1,0:T(8,128)(2,1)}, bf16[256,512]{1,0:T(8,128)(2,1)S(1)}, u32[]{:S(2)}) copy-start(bf16[256,512]{1,0:T(8,128)(2,1)S(1)} %fusion.21) | copy-start | bytes 786436
  183.8 59.1 %copy-start.15 = (f32[512,512]{1,0:T(8,128)S(1)}, f32[512,512]{1,0:T(8,128)}, u32[]{:S(2)}) copy-start(f32[512,512]{1,0:T(8,128)} %copy-done.14) | copy-start | bytes 3145732
  183.8 56.0 %all-to-all-start.2 = ((bf16[32,128,512]{2,1,0:T(8,128)(2,1)}), bf16[32,128,512]{2,1,0:T(8,128)(2,1)}, u32[]{:S(2)}, u32[]{:S(2)}) async-start(bf16[32,128,512]{2,1,0:T(8,128)(2,1)} %broadcast_select_fusion), calls=%async_computation.2 | async-start | bytes 8388608 | tf_op jit(solution)/shard_map/all_to_all | solution.py:136
  193.0 344.5 %all-reduce.2.cloned.1.call-start = ((), (), s32[]{:S(2)}) async-start(), calls=%async_computation.3 | async-start | bytes 14680064 | tf_op jit(solution)/shard_map/psum | solution.py:154
  247.8 5.5 copy-start.23
  247.8 5.5 %copy-start.25 = (f32[256,512]{1,0:T(8,128)S(1)}, f32[256,512]{1,0:T(8,128)}, u32[]{:S(2)}) copy-start(f32[256,512]{1,0:T(8,128)} %copy-done.24) | copy-start | bytes 1572868
  247.8 5.5 copy-start.26
  247.8 5.5 copy-start.27
  (18 other events, 54.1 us)
Sparse Core Ops, SparseCore 0:
  255.7 281.7 all-reduce.1
where the time goes:
time: 549 us; the launch traced here: 548 us
  waiting for transfers between devices  394 us (72%)
  local copies, waits for them, and re-layouts  39.7 us (7%)
  starting transfers between devices  38.4 us (7%)
  other arithmetic  32.7 us (6%)
  matrix products  28.2 us (5%)
  between operations  14.8 us (3%)
    psum x1, waiting for transfers between devices, body(): summed_grads = lax.psum(partials, ('band', 'patch', 'rep'))  280 us
    all_to_all x1, waiting for transfers between devices, body(): lax.all_to_all(send_rows, 'band', split_axis=0, concat_axis=0, tiled=True)  51.6 us
    all_to_all x1, waiting for transfers between devices, body(): lax.all_to_all(outgoing, 'band', split_axis=0, concat_axis=0, tiled=True)  46.7 us
    dot_general x21, matrix products, matmul(): return jnp.dot(left, right, preferred_element_type=jnp.float32)  28.2 us
    gather x1, local copies, waits for them, and re-layouts, body(): jnp.take(grad_aggregate, got_ids, axis=0, mode='fill', fill_value=0)  17.3 us
    add x4, other arithmetic, body(): grad_pad + jax.ops.segment_sum(edge_grad, edge_rows, num_segments=3 * mes...  15.2 us
    ppermute x2, starting transfers between devices, with_halo(): lax.ppermute(head, axis, [((i + 1) % count, i) for i in range(count)])  14.8 us
    ppermute x2, waiting for transfers between devices, with_halo(): lax.ppermute(tail, axis, [(i, (i + 1) % count) for i in range(count)])  13.7 us
  transfers between devices with their start and end apart: 8, of which 6 were waited for; matrix products, arithmetic and copies ran while one was open for 2% of the time, Pallas kernels for 0%

commit v1 on v0

v1 whole, which is shorter than its diff:
```python
import math

import jax
import jax.numpy as jnp
from jax import lax
from jax.experimental import pallas as pl
from jax.experimental.pallas import tpu as pltpu
from jax.sharding import PartitionSpec as P

F32 = jnp.float32
BF16 = jnp.bfloat16
I32 = jnp.int32
ALL = ("band", "patch", "rep")
NX, NY, NZ, NR = 4, 4, 8, 2
LAT = 512
BLK = 128
GB = 4
MESH = 256
K = 6
META = 16
VMEM = pl.BlockSpec(memory_space=pltpu.VMEM)
SMEM = pl.BlockSpec(memory_space=pltpu.SMEM)


def nn(a, b):
    return lax.dot_general(a, b, (((1,), (0,)), ((), ())), preferred_element_type=F32)


def nt(a, b):
    return lax.dot_general(a, b, (((1,), (1,)), ((), ())), preferred_element_type=F32)


def tn(a, b):
    return lax.dot_general(a, b, (((0,), (0,)), ((), ())), preferred_element_type=F32)


def sigmoid(v):
    return 0.5 * jnp.tanh(0.5 * v) + 0.5


def call(kernel, ins, outs, scratch=(), flops=0, limit=40):
    specs_in = [SMEM if s else VMEM for _, s in ins]
    out_shape = [jax.ShapeDtypeStruct(shape, dtype) for shape, dtype, _ in outs]
    specs_out = [SMEM if s else VMEM for _, _, s in outs]
    return pl.pallas_call(
        kernel,
        out_shape=out_shape,
        in_specs=specs_in,
        out_specs=specs_out,
        scratch_shapes=list(scratch),
        compiler_params=pltpu.CompilerParams(vmem_limit_bytes=limit * 1024 * 1024),
        cost_estimate=pl.CostEstimate(flops=flops, bytes_accessed=1000000, transcendentals=0),
    )(*[a for a, _ in ins])


def device(x, y, z, r):
    return ((x * NY + y) * NZ + z) * NR + r


def shifts(k, flip):
    pairs = []
    for x in range(NX):
        for y in range(NY):
            for z in range(NZ):
                for r in range(NR):
                    along_x = (r == 0) != flip
                    to = device((x + k) % NX, y, z, r) if along_x else device(x, (y + k) % NY, z, r)
                    pairs.append((device(x, y, z, r), to))
    return pairs


def first(v, k):
    return lax.ppermute(v, ALL, shifts(k, False))


def second(v, k):
    return lax.ppermute(v, ALL, shifts(k, True))


def split_code(code, rep):
    t = lax.shift_right_logical(code, 1)
    tx = lax.shift_right_logical(t, 2)
    ty = t & 3
    d1 = jnp.where(rep == 0, tx, ty)
    d2 = jnp.where(rep == 0, ty, tx)
    return d1, d2, code & 1


def grid_forward(codes, x, w, slot, out, slope):
    row = lax.broadcasted_iota(I32, (BLK, BLK), 0)
    for g in range(GB):
        rows = pl.ds(g * BLK, BLK)
        v = nn(x[rows, :], w[...])
        sg = sigmoid(v)
        h = v * sg
        slope[rows, :] = (sg + h * (1.0 - sg)).astype(BF16)
        pick = jnp.where(row == slot[g : g + 1, :], 1.0, 0.0).astype(BF16)
        out[rows, :] = nn(pick, h.astype(BF16)).astype(BF16)
    meta_row = lax.broadcasted_iota(I32, (META, LAT), 0)
    meta = jnp.zeros((META, LAT), F32)
    for g in range(GB):
        meta = jnp.where(meta_row == g, codes[g].astype(F32), meta)
    out[pl.ds(GB * BLK, META), :] = meta.astype(BF16)


def route_sum(pos, p0, p1, p2, p3, q0, q1, q2, q3, table, acc):
    acc[...] = jnp.zeros_like(acc)
    own1, own2, rep = pos[0], pos[1], pos[2]
    for j, p in enumerate((p0, p1, p2, p3)):
        meta = p[pl.ds(GB * BLK, META), :].astype(F32)
        for i in range(GB):
            code = jnp.max(meta[i : i + 1, 0:128]).astype(I32)
            table[j * GB + i] = code
            d1, d2, blk = split_code(code, rep)
            slot = ((d2 - own2) & 3) * 2 + blk

            @pl.when(d1 == own1)
            def _():
                acc[slot] += p[pl.ds(i * BLK, BLK), :].astype(F32)

    for k, q in enumerate((q0, q1, q2, q3)):
        for b in range(2):
            q[pl.ds(b * BLK, BLK), :] = acc[2 * k + b].astype(q.dtype)


def mesh_forward(q0, r1, r2, r3, ml, w1, w2, w3, ah, agg, sq, slope, lat):
    total = q0[...] + r1[...].astype(F32) + r2[...].astype(F32) + r3[...].astype(F32)
    ah[...] = total.astype(BF16)
    agg[...] = nn(ah[...], w1[...]).astype(BF16)
    v = nn(agg[...], w2[...])
    sg = sigmoid(v)
    s = v * sg
    slope[...] = (sg + s * (1.0 - sg)).astype(BF16)
    sq[...] = s.astype(BF16)
    lat[...] = (ml[...].astype(F32) + nn(sq[...], w3[...])).astype(BF16)


def own_tables(lat, w4, w5, snd, rcv):
    snd[...] = nn(lat[...], w4[...]).astype(BF16)
    rcv[...] = nn(lat[...], w5[...])


def cot_tables(cot, cp, cn, w6, gs):
    for j, c in enumerate((cp, cot, cn)):
        gs[pl.ds(j * MESH, MESH), :] = nt(c[pl.ds(0, MESH), :], w6[...])


def edges_backward(
    lp, ln, snd, rcv, col, row, cp, cn, gs, cot, slope2, w1, w2, w3, w4, w5,
    summed_b, gsend_b, grecv_b, gl_b, gsec_b, ga_b, gm_b,
    table, srcv, ecol, e, gsend,
):
    table[pl.ds(MESH, MESH), :] = snd[...]
    table[pl.ds(0, MESH), :] = nn(lp[...], w4[...]).astype(BF16)
    table[pl.ds(2 * MESH, MESH), :] = nn(ln[...], w4[...]).astype(BF16)
    srcv[pl.ds(0, MESH), :] = nn(lp[...], w5[...])
    srcv[pl.ds(MESH, MESH), :] = nn(ln[...], w5[...])
    half = 128
    lane = lax.broadcasted_iota(I32, (half, 3 * MESH), 1)
    for m in range(2):
        rows = pl.ds(m * half, half)
        total = jnp.zeros((half, LAT), F32)
        recv = jnp.zeros((half, LAT), F32)
        for k in range(K):
            pick = jnp.where(lane == col[rows, k : k + 1], 1.0, 0.0).astype(BF16)
            v = nn(pick, table[...]) + rcv[rows, :]
            sg = sigmoid(v)
            s = v * sg
            total = total + s
            eg = (gs[pl.ds(MESH + m * half, half), :] * (sg + s * (1.0 - sg))).astype(BF16)
            recv = recv + eg.astype(F32)
            e[pl.ds(k * MESH + m * half, half), :] = eg
        summed_b[rows, :] = total.astype(BF16)
        grecv_b[rows, :] = recv.astype(BF16)
    own = lax.broadcasted_iota(I32, (MESH, MESH), 0)
    acc = jnp.zeros((MESH, LAT), F32)
    for k in range(K):
        pick = jnp.where(own + MESH == row[k : k + 1, :], 1.0, 0.0).astype(BF16)
        acc = acc + nn(pick, e[pl.ds(k * MESH, MESH), :])
    gsend[...] = acc
    lane2 = lax.broadcasted_iota(I32, (half, MESH), 1).astype(F32)
    ownf = own.astype(F32)
    for side, c in enumerate((cp, cn)):
        codes = c[pl.ds(MESH, META), 0:MESH].astype(F32)
        ecol[...] = jnp.transpose(codes)
        for k in range(K):
            for m in range(2):
                rows = pl.ds(m * half, half)
                pick = jnp.where(lane2 == ecol[rows, k : k + 1], 1.0, 0.0).astype(BF16)
                v = nn(pick, table[pl.ds(MESH, MESH), :]) + srcv[pl.ds(side * MESH + m * half, half), :]
                sg = sigmoid(v)
                s = v * sg
                g = gs[pl.ds(2 * side * MESH + m * half, half), :]
                e[pl.ds(k * MESH + m * half, half), :] = (g * (sg + s * (1.0 - sg))).astype(BF16)
        acc = gsend[...]
        for k in range(K):
            pick = jnp.where(ownf == codes[k : k + 1, :], 1.0, 0.0).astype(BF16)
            acc = acc + nn(pick, e[pl.ds(k * MESH, MESH), :])
        gsend[...] = acc
    gsend_b[...] = gsend[...].astype(BF16)
    gl = cot[...].astype(F32) + nt(gsend_b[...], w4[...]) + nt(grecv_b[...], w5[...])
    gl_b[...] = gl.astype(BF16)
    gsec_b[...] = (nt(gl_b[...], w3[...]) * slope2[...].astype(F32)).astype(BF16)
    ga_b[...] = nt(gsec_b[...], w2[...]).astype(BF16)
    gm_b[...] = nt(ga_b[...], w1[...]).astype(BF16)


def mesh_weights(pos, ah, agg, sq, lat, summed, ga, gsec, gl, gsend, grecv, cot, keep, give):
    rep = pos[2]
    pairs = ((ah, ga), (agg, gsec), (sq, gl), (lat, gsend), (lat, grecv), (summed, cot))
    for w, (left, right) in enumerate(pairs):
        for out, h in ((keep, rep), (give, 1 - rep)):
            cols = pl.ds(pl.multiple_of(h * 256, 256), 256)
            part = tn(left[...], right[:, cols]).astype(BF16)
            for t in range(2):
                q, at = (2 * w + t) // 3, (2 * w + t) % 3
                for c in range(2):
                    for b in range(16):
                        out[c * 4 + q, pl.ds(b * 48 + at * 16, 16), :] = part[
                            b * 32 + t * 16 : b * 32 + t * 16 + 16, c * 128 : c * 128 + 128
                        ]


def return_pick(pos, table, g0, g1, g2, g3, r0, r1, r2, r3):
    own1, own2, rep = pos[0], pos[1], pos[2]
    sources = (g0, g1, g2, g3)
    for k, r in enumerate((r0, r1, r2, r3)):
        j = (4 - k) % 4
        for i in range(GB):
            d1, d2, blk = split_code(table[j * GB + i], rep)
            at = (own2 - d2) & 3
            for n in range(4):

                @pl.when((d1 == own1) & (at == n))
                def _():
                    start = pl.multiple_of(blk * BLK, BLK)
                    r[pl.ds(i * BLK, BLK), :] = sources[n][pl.ds(start, BLK), :]


def grid_backward(pos, codes, r0, r1, r2, r3, x, slot, slope, gf, part, picked):
    own1, rep = pos[0], pos[2]
    row = lax.broadcasted_iota(I32, (BLK, BLK), 0)
    for i in range(GB):
        d1, _, _ = split_code(codes[i], rep)
        at = (own1 - d1) & 3
        rows = pl.ds(i * BLK, BLK)
        for n, r in enumerate((r0, r1, r2, r3)):

            @pl.when(at == n)
            def _():
                picked[rows, :] = r[rows, :]

    for i in range(GB):
        rows = pl.ds(i * BLK, BLK)
        pick = jnp.where(row == slot[i : i + 1, :], 1.0, 0.0).astype(BF16)
        gf[rows, :] = (tn(pick, picked[rows, :]) * slope[rows, :].astype(F32)).astype(BF16)
    w = tn(x[...], gf[...]).astype(BF16)
    for b in range(16):
        for c in range(4):
            part[b, pl.ds(c * 32, 32), :] = w[b * 32 : b * 32 + 32, c * 128 : c * 128 + 128]


def grid_output(gf, w, out):
    out[...] = nt(gf[...], w[...]).astype(BF16)


def z_sum(parts, out):
    total = parts[0].astype(F32)
    for j in range(1, 8):
        total = total + parts[j].astype(F32)
    out[...] = total.astype(BF16)


def band_sum(parts, out):
    total = parts[0].astype(F32)
    for j in range(1, 16):
        total = total + parts[j].astype(F32)
    done = total.astype(BF16)
    for j in range(16):
        out[j] = done


def finish(parts, out, *, grid_scale, mesh_scale):
    total = parts[0, 0:128, :].astype(F32)
    for j in range(1, 16):
        total = total + parts[j, 0:128, :].astype(F32)
    total = total * grid_scale
    for c in range(4):
        out[0, :, pl.ds(c * 128, 128)] = total[c * 32 : c * 32 + 32, :]
    for z in range(8):
        c, q = z // 4, z % 4
        for r in range(2):
            piece = parts[z * 2 + r, 128:176, :].astype(F32)
            for t in range(3):
                n = q * 3 + t
                scale = grid_scale if n < 2 else mesh_scale
                out[1 + n // 2, pl.ds((n % 2) * 16, 16), pl.ds(r * 256 + c * 128, 128)] = (
                    piece[t * 16 : t * 16 + 16, :] * scale
                )


def body(
    grid_latents, mesh_latents, weights, target_band, target_block, node_slot, neighbours, mesh_cotangent
):
    grid_scale = 1.0 / math.sqrt(NR * GB * BLK * NX * NY * NZ)
    mesh_scale = 1.0 / math.sqrt(NR * MESH * NX * NY * NZ)
    band = lax.axis_index("band")
    patch = lax.axis_index("patch")
    rep = lax.axis_index("rep")
    bx, by = band // 4, band % 4
    pos = jnp.stack(
        [jnp.where(rep == 0, bx, by), jnp.where(rep == 0, by, bx), rep, patch]
    ).astype(I32)
    w = [weights[i] for i in range(7)]
    x = grid_latents[0]
    ml = mesh_latents[0]
    cot = mesh_cotangent[0]
    codes = target_band[:, 0] * 2 + target_block
    slot = node_slot.reshape(GB, BLK)

    p0, slope1 = call(
        grid_forward,
        [(codes, 1), (x, 0), (w[0], 0), (slot, 0)],
        [((GB * BLK + META, LAT), BF16, 0), ((GB * BLK, LAT), BF16, 0)],
        flops=2 * 512**3,
    )
    p = [p0] + [first(p0, k) for k in (1, 2, 3)]

    neighbours, cot_late, p0_late = lax.optimization_barrier((neighbours, cot, p0))
    here = band * NZ + patch
    off = jnp.mod(neighbours // MESH - here + 1, NX * NY * NZ)
    local = jnp.mod(neighbours, MESH)
    code = off * MESH + local
    code_row = jnp.pad(code.T, ((0, 2), (0, 0)))

    def side(which):
        rows = jnp.where(off == which, local, 300).astype(BF16).T
        rows = jnp.pad(rows, ((0, META - K), (0, LAT - MESH)))
        return jnp.concatenate([cot_late, rows], axis=0)

    ring = NX * NY * NZ
    up = [(i, (i + 1) % ring) for i in range(ring)]
    down = [((i + 1) % ring, i) for i in range(ring)]
    cp = lax.ppermute(side(2), ("band", "patch"), up)
    cn = lax.ppermute(side(0), ("band", "patch"), down)
    gs = call(
        cot_tables,
        [(cot, 0), (cp, 0), (cn, 0), (w[6], 0)],
        [((3 * MESH, LAT), F32, 0)],
        flops=6 * 256 * 512 * 512,
    )[0]

    mesh_bf = ((MESH, LAT), BF16, 0)
    mesh_f = ((MESH, LAT), F32, 0)
    q0, q1, q2, q3, table = call(
        route_sum,
        [(pos, 1)] + [(v, 0) for v in p],
        [mesh_f, mesh_bf, mesh_bf, mesh_bf, ((16,), I32, 1)],
        scratch=[pltpu.VMEM((8, BLK, LAT), F32)],
        flops=2 * 512**3,
    )
    got = [second(q, k) for k, q in ((1, q1), (2, q2), (3, q3))]
    ah, agg, sq, slope2, lat = call(
        mesh_forward,
        [(v, 0) for v in (q0, *got, ml, w[1], w[2], w[3])],
        [mesh_bf] * 5,
        flops=6 * 256 * 512 * 512,
    )
    lp = lax.ppermute(lat, ("band", "patch"), up)
    ln = lax.ppermute(lat, ("band", "patch"), down)
    snd, rcv = call(
        own_tables, [(v, 0) for v in (lat, w[4], w[5])], [mesh_bf, mesh_f], flops=4 * 256 * 512 * 512
    )
    summed, gsend, grecv, gl, gsec, ga, gm = call(
        edges_backward,
        [
            (v, 0)
            for v in (
                lp, ln, snd, rcv, code, code_row, cp, cn, gs, cot, slope2, w[1], w[2], w[3], w[4], w[5],
            )
        ],
        [mesh_bf] * 7,
        scratch=[
            pltpu.VMEM((3 * MESH, LAT), BF16),
            pltpu.VMEM((2 * MESH, LAT), F32),
            pltpu.VMEM((MESH, META), F32),
            pltpu.VMEM((K * MESH, LAT), BF16),
            pltpu.VMEM((MESH, LAT), F32),
        ],
        flops=5 * 10**9,
    )
    g = [gm] + [second(gm, k) for k in (1, 2, 3)]

    keep, give = call(
        mesh_weights,
        [(pos, 1)] + [(v, 0) for v in (ah, agg, sq, lat, summed, ga, gsec, gl, gsend, grecv, cot)],
        [((8, 768, 128), BF16, 0)] * 2,
        flops=12 * 256 * 512 * 512,
    )
    other = lax.ppermute(give, "rep", [(0, 1), (1, 0)])
    both = (keep.astype(F32) + other.astype(F32)).astype(BF16)
    zparts = lax.all_to_all(both, "patch", split_axis=0, concat_axis=0, tiled=True)

    r = call(
        return_pick,
        [(pos, 1), (table, 1)] + [(v, 0) for v in g],
        [((GB * BLK, LAT), BF16, 0)] * 4,
        flops=2 * 512**3,
    )
    rr = [r[0]] + [first(r[k], k) for k in (1, 2, 3)]
    gf, part1 = call(
        grid_backward,
        [(pos, 1), (codes, 1)] + [(v, 0) for v in (*rr, x, slot, slope1)],
        [((GB * BLK, LAT), BF16, 0), ((16, 128, 128), BF16, 0)],
        scratch=[pltpu.VMEM((GB * BLK, LAT), BF16)],
        flops=4 * 512**3,
    )
    mesh_part = call(z_sum, [(zparts, 0)], [((768, 128), BF16, 0)], flops=10**6)[0]
    mine = jnp.concatenate([part1, mesh_part.reshape(16, 48, 128)], axis=1)
    over_band = lax.all_to_all(mine, "band", split_axis=0, concat_axis=0, tiled=True)
    spread = call(band_sum, [(over_band, 0)], [((16, 176, 128), BF16, 0)], flops=10**6)[0]
    final = lax.all_to_all(spread, ("patch", "rep"), split_axis=0, concat_axis=0, tiled=True)
    grid_grad = call(
        grid_output, [(gf, 0), (w[0], 0)], [((GB * BLK, LAT), BF16, 0)], flops=2 * 512**3
    )[0]

    def last(parts, out):
        finish(parts, out, grid_scale=grid_scale, mesh_scale=mesh_scale)

    weight_part = call(last, [(final, 0)], [((7, 32, LAT), F32, 0)], flops=10**6)[0]
    return (grid_grad[None], gl[None], weight_part)


def solution(mesh):
    return jax.shard_map(
        body,
        mesh=mesh,
        in_specs=(
            P("rep", ("band", "patch"), None),
            P("rep", ("band", "patch"), None),
            P(),
            P(("band", "patch"), None),
            P(("band", "patch")),
            P(("band", "patch")),
            P(("band", "patch"), None),
            P("rep", ("band", "patch"), None),
        ),
        out_specs=(
            P("rep", ("band", "patch"), None),
            P("rep", ("band", "patch"), None),
            P(None, "band", None),
        ),
        check_vma=False,
    )
```

time: 549 us -> 181 us (0.33)
  waiting for transfers between devices: 394 us -> 70.2 us
  Pallas kernels: 0 us -> 29.6 us
  other arithmetic: 32.7 us -> 3.16 us
  matrix products: 28.2 us -> 0 us
  local copies, waits for them, and re-layouts: 39.7 us -> 13.4 us
  between operations: 14.8 us -> 0.88 us
  blocking collectives: 0 us -> 13.8 us
  starting transfers between devices: 38.4 us -> 49 us
    psum x1 -> x0, waiting for transfers between devices: 280 us -> none  [body(): summed_grads = lax.psum(partials, ('band', 'patch', 'rep'))]
    all_to_all x3 -> x2, waiting for transfers between devices: 98.3 us -> 26.9 us  [the longest x1 20.1 us: body(): lax.all_to_all(spread, ('patch', 'rep'), split_axis=0, concat_axis=0, til...]
    pallas_call x0 -> x13, Pallas kernels: none -> 29.6 us  [call(): pl.pallas_call(kernel, out_shape=out_shape, in_specs=specs_in, out_specs=...]
    gather x8 -> x0, local copies, waits for them, and re-layouts: 29.1 us -> none  [the longest x1 17.3 us: body(): jnp.take(grad_aggregate, got_ids, axis=0, mode='fill', fill_value=0)]
    dot_general x21 -> x0, matrix products: 28.2 us -> none  [matmul(): return jnp.dot(left, right, preferred_element_type=jnp.float32)]
    ppermute x4 -> x17, waiting for transfers between devices: 15.9 us -> 43.3 us  [the longest x6 28.1 us: first(): return lax.ppermute(v, ALL, shifts(k, False))]
    ppermute x4 -> x17, starting transfers between devices: 14.8 us -> 37.1 us  [the longest x6 8.93 us: second(): return lax.ppermute(v, ALL, shifts(k, True))]
    add x5 -> x1, other arithmetic: 15.2 us -> 0.01 us  [body(): codes = target_band[:, 0] * 2 + target_block]
  transfers between devices with their start and end apart: 8 -> 19, of which waited for: 6 -> 11; matrix products, arithmetic and copies ran while one was open for 2% -> 2% of each run, Pallas kernels for 0% -> 5%
where the time goes in v1:
time: 181 us; the launch traced here: 180 us
  waiting for transfers between devices  70.2 us (39%)
  starting transfers between devices  49 us (27%)
  Pallas kernels  29.6 us (16%)
  blocking collectives  13.8 us (8%)
  local copies, waits for them, and re-layouts  13.4 us (7%)
  other arithmetic  3.16 us (2%)
    pallas_call x13, Pallas kernels, call(): pl.pallas_call(kernel, out_shape=out_shape, in_specs=specs_in, out_specs=...  29.6 us
    ppermute x6, waiting for transfers between devices, first(): return lax.ppermute(v, ALL, shifts(k, False))  28.1 us
    all_to_all x1, waiting for transfers between devices, body(): lax.all_to_all(spread, ('patch', 'rep'), split_axis=0, concat_axis=0, til...  20.1 us
    all_to_all x1, blocking collectives, body(): lax.all_to_all(mine, 'band', split_axis=0, concat_axis=0, tiled=True)  13.8 us
    ppermute x6, starting transfers between devices, second(): return lax.ppermute(v, ALL, shifts(k, True))  8.93 us
    unnamed x52, local copies, waits for them, and re-layouts  8.78 us
    ppermute x1, starting transfers between devices, body(): other = lax.ppermute(give, 'rep', [(0, 1), (1, 0)])  8.18 us
    all_to_all x1, starting transfers between devices, body(): lax.all_to_all(spread, ('patch', 'rep'), split_axis=0, concat_axis=0, til...  8.17 us
  transfers between devices with their start and end apart: 19, of which 11 were waited for; matrix products, arithmetic and copies ran while one was open for 2% of the time, Pallas kernels for 5%

profile of v1, /device:TPU:1, one launch (start us, length us, event | category | flops | bytes accessed | tf_op | source)
XLA Modules:
  0.0 180.0 jit_solution(4590651726521770299)
XLA Ops:
  0.7 3.1 %slice_bitcast_fusion = (bf16[512,512]{1,0:T(8,128)(2,1)}, bf16[512,512]{1,0:T(8,128)(2,1)S(1)}, bf16[512,512]{1,0:T(8,128)(2,1)S(1)}, bf16[512,512]{1,0:T(8,128...) fusion(bf16[7,512,512]{2,1,0:T(8,128)(2,1)} %param.10), kind=kLoop, calls=%fused_computation.5 | loop fusion | bytes 7340032 | tf_op jit(solution)/shard_map/squeeze | solution.py:314
  3.8 2.7 %shard_map.103 = (bf16[528,512]{1,0:T(8,128)(2,1)}, bf16[512,512]{1,0:T(8,128)(2,1)S(1)}) custom-call(s32[4]{0:T(128)S(1)} %bitcast_add_fusion.codes, bf16[512,512]{1,0:T(8,128)(2,1)S(1)} %bitcast.32, bf16[512,512]{1,0:T(8,128)(2,1)S(1)} %get-tuple-element.70.w, s32[4,128]{1,0:T(4,128)S(1)} %bitcast.40), custom_call_target="tpu_custom_call" | custom-call | flops 268435456 | bytes 1000000 | tf_op jit(solution)/shard_map/pallas_call | solution.py:45
  7.3 3.6 %collective-permute-start.2 = (bf16[528,512]{1,0:T(8,128)(2,1)}, bf16[528,512]{1,0:T(8,128)(2,1)}, u32[]{:S(2)}, u32[]{:S(2)}) collective-permute-start(bf16[528,512]{1,0:T(8,128)(2,1)} %get-tuple-element.34.p0), channel_id=1, source_target_pairs={{0,192},{1,49},{2,194},{3,51},{4,196},{5,53},{6,198},{7,55},{8,200... | collective-permute-start | bytes 1622024 | tf_op jit(solution)/shard_map/ppermute | solution.py:73
  12.0 11.3 %collective-permute-done.2.p3 = bf16[528,512]{1,0:T(8,128)(2,1)} collective-permute-done((bf16[528,512]{1,0:T(8,128)(2,1)}, bf16[528,512]{1,0:T(8,128)(2,1)}, u32[]{:S(2)}, u32[]{:S(2)}) %collective-permute-start.2) | collective-permute-done | bytes 540704 | tf_op jit(solution)/shard_map/ppermute | solution.py:73
  23.3 3.7 %collective-permute-done.p1 = bf16[528,512]{1,0:T(8,128)(2,1)} collective-permute-done((bf16[528,512]{1,0:T(8,128)(2,1)}, bf16[528,512]{1,0:T(8,128)(2,1)}, u32[]{:S(2)}, u32[]{:S(2)}) %collective-permute-start) | collective-permute-done | bytes 540704 | tf_op jit(solution)/shard_map/ppermute | solution.py:73
  27.0 4.3 %shard_map.104 = (f32[256,512]{1,0:T(8,128)S(1)}, bf16[256,512]{1,0:T(8,128)(2,1)S(1)}, bf16[256,512]{1,0:T(8,128)(2,1)S(1)}, bf16[256,512]{1,0:T(8,128)(2,1)S(1)}, s32[16]{0:T(128)S(1)}) custom-call(s32[4]{0:T(128)S(1)} %pad_add_fusion.pos, bf16[528,512]{1,0:T(8,128)(2,1)} %get-tuple-element.34.p0, bf16[528,512]{1,0:T(8,128)(2,1)} %collective-permute-done.p1, ...), custom_call_target="tpu_custom_call" | custom-call | flops 268435456 | bytes 1000000 | tf_op jit(solution)/shard_map/pallas_call | solution.py:45
  32.3 2.3 %collective-permute-start.4 = (bf16[256,512]{1,0:T(8,128)(2,1)S(1)}, bf16[256,512]{1,0:T(8,128)(2,1)S(1)}, u32[]{:S(2)}, u32[]{:S(2)}) collective-permute-start(bf16[256,512]{1,0:T(8,128)(2,1)S(1)} %get-tuple-element.38), channel_id=1, source_target_pairs={{0,32},{1,129},{2,34},{3,131},{4,36},{5,133},{6,38},{7,135},{8,40}... | collective-permute-start | bytes 786440 | tf_op jit(solution)/shard_map/ppermute | solution.py:77
  37.3 5.8 %collective-permute-start.9 = (bf16[272,512]{1,0:T(8,128)(2,1)}, bf16[272,512]{1,0:T(8,128)(2,1)}, u32[]{:S(2)}, u32[]{:S(2)}) collective-permute-start(bf16[272,512]{1,0:T(8,128)(2,1)} %get-tuple-element.72), channel_id=1, source_target_pairs={{2,0},{4,2},{6,4},{8,6},{10,8},{12,10},{14,12},{16,14},{18,16},{20... | collective-permute-start | bytes 835592 | tf_op jit(solution)/shard_map/ppermute | solution.py:345
  43.1 1.6 shard_map.105
  47.5 6.9 %collective-permute-start.7 = (bf16[256,512]{1,0:T(8,128)(2,1)}, bf16[256,512]{1,0:T(8,128)(2,1)}, u32[]{:S(2)}, u32[]{:S(2)}) collective-permute-start(bf16[256,512]{1,0:T(8,128)(2,1)} %get-tuple-element.40.lat), channel_id=1, source_target_pairs={{2,0},{4,2},{6,4},{8,6},{10,8},{12,10},{14,12},{16,14},{18,16},{20... | collective-permute-start | bytes 786440 | tf_op jit(solution)/shard_map/ppermute | solution.py:370
  56.9 1.7 shard_map.107.gs
  58.6 1.4 shard_map.106
  60.0 5.3 %collective-permute-done.6.lp = bf16[256,512]{1,0:T(8,128)(2,1)} collective-permute-done((bf16[256,512]{1,0:T(8,128)(2,1)}, bf16[256,512]{1,0:T(8,128)(2,1)}, u32[]{:S(2)}, u32[]{:S(2)}) %collective-permute-start.6) | collective-permute-done | bytes 262176 | tf_op jit(solution)/shard_map/ppermute | solution.py:369
  65.3 10.1 %shard_map.108 = (bf16[256,512]{1,0:T(8,128)(2,1)S(1)}, bf16[256,512]{1,0:T(8,128)(2,1)S(1)}, bf16[256,512]{1,0:T(8,128)(2,1)S(1)}, bf16[256,512]{1,0:T(8,128)(2...) custom-call(bf16[256,512]{1,0:T(8,128)(2,1)} %collective-permute-done.6.lp, ...), custom_call_target="tpu_custom_call" | custom-call | flops 5000000000 | bytes 1000000 | tf_op jit(solution)/shard_map/pallas_call | solution.py:45
  77.1 2.0 %shard_map.112 = (bf16[8,768,128]{2,1,0:T(8,128)(2,1)S(1)}, bf16[8,768,128]{2,1,0:T(8,128)(2,1)S(1)}) custom-call(s32[4]{0:T(128)S(1)} %pad_add_fusion.pos, bf16[256,512]{1,0:T(8,128)(2,1)S(1)} %copy-done.15, bf16[256,512]{1,0:T(8,128)(2,1)S(1)} %copy-done.17, bf16[256,512]{1,0:T(8,128)(2,1)S(1)} %copy-done.19, bf16[256,512]{1,0:T(8,128)(2,1)} %get-tuple-element.40.lat, ...), custom_call_target="tpu_custom_call" | custom-call | flops 805306368 | bytes 1000000 | tf_op jit(solution)/shard_map/pallas_call | solution.py:45
  79.0 8.2 %collective-permute-start.16 = (bf16[8,768,128]{2,1,0:T(8,128)(2,1)S(1)}, bf16[8,768,128]{2,1,0:T(8,128)(2,1)S(1)}, u32[]{:S(2)}, u32[]{:S(2)}) collective-permute-start(bf16[8,768,128]{2,1,0:T(8,128)(2,1)S(1)} %get-tuple-element.64), channel_id=1, source_target_pairs={{0,1},{1,0},{2,3},{3,2},{4,5},{5,4},{6,7},{7,6},{8,9},{9,8},{10,11... | collective-permute-start | bytes 4718600 | tf_op jit(solution)/shard_map/ppermute | solution.py:400
  87.2 3.0 %collective-permute-done.16 = bf16[8,768,128]{2,1,0:T(8,128)(2,1)S(1)} collective-permute-done((bf16[8,768,128]{2,1,0:T(8,128)(2,1)S(1)}, bf16[8,768,128]{2,1,0:T(8,128)(2,1)S(1)}, u32[]{:S(2)}, u32[]{:S(2)}) %collective-permute-start.16) | collective-permute-done | bytes 1572896 | tf_op jit(solution)/shard_map/ppermute | solution.py:400
  90.3 1.6 add_convert_fusion
  91.9 3.7 %all-to-all-start = ((bf16[8,768,128]{2,1,0:T(8,128)(2,1)}), bf16[8,768,128]{2,1,0:T(8,128)(2,1)S(1)}, u32[]{:S(2)}, u32[]{:S(2)}) async-start(bf16[8,768,128]{2,1,0:T(8,128)(2,1)} %add_convert_fusion), calls=%async_computation | async-start | bytes 3145728 | tf_op jit(solution)/shard_map/all_to_all | solution.py:402
  96.1 3.9 %collective-permute-start.11 = (bf16[256,512]{1,0:T(8,128)(2,1)S(1)}, bf16[256,512]{1,0:T(8,128)(2,1)S(1)}, u32[]{:S(2)}, u32[]{:S(2)}) collective-permute-start(bf16[256,512]{1,0:T(8,128)(2,1)S(1)} %copy-done.12), channel_id=1, source_target_pairs={{0,32},{1,129},{2,34},{3,131},{4,36},{5,133},{6,38},{7,135},{8,40}... | collective-permute-start | bytes 786440 | tf_op jit(solution)/shard_map/ppermute | solution.py:77
  100.0 2.3 %collective-permute-done.12.g3 = bf16[256,512]{1,0:T(8,128)(2,1)S(1)} collective-permute-done((bf16[256,512]{1,0:T(8,128)(2,1)S(1)}, bf16[256,512]{1,0:T(8,128)(2,1)S(1)}, u32[]{:S(2)}, u32[]{:S(2)}) %collective-permute-start.12) | collective-permute-done | bytes 262176 | tf_op jit(solution)/shard_map/ppermute | solution.py:77
  102.3 1.8 collective-permute-done.11.g2
  104.1 2.8 %collective-permute-done.10.g1 = bf16[256,512]{1,0:T(8,128)(2,1)S(1)} collective-permute-done((bf16[256,512]{1,0:T(8,128)(2,1)S(1)}, bf16[256,512]{1,0:T(8,128)(2,1)S(1)}, u32[]{:S(2)}, u32[]{:S(2)}) %collective-permute-start.10) | collective-permute-done | bytes 262176 | tf_op jit(solution)/shard_map/ppermute | solution.py:77
  106.9 1.3 shard_map.109
  108.2 1.4 collective-permute-start.14
  109.6 1.3 collective-permute-start.15
  110.9 12.5 %collective-permute-done.13.r1 = bf16[512,512]{1,0:T(8,128)(2,1)S(1)} collective-permute-done((bf16[512,512]{1,0:T(8,128)(2,1)S(1)}, bf16[512,512]{1,0:T(8,128)(2,1)S(1)}, u32[]{:S(2)}, u32[]{:S(2)}) %collective-permute-start.13) | collective-permute-done | bytes 524320 | tf_op jit(solution)/shard_map/ppermute | solution.py:73
  124.0 1.3 shard_map.110
  126.9 6.8 %all-to-all-done.parts = bf16[8,768,128]{2,1,0:T(8,128)(2,1)S(1)} async-done(((bf16[8,768,128]{2,1,0:T(8,128)(2,1)}), bf16[8,768,128]{2,1,0:T(8,128)(2,1)S(1)}, u32[]{:S(2)}, u32[]{:S(2)}) %all-to-all-start) | async-done | bytes 1572896 | tf_op jit(solution)/shard_map/all_to_all | solution.py:402
  134.8 13.8 %all_to_all.15.parts = bf16[16,176,128]{2,1,0:T(8,128)(2,1)S(1)} all-to-all(bf16[16,176,128]{2,1,0:T(8,128)(2,1)S(1)} %pad_maximum_fusion), channel_id=1, replica_groups=mesh['band'=16,'patch'=8,'rep'=2] {'band'}, dimensions={0} | all-to-all | bytes 1441792 | tf_op jit(solution)/shard_map/all_to_all | solution.py:420
  149.6 8.2 %all-to-all-start.2 = ((bf16[16,176,128]{2,1,0:T(8,128)(2,1)}), bf16[16,176,128]{2,1,0:T(8,128)(2,1)S(1)}, u32[]{:S(2)}, u32[]{:S(2)}) async-start(bf16[16,176,128]{2,1,0:T(8,128)(2,1)} %shard_map.114), calls=%async_computation.2 | async-start | bytes 1441792 | tf_op jit(solution)/shard_map/all_to_all | solution.py:422
  159.1 20.1 %all-to-all-done.2.parts = bf16[16,176,128]{2,1,0:T(8,128)(2,1)S(1)} async-done(((bf16[16,176,128]{2,1,0:T(8,128)(2,1)}), bf16[16,176,128]{2,1,0:T(8,128)(2,1)S(1)}, u32[]{:S(2)}, u32[]{:S(2)}) %all-to-all-start.2) | async-done | bytes 720928 | tf_op jit(solution)/shard_map/all_to_all | solution.py:422
  (81 shorter events, 19.7 us)
Async XLA Ops:
  0.6 3.1 %copy-start.24 = (s32[4]{0:T(128)S(1)}, s32[4]{0:T(128)}, u32[]{:S(2)}) copy-start(s32[4]{0:T(128)} %param.12) | copy-start | bytes 52
  0.6 3.1 %copy-start.25 = (s32[4,1]{0,1:T(1,128)S(1)}, s32[4,1]{0,1:T(1,128)}, u32[]{:S(2)}) copy-start(s32[4,1]{0,1:T(1,128)} %param.11) | copy-start | bytes 52
  3.8 32.0 %copy-start.23 = (s32[256,6]{0,1:T(8,128)S(1)}, s32[256,6]{0,1:T(8,128)}, u32[]{:S(2)}) copy-start(s32[256,6]{0,1:T(8,128)} %param.14) | copy-start | bytes 18436
  3.8 32.6 %copy-start.3 = (bf16[1,256,512]{2,1,0:T(8,128)(2,1)S(1)}, bf16[1,256,512]{2,1,0:T(8,128)(2,1)}, u32[]{:S(2)}) copy-start(bf16[1,256,512]{2,1,0:T(8,128)(2,1)} %param.15) | copy-start | bytes 786436
  7.3 16.0 %collective-permute-start.2 = (bf16[528,512]{1,0:T(8,128)(2,1)}, bf16[528,512]{1,0:T(8,128)(2,1)}, u32[]{:S(2)}, u32[]{:S(2)}) collective-permute-start(bf16[528,512]{1,0:T(8,128)(2,1)} %get-tuple-element.34.p0), channel_id=1, source_target_pairs={{0,192},{1,49},{2,194},{3,51},{4,196},{5,53},{6,198},{7,55},{8,200... | collective-permute-start | bytes 1622024 | tf_op jit(solution)/shard_map/ppermute | solution.py:73
  10.9 12.4 %collective-permute-start.1 = (bf16[528,512]{1,0:T(8,128)(2,1)}, bf16[528,512]{1,0:T(8,128)(2,1)}, u32[]{:S(2)}, u32[]{:S(2)}) collective-permute-start(bf16[528,512]{1,0:T(8,128)(2,1)} %get-tuple-element.34.p0), channel_id=1, source_target_pairs={{0,128},{1,33},{2,130},{3,35},{4,132},{5,37},{6,134},{7,39},{8,136... | collective-permute-start | bytes 1622024 | tf_op jit(solution)/shard_map/ppermute | solution.py:73
  11.2 15.8 %collective-permute-start = (bf16[528,512]{1,0:T(8,128)(2,1)}, bf16[528,512]{1,0:T(8,128)(2,1)}, u32[]{:S(2)}, u32[]{:S(2)}) collective-permute-start(bf16[528,512]{1,0:T(8,128)(2,1)} %get-tuple-element.34.p0), channel_id=1, source_target_pairs={{0,64},{1,17},{2,66},{3,19},{4,68},{5,21},{6,70},{7,23},{8,72},{9,... | collective-permute-start | bytes 1622024 | tf_op jit(solution)/shard_map/ppermute | solution.py:73
  11.9 31.2 %copy-start.10 = (bf16[1,256,512]{2,1,0:T(8,128)(2,1)S(1)}, bf16[1,256,512]{2,1,0:T(8,128)(2,1)}, u32[]{:S(2)}) copy-start(bf16[1,256,512]{2,1,0:T(8,128)(2,1)} %param.9) | copy-start | bytes 786436
  31.3 11.7 %collective-permute-start.3 = (bf16[256,512]{1,0:T(8,128)(2,1)S(1)}, bf16[256,512]{1,0:T(8,128)(2,1)S(1)}, u32[]{:S(2)}, u32[]{:S(2)}) collective-permute-start(bf16[256,512]{1,0:T(8,128)(2,1)S(1)} %get-tuple-element.37), channel_id=1, source_target_pairs={{0,16},{1,65},{2,18},{3,67},{4,20},{5,69},{6,22},{7,71},{8,24},{9,... | collective-permute-start | bytes 786440 | tf_op jit(solution)/shard_map/ppermute | solution.py:77
  32.3 10.8 %collective-permute-start.4 = (bf16[256,512]{1,0:T(8,128)(2,1)S(1)}, bf16[256,512]{1,0:T(8,128)(2,1)S(1)}, u32[]{:S(2)}, u32[]{:S(2)}) collective-permute-start(bf16[256,512]{1,0:T(8,128)(2,1)S(1)} %get-tuple-element.38), channel_id=1, source_target_pairs={{0,32},{1,129},{2,34},{3,131},{4,36},{5,133},{6,38},{7,135},{8,40}... | collective-permute-start | bytes 786440 | tf_op jit(solution)/shard_map/ppermute | solution.py:77
  34.6 8.4 %collective-permute-start.5 = (bf16[256,512]{1,0:T(8,128)(2,1)S(1)}, bf16[256,512]{1,0:T(8,128)(2,1)S(1)}, u32[]{:S(2)}, u32[]{:S(2)}) collective-permute-start(bf16[256,512]{1,0:T(8,128)(2,1)S(1)} %get-tuple-element.39), channel_id=1, source_target_pairs={{0,48},{1,193},{2,50},{3,195},{4,52},{5,197},{6,54},{7,199},{8,56}... | collective-permute-start | bytes 786440 | tf_op jit(solution)/shard_map/ppermute | solution.py:77
  37.3 18.6 %collective-permute-start.9 = (bf16[272,512]{1,0:T(8,128)(2,1)}, bf16[272,512]{1,0:T(8,128)(2,1)}, u32[]{:S(2)}, u32[]{:S(2)}) collective-permute-start(bf16[272,512]{1,0:T(8,128)(2,1)} %get-tuple-element.72), channel_id=1, source_target_pairs={{2,0},{4,2},{6,4},{8,6},{10,8},{12,10},{14,12},{16,14},{18,16},{20... | collective-permute-start | bytes 835592 | tf_op jit(solution)/shard_map/ppermute | solution.py:345
  43.0 12.8 %collective-permute-start.8 = (bf16[272,512]{1,0:T(8,128)(2,1)}, bf16[272,512]{1,0:T(8,128)(2,1)}, u32[]{:S(2)}, u32[]{:S(2)}) collective-permute-start(bf16[272,512]{1,0:T(8,128)(2,1)} %get-tuple-element.73), channel_id=1, source_target_pairs={{0,2},{2,4},{4,6},{6,8},{8,10},{10,12},{12,14},{14,16},{16,18},{18... | collective-permute-start | bytes 835592 | tf_op jit(solution)/shard_map/ppermute | solution.py:344
  47.5 12.6 %collective-permute-start.7 = (bf16[256,512]{1,0:T(8,128)(2,1)}, bf16[256,512]{1,0:T(8,128)(2,1)}, u32[]{:S(2)}, u32[]{:S(2)}) collective-permute-start(bf16[256,512]{1,0:T(8,128)(2,1)} %get-tuple-element.40.lat), channel_id=1, source_target_pairs={{2,0},{4,2},{6,4},{8,6},{10,8},{12,10},{14,12},{16,14},{18,16},{20... | collective-permute-start | bytes 786440 | tf_op jit(solution)/shard_map/ppermute | solution.py:370
  54.3 11.0 %collective-permute-start.6 = (bf16[256,512]{1,0:T(8,128)(2,1)}, bf16[256,512]{1,0:T(8,128)(2,1)}, u32[]{:S(2)}, u32[]{:S(2)}) collective-permute-start(bf16[256,512]{1,0:T(8,128)(2,1)} %get-tuple-element.40.lat), channel_id=1, source_target_pairs={{0,2},{2,4},{4,6},{6,8},{8,10},{10,12},{12,14},{14,16},{16,18},{18... | collective-permute-start | bytes 786440 | tf_op jit(solution)/shard_map/ppermute | solution.py:369
  56.9 8.4 %copy-start.21 = (bf16[256,512]{1,0:T(8,128)(2,1)S(1)}, bf16[256,512]{1,0:T(8,128)(2,1)}, u32[]{:S(2)}) copy-start(bf16[256,512]{1,0:T(8,128)(2,1)} %copy-done.20) | copy-start | bytes 786436
  65.3 10.8 %copy-start.15 = (bf16[256,512]{1,0:T(8,128)(2,1)S(1)}, bf16[256,512]{1,0:T(8,128)(2,1)}, u32[]{:S(2)}) copy-start(bf16[256,512]{1,0:T(8,128)(2,1)} %copy-done.14) | copy-start | bytes 786436
  65.3 10.8 %copy-start.17 = (bf16[256,512]{1,0:T(8,128)(2,1)S(1)}, bf16[256,512]{1,0:T(8,128)(2,1)}, u32[]{:S(2)}) copy-start(bf16[256,512]{1,0:T(8,128)(2,1)} %copy-done.16) | copy-start | bytes 786436
  65.3 10.8 %copy-start.19 = (bf16[256,512]{1,0:T(8,128)(2,1)S(1)}, bf16[256,512]{1,0:T(8,128)(2,1)}, u32[]{:S(2)}) copy-start(bf16[256,512]{1,0:T(8,128)(2,1)} %copy-done.18) | copy-start | bytes 786436
  79.0 11.2 %collective-permute-start.16 = (bf16[8,768,128]{2,1,0:T(8,128)(2,1)S(1)}, bf16[8,768,128]{2,1,0:T(8,128)(2,1)S(1)}, u32[]{:S(2)}, u32[]{:S(2)}) collective-permute-start(bf16[8,768,128]{2,1,0:T(8,128)(2,1)S(1)} %get-tuple-element.64), channel_id=1, source_target_pairs={{0,1},{1,0},{2,3},{3,2},{4,5},{5,4},{6,7},{7,6},{8,9},{9,8},{10,11... | collective-permute-start | bytes 4718600 | tf_op jit(solution)/shard_map/ppermute | solution.py:400
  91.9 3.7 %copy-start.12 = (bf16[256,512]{1,0:T(8,128)(2,1)S(1)}, bf16[256,512]{1,0:T(8,128)(2,1)}, u32[]{:S(2)}) copy-start(bf16[256,512]{1,0:T(8,128)(2,1)} %copy-done.11) | copy-start | bytes 786436
  91.9 32.1 %copy-start.2 = (bf16[1,512,512]{2,1,0:T(8,128)(2,1)S(1)}, bf16[1,512,512]{2,1,0:T(8,128)(2,1)}, u32[]{:S(2)}) copy-start(bf16[1,512,512]{2,1,0:T(8,128)(2,1)} %param.8) | copy-start | bytes 1572868
  91.9 32.1 %copy-start.5 = (bf16[512,512]{1,0:T(8,128)(2,1)S(1)}, bf16[512,512]{1,0:T(8,128)(2,1)}, u32[]{:S(2)}) copy-start(bf16[512,512]{1,0:T(8,128)(2,1)} %copy-done.4) | copy-start | bytes 1572868
  91.9 41.9 %all-to-all-start = ((bf16[8,768,128]{2,1,0:T(8,128)(2,1)}), bf16[8,768,128]{2,1,0:T(8,128)(2,1)S(1)}, u32[]{:S(2)}, u32[]{:S(2)}) async-start(bf16[8,768,128]{2,1,0:T(8,128)(2,1)} %add_convert_fusion), calls=%async_computation | async-start | bytes 3145728 | tf_op jit(solution)/shard_map/all_to_all | solution.py:402
  95.6 6.7 %collective-permute-start.12 = (bf16[256,512]{1,0:T(8,128)(2,1)S(1)}, bf16[256,512]{1,0:T(8,128)(2,1)S(1)}, u32[]{:S(2)}, u32[]{:S(2)}) collective-permute-start(bf16[256,512]{1,0:T(8,128)(2,1)S(1)} %copy-done.12), channel_id=1, source_target_pairs={{0,48},{1,193},{2,50},{3,195},{4,52},{5,197},{6,54},{7,199},{8,56}... | collective-permute-start | bytes 786440 | tf_op jit(solution)/shard_map/ppermute | solution.py:77
  96.1 7.9 %collective-permute-start.11 = (bf16[256,512]{1,0:T(8,128)(2,1)S(1)}, bf16[256,512]{1,0:T(8,128)(2,1)S(1)}, u32[]{:S(2)}, u32[]{:S(2)}) collective-permute-start(bf16[256,512]{1,0:T(8,128)(2,1)S(1)} %copy-done.12), channel_id=1, source_target_pairs={{0,32},{1,129},{2,34},{3,131},{4,36},{5,133},{6,38},{7,135},{8,40}... | collective-permute-start | bytes 786440 | tf_op jit(solution)/shard_map/ppermute | solution.py:77
  100.0 6.9 %collective-permute-start.10 = (bf16[256,512]{1,0:T(8,128)(2,1)S(1)}, bf16[256,512]{1,0:T(8,128)(2,1)S(1)}, u32[]{:S(2)}, u32[]{:S(2)}) collective-permute-start(bf16[256,512]{1,0:T(8,128)(2,1)S(1)} %copy-done.12), channel_id=1, source_target_pairs={{0,16},{1,65},{2,18},{3,67},{4,20},{5,69},{6,22},{7,71},{8,24},{9,... | collective-permute-start | bytes 786440 | tf_op jit(solution)/shard_map/ppermute | solution.py:77
  108.1 15.2 %collective-permute-start.13 = (bf16[512,512]{1,0:T(8,128)(2,1)S(1)}, bf16[512,512]{1,0:T(8,128)(2,1)S(1)}, u32[]{:S(2)}, u32[]{:S(2)}) collective-permute-start(bf16[512,512]{1,0:T(8,128)(2,1)S(1)} %get-tuple-element.48), channel_id=1, source_target_pairs={{0,64},{1,17},{2,66},{3,19},{4,68},{5,21},{6,70},{7,23},{8,72},{9,... | collective-permute-start | bytes 1572872 | tf_op jit(solution)/shard_map/ppermute | solution.py:73
  108.2 15.1 %collective-permute-start.14 = (bf16[512,512]{1,0:T(8,128)(2,1)S(1)}, bf16[512,512]{1,0:T(8,128)(2,1)S(1)}, u32[]{:S(2)}, u32[]{:S(2)}) collective-permute-start(bf16[512,512]{1,0:T(8,128)(2,1)S(1)} %get-tuple-element.49), channel_id=1, source_target_pairs={{0,128},{1,33},{2,130},{3,35},{4,132},{5,37},{6,134},{7,39},{8,136... | collective-permute-start | bytes 1572872 | tf_op jit(solution)/shard_map/ppermute | solution.py:73
  109.6 14.4 %collective-permute-start.15 = (bf16[512,512]{1,0:T(8,128)(2,1)S(1)}, bf16[512,512]{1,0:T(8,128)(2,1)S(1)}, u32[]{:S(2)}, u32[]{:S(2)}) collective-permute-start(bf16[512,512]{1,0:T(8,128)(2,1)S(1)} %get-tuple-element.50), channel_id=1, source_target_pairs={{0,192},{1,49},{2,194},{3,51},{4,196},{5,53},{6,198},{7,55},{8,200... | collective-permute-start | bytes 1572872 | tf_op jit(solution)/shard_map/ppermute | solution.py:73
  148.6 9.2 %copy-start.7 = (bf16[512,512]{1,0:T(8,128)(2,1)S(1)}, bf16[512,512]{1,0:T(8,128)(2,1)}, u32[]{:S(2)}) copy-start(bf16[512,512]{1,0:T(8,128)(2,1)} %copy-done.6) | copy-start | bytes 1572868
  149.6 29.5 %all-to-all-start.2 = ((bf16[16,176,128]{2,1,0:T(8,128)(2,1)}), bf16[16,176,128]{2,1,0:T(8,128)(2,1)S(1)}, u32[]{:S(2)}, u32[]{:S(2)}) async-start(bf16[16,176,128]{2,1,0:T(8,128)(2,1)} %shard_map.114), calls=%async_computation.2 | async-start | bytes 1441792 | tf_op jit(solution)/shard_map/all_to_all | solution.py:422
  (13 other events, 15.2 us)

commit v2 on v1

v2 whole, which is shorter than its diff:
```python
import math

import jax
import jax.numpy as jnp
from jax import lax
from jax.experimental import pallas as pl
from jax.experimental.pallas import tpu as pltpu
from jax.sharding import PartitionSpec as P

F32 = jnp.float32
BF16 = jnp.bfloat16
I32 = jnp.int32
ALL = ("band", "patch", "rep")
NX, NY, NZ, NR = 4, 4, 8, 2
LAT = 512
BLK = 128
GB = 4
MESH = 256
K = 6
META = 16
RETURN_FLOPS = 25 * 10**9
VMEM = pl.BlockSpec(memory_space=pltpu.VMEM)
SMEM = pl.BlockSpec(memory_space=pltpu.SMEM)
FIRST = pl.BlockSpec((1, 512, 512), lambda i: (0, 0, 0), memory_space=pltpu.VMEM)


def nn(a, b):
    return lax.dot_general(a, b, (((1,), (0,)), ((), ())), preferred_element_type=F32)


def nt(a, b):
    return lax.dot_general(a, b, (((1,), (1,)), ((), ())), preferred_element_type=F32)


def tn(a, b):
    return lax.dot_general(a, b, (((0,), (0,)), ((), ())), preferred_element_type=F32)


def sigmoid(v):
    return 0.5 * jnp.tanh(0.5 * v) + 0.5


def call(kernel, ins, outs, scratch=(), flops=0, limit=8, **more):
    specs_in = [(VMEM, SMEM, FIRST)[s] for _, s in ins]
    out_shape = [jax.ShapeDtypeStruct(shape, dtype) for shape, dtype, _ in outs]
    specs_out = [SMEM if s else VMEM for _, _, s in outs]
    return pl.pallas_call(
        kernel,
        out_shape=out_shape,
        in_specs=specs_in,
        out_specs=specs_out,
        scratch_shapes=list(scratch),
        compiler_params=pltpu.CompilerParams(vmem_limit_bytes=limit * 1024 * 1024),
        cost_estimate=pl.CostEstimate(flops=flops, bytes_accessed=1000000, transcendentals=0),
        **more,
    )(*[a for a, _ in ins])


def device(x, y, z, r):
    return ((x * NY + y) * NZ + z) * NR + r


def shifts(k, flip):
    pairs = []
    for x in range(NX):
        for y in range(NY):
            for z in range(NZ):
                for r in range(NR):
                    along_x = (r == 0) != flip
                    to = device((x + k) % NX, y, z, r) if along_x else device(x, (y + k) % NY, z, r)
                    pairs.append((device(x, y, z, r), to))
    return pairs


def first(v, k):
    return lax.ppermute(v, ALL, shifts(k, False))


def second(v, k):
    return lax.ppermute(v, ALL, shifts(k, True))


def split_code(code, rep):
    t = lax.shift_right_logical(code, 1)
    tx = lax.shift_right_logical(t, 2)
    ty = t & 3
    d1 = jnp.where(rep == 0, tx, ty)
    d2 = jnp.where(rep == 0, ty, tx)
    return d1, d2, code & 1


def place(pos):
    v = pos[0]
    return v & 3, lax.shift_right_logical(v, 2) & 3, lax.shift_right_logical(v, 4) & 1, lax.shift_right_logical(v, 5)


def grid_forward(tb, tk, x, w, slot, out, slope):
    row = lax.broadcasted_iota(I32, (BLK, BLK), 0)
    for g in range(GB):
        rows = pl.ds(g * BLK, BLK)
        v = nn(x[rows, :], w[0])
        sg = sigmoid(v)
        h = v * sg
        slope[rows, :] = (sg + h * (1.0 - sg)).astype(BF16)
        pick = jnp.where(row == slot[g : g + 1, :], 1.0, 0.0).astype(BF16)
        out[rows, :] = nn(pick, h.astype(BF16)).astype(BF16)
    meta_row = lax.broadcasted_iota(I32, (META, LAT), 0)
    meta = jnp.zeros((META, LAT), F32)
    for g in range(GB):
        meta = jnp.where(meta_row == g, (tb[g] * 2 + tk[g]).astype(F32), meta)
    out[pl.ds(GB * BLK, META), :] = meta.astype(BF16)


def edge_codes(pos, near, row, col, up, down):
    local = (near[...] & (MESH - 1)).astype(F32)
    off = (lax.shift_right_logical(near[...], 8) - place(pos)[3] + 1) & (NX * NY * NZ - 1)
    code = off.astype(F32) * MESH + local
    full = jnp.concatenate([code, jnp.zeros((META - K, MESH), F32)], axis=0)
    row[...] = full
    col[...] = jnp.transpose(full)
    for out, which in ((up, 2), (down, 0)):
        ends = jnp.where(off == which, local, 300.0)
        ends = jnp.concatenate([ends, jnp.full((META - K, MESH), 300.0, F32)], axis=0)
        out[...] = jnp.concatenate([ends, ends], axis=1).astype(BF16)


def route_sum(pos, p0, p1, p2, p3, q0, q1, q2, q3, table, acc):
    own1, own2, rep, _ = place(pos)
    sources = (p0, p1, p2, p3)
    codes = []
    for p in sources:
        meta = p[pl.ds(GB * BLK, META), 0:128].astype(F32)
        codes += [jnp.max(meta[i : i + 1, :]).astype(I32) for i in range(GB)]
    acc[...] = jnp.zeros_like(acc)
    for n, code in enumerate(codes):
        table[n] = code
        d1, d2, blk = split_code(code, rep)
        slot = ((d2 - own2) & 3) * 2 + blk
        p, i = sources[n // GB], n % GB

        @pl.when(d1 == own1)
        def _():
            acc[slot] += p[pl.ds(i * BLK, BLK), :].astype(F32)

    for k, q in enumerate((q0, q1, q2, q3)):
        for b in range(2):
            q[pl.ds(b * BLK, BLK), :] = acc[2 * k + b].astype(q.dtype)


def mesh_forward(q0, r1, r2, r3, ml, w, up, down, ah, agg, sq, slope, lat_up, lat_down):
    total = q0[...] + r1[...].astype(F32) + r2[...].astype(F32) + r3[...].astype(F32)
    ah[...] = total.astype(BF16)
    agg[...] = nn(ah[...], w[1]).astype(BF16)
    v = nn(agg[...], w[2])
    sg = sigmoid(v)
    s = v * sg
    slope[...] = (sg + s * (1.0 - sg)).astype(BF16)
    sq[...] = s.astype(BF16)
    lat = (ml[...].astype(F32) + nn(sq[...], w[3])).astype(BF16)
    for out, ends in ((lat_up, up), (lat_down, down)):
        out[pl.ds(0, MESH), :] = lat
        out[pl.ds(MESH, META), :] = ends[...]


def own_tables(lat, w, snd, rcv):
    rows = lat[pl.ds(0, MESH), :]
    snd[...] = (nn(rows, w[4]) * 0.5).astype(BF16)
    rcv[...] = nn(rows, w[5]) * 0.5


def cot_tables(cot, cp, cn, w, gs):
    for j, c in enumerate((cp, cot, cn)):
        gs[pl.ds(j * MESH, MESH), :] = nt(c[...], w[6]) * 0.5


def edges_backward(
    lp, ln, snd, rcv, col, row, gs, cot, slope2, w,
    summed_b, gsend_b, grecv_b, gl_b, gsec_b, ga_b, gm_b, gl_out, gm_own,
    table, srcv, ecol, e, gsend,
):
    table[pl.ds(MESH, MESH), :] = snd[...]
    for j, c in enumerate((lp, ln)):
        rows = c[pl.ds(0, MESH), :]
        table[pl.ds(2 * j * MESH, MESH), :] = (nn(rows, w[4]) * 0.5).astype(BF16)
        srcv[pl.ds(j * MESH, MESH), :] = nn(rows, w[5]) * 0.5
    half = 128
    lane = lax.broadcasted_iota(I32, (half, 3 * MESH), 1).astype(F32)
    for m in range(2):
        rows = pl.ds(m * half, half)
        total = jnp.zeros((half, LAT), F32)
        recv = jnp.zeros((half, LAT), F32)
        for k in range(K):
            pick = jnp.where(lane == col[rows, k : k + 1], 1.0, 0.0).astype(BF16)
            h = nn(pick, table[...]) + rcv[rows, :]
            t = jnp.tanh(h)
            u = 1.0 + t
            s = h * u
            total = total + s
            eg = (gs[pl.ds(MESH + m * half, half), :] * (u + s * (1.0 - t))).astype(BF16)
            recv = recv + eg.astype(F32)
            e[pl.ds(k * MESH + m * half, half), :] = eg
        summed_b[rows, :] = total.astype(BF16)
        grecv_b[rows, :] = recv.astype(BF16)
    own = lax.broadcasted_iota(I32, (MESH, MESH), 0).astype(F32)
    acc = jnp.zeros((MESH, LAT), F32)
    for k in range(K):
        pick = jnp.where(own + float(MESH) == row[k : k + 1, :], 1.0, 0.0).astype(BF16)
        acc = acc + nn(pick, e[pl.ds(k * MESH, MESH), :])
    gsend[...] = acc
    lane2 = lax.broadcasted_iota(I32, (half, MESH), 1).astype(F32)
    for side, c in enumerate((lp, ln)):
        codes = c[pl.ds(MESH, META), 0:MESH].astype(F32)
        ecol[...] = jnp.transpose(codes)
        for k in range(K):
            for m in range(2):
                rows = pl.ds(m * half, half)
                pick = jnp.where(lane2 == ecol[rows, k : k + 1], 1.0, 0.0).astype(BF16)
                h = nn(pick, table[pl.ds(MESH, MESH), :]) + srcv[pl.ds(side * MESH + m * half, half), :]
                t = jnp.tanh(h)
                u = 1.0 + t
                g = gs[pl.ds(2 * side * MESH + m * half, half), :]
                e[pl.ds(k * MESH + m * half, half), :] = (g * (u + h * u * (1.0 - t))).astype(BF16)
        acc = gsend[...]
        for k in range(K):
            pick = jnp.where(own == codes[k : k + 1, :], 1.0, 0.0).astype(BF16)
            acc = acc + nn(pick, e[pl.ds(k * MESH, MESH), :])
        gsend[...] = acc
    gsend_b[...] = gsend[...].astype(BF16)
    gl = cot[...].astype(F32) + nt(gsend_b[...], w[4]) + nt(grecv_b[...], w[5])
    gl_b[...] = gl.astype(BF16)
    gl_out[...] = gl_b[...]
    gsec_b[...] = (nt(gl_b[...], w[3]) * slope2[...].astype(F32)).astype(BF16)
    ga_b[...] = nt(gsec_b[...], w[2]).astype(BF16)
    gm_b[...] = nt(ga_b[...], w[1]).astype(BF16)
    gm_own[...] = gm_b[...]


ZROWS = 512
BROWS = 224


def mesh_weights(pos, ah, agg, sq, lat, summed, ga, gsec, gl, gsend, grecv, cot, keep, give):
    rep = place(pos)[2]
    pairs = ((ah, ga), (agg, gsec), (sq, gl), (lat, gsend), (lat, grecv), (summed, cot))
    for out, h in ((give, 1 - rep), (keep, rep)):
        cols = pl.ds(pl.multiple_of(h * 256, 256), 256)
        for w, (left, right) in enumerate(pairs):
            part = tn(left[pl.ds(0, MESH), :], right[:, cols]).astype(BF16)
            for c in range(2):
                for b in range(16):
                    if w < 2:
                        at = NZ * ZROWS + b * 128 + w * 64 + c * 32
                    else:
                        at = (c * 4 + w - 2) * ZROWS + b * 32
                    out[pl.ds(at, 32), :] = part[b * 32 : b * 32 + 32, c * 128 : c * 128 + 128]


def pair_sum(a, b, out, moved):
    for dst, base in ((out, 0), (moved, NZ * ZROWS)):

        @pl.loop(0, dst.shape[0], step=64)
        def _(at):
            at = pl.multiple_of(at, 64)
            rows = pl.ds(base + at, 64)
            dst[pl.ds(at, 64), :] = (a[rows, :].astype(F32) + b[rows, :].astype(F32)).astype(BF16)


def return_pick(pos, table, g0, g1, g2, g3, r0, r1, r2, r3):
    own1, own2, rep, _ = place(pos)
    sources = (g0, g1, g2, g3)
    for k, r in enumerate((r0, r1, r2, r3)):
        j = (4 - k) % 4
        for i in range(GB):
            d1, d2, blk = split_code(table[j * GB + i], rep)
            at = (own2 - d2) & 3
            for n in range(4):

                @pl.when((d1 == own1) & (at == n))
                def _():
                    start = pl.multiple_of(blk * BLK, BLK)
                    r[pl.ds(i * BLK, BLK), :] = sources[n][pl.ds(start, BLK), :]


def grid_backward(pos, tb, r0, r1, r2, r3, x, slot, slope, gf, keep, give, picked):
    own1, _, rep, _ = place(pos)
    row = lax.broadcasted_iota(I32, (BLK, BLK), 0)
    for i in range(GB):
        d1, _, _ = split_code(tb[i] * 2, rep)
        at = (own1 - d1) & 3
        rows = pl.ds(i * BLK, BLK)
        for n, r in enumerate((r0, r1, r2, r3)):

            @pl.when(at == n)
            def _():
                picked[rows, :] = r[rows, :]

    for i in range(GB):
        rows = pl.ds(i * BLK, BLK)
        pick = jnp.where(row == slot[i : i + 1, :], 1.0, 0.0).astype(BF16)
        gf[rows, :] = (tn(pick, picked[rows, :]) * slope[rows, :].astype(F32)).astype(BF16)
    for out, h in ((give, 1 - rep), (keep, rep)):
        cols = pl.ds(pl.multiple_of(h * 256, 256), 256)
        part = tn(x[...], gf[:, cols]).astype(BF16)
        for b in range(16):
            for c in range(2):
                out[b, pl.ds(c * 32, 32), :] = part[b * 32 : b * 32 + 32, c * 128 : c * 128 + 128]


def grid_output(gf, w, out):
    out[...] = nt(gf[...], w[0]).astype(BF16)


def first_input(pos, keep, other, moved, zparts, *outs):
    own1, own2, rep, _ = place(pos)
    for k, out in enumerate(outs):
        for j in range(4):
            d, e = (own1 + k) & 3, (own2 + j) & 3
            b = jnp.where(rep == 0, d * 4 + e, e * 4 + d)
            out[pl.ds(j * BROWS, 64), :] = (keep[b].astype(F32) + other[b].astype(F32)).astype(BF16)
            rows = pl.ds(pl.multiple_of(b * 128, 128), 128)
            out[pl.ds(j * BROWS + 64, 128), :] = moved[rows, :]
            rows = pl.ds(pl.multiple_of(b * 32, 32), 32)
            total = zparts[0, rows, :].astype(F32)
            for z in range(1, NZ):
                total = total + zparts[z, rows, :].astype(F32)
            out[pl.ds(j * BROWS + 192, 32), :] = total.astype(BF16)


def first_sum(a, b, c, d, *outs):
    for j, out in enumerate(outs):
        rows = pl.ds(j * BROWS, BROWS)
        total = a[rows, :].astype(F32) + b[rows, :].astype(F32)
        out[...] = (total + c[rows, :].astype(F32) + d[rows, :].astype(F32)).astype(BF16)


def band_sum(a, b, c, d, out):
    total = a[...].astype(F32) + b[...].astype(F32) + c[...].astype(F32) + d[...].astype(F32)
    done = total.astype(BF16)
    for j in range(NZ):
        out[j] = done


def z_collect(parts, out):
    total = parts[0, 0:192, :].astype(F32)
    for j in range(1, NZ):
        total = total + parts[j, 0:192, :].astype(F32)
    out[pl.ds(0, 192), :] = total.astype(BF16)
    for j in range(NZ):
        out[pl.ds(192 + 32 * j, 32), :] = parts[j, 192:224, :]


def finish(pos, mine, other, out, *, grid_scale, mesh_scale):
    rep = place(pos)[2]
    for src, h in ((mine, rep), (other, 1 - rep)):
        for c in range(2):
            cols = pl.ds(pl.multiple_of(h * 256 + c * 128, 128), 128)
            for w in range(7):
                at = w * 64 + c * 32 if w < 3 else 192 + 32 * (c * 4 + w - 3)
                scale = grid_scale if w < 2 else mesh_scale
                out[w, :, cols] = src[pl.ds(at, 32), :].astype(F32) * scale


def body(
    grid_latents, mesh_latents, weights, target_band, target_block, node_slot, neighbours, mesh_cotangent
):
    grid_scale = 1.0 / math.sqrt(NR * GB * BLK * NX * NY * NZ)
    mesh_scale = 1.0 / math.sqrt(NR * MESH * NX * NY * NZ)
    band = lax.axis_index("band")
    patch = lax.axis_index("patch")
    rep = lax.axis_index("rep")
    bx, by = band >> 2, band & 3
    pos = jnp.where(rep == 0, bx | (by << 2), by | (bx << 2)) | (rep << 4) | ((band * NZ + patch) << 5)
    pos = pos.astype(I32).reshape(1)
    x = grid_latents[0]
    ml = mesh_latents[0]
    cot = mesh_cotangent[0]
    tb = target_band.reshape(GB)
    tk = target_block
    slot = node_slot.reshape(GB, BLK)
    ring = NX * NY * NZ
    up = [(i, (i + 1) % ring) for i in range(ring)]
    down = [((i + 1) % ring, i) for i in range(ring)]
    tie = lax.optimization_barrier

    cp = lax.ppermute(cot, ("band", "patch"), up)
    cn = lax.ppermute(cot, ("band", "patch"), down)
    p0, slope1 = call(
        grid_forward,
        [(tb, 1), (tk, 1), (x, 0), (weights, 2), (slot, 0)],
        [((GB * BLK + META, LAT), BF16, 0), ((GB * BLK, LAT), BF16, 0)],
        limit=60,
        grid=(1,),
        flops=2 * 512**3,
    )
    p = [p0] + [first(p0, k) for k in (1, 2, 3)]

    near, _ = tie((neighbours.T, p0))
    row, col, code_up, code_down = call(
        edge_codes,
        [(pos, 1), (near, 0)],
        [((META, MESH), F32, 0), ((MESH, META), F32, 0), ((META, LAT), BF16, 0), ((META, LAT), BF16, 0)],
        flops=10**6,
    )

    mesh_bf = ((MESH, LAT), BF16, 0)
    mesh_f = ((MESH, LAT), F32, 0)
    pay = ((MESH + META, LAT), BF16, 0)
    gs = call(
        cot_tables,
        [(cot, 0), (cp, 0), (cn, 0), (weights, 0)],
        [((3 * MESH, LAT), F32, 0)],
        flops=6 * 256 * 512 * 512,
    )[0]
    p[1], gs, row, col = tie((p[1], gs, row, col))
    q0, q1, q2, q3, table = call(
        route_sum,
        [(pos, 1)] + [(v, 0) for v in p],
        [mesh_f, mesh_bf, mesh_bf, mesh_bf, ((16,), I32, 1)],
        scratch=[pltpu.VMEM((8, BLK, LAT), F32)],
        flops=2 * 512**3,
    )
    got = [second(q, k) for k, q in ((1, q1), (2, q2), (3, q3))]
    ah, agg, sq, slope2, lat_up, lat_down = call(
        mesh_forward,
        [(v, 0) for v in (q0, *got, ml)] + [(weights, 0), (code_up, 0), (code_down, 0)],
        [mesh_bf] * 4 + [pay] * 2,
        flops=6 * 256 * 512 * 512,
    )
    lp = lax.ppermute(lat_up, ("band", "patch"), up)
    ln = lax.ppermute(lat_down, ("band", "patch"), down)
    snd, rcv = call(
        own_tables,
        [(lat_up, 0), (weights, 0)],
        [mesh_bf, mesh_f],
        flops=4 * 256 * 512 * 512
    )
    summed, gsend, grecv, gl, gsec, ga, gm, gl_out, gm_own = call(
        edges_backward,
        [(v, 0) for v in (lp, ln, snd, rcv, col, row, gs, cot, slope2)] + [(weights, 0)],
        [mesh_bf] * 9,
        scratch=[
            pltpu.VMEM((3 * MESH, LAT), BF16),
            pltpu.VMEM((2 * MESH, LAT), F32),
            pltpu.VMEM((MESH, META), F32),
            pltpu.VMEM((K * MESH, LAT), BF16),
            pltpu.VMEM((MESH, LAT), F32),
        ],
        flops=5 * 10**9,
        limit=16,
    )
    g = [gm_own] + [second(gm, k) for k in (1, 2, 3)]


    keep, give = call(
        mesh_weights,
        [(pos, 1)]
        + [(v, 0) for v in (ah, agg, sq, lat_up, summed, ga, gsec, gl, gsend, grecv, cot)],
        [((6144, 128), BF16, 0)] * 2,
        flops=12 * 256 * 512 * 512,
    )
    swap = [(0, 1), (1, 0)]
    other = lax.ppermute(give, "rep", swap)
    r = call(
        return_pick,
        [(pos, 1), (table, 1)] + [(v, 0) for v in g],
        [((GB * BLK, LAT), BF16, 0)] * 4,
        flops=RETURN_FLOPS,
    )
    rr = [r[0]] + [first(r[k], k) for k in (1, 2, 3)]
    both, moved = call(
        pair_sum,
        [(keep, 0), (other, 0)],
        [((NZ * ZROWS, 128), BF16, 0), ((2048, 128), BF16, 0)],
        flops=10**6,
    )
    zparts = lax.all_to_all(both, "patch", split_axis=0, concat_axis=0, tiled=True)
    zparts = zparts.reshape(NZ, ZROWS, 128)
    gf, keep1, give1 = call(
        grid_backward,
        [(pos, 1), (tb, 1)] + [(v, 0) for v in (*rr, x, slot, slope1)],
        [((GB * BLK, LAT), BF16, 0)] + [((16, 64, 128), BF16, 0)] * 2,
        scratch=[pltpu.VMEM((GB * BLK, LAT), BF16)],
        flops=4 * 512**3,
    )
    other1 = lax.ppermute(give1, "rep", swap)
    grid_grad = call(
        grid_output,
        [(gf, 0), (weights, 0)],
        [((GB * BLK, LAT), BF16, 0)],
        flops=2 * 512**3,
    )[0]
    keep1, grid_grad = tie((keep1, grid_grad))
    f = call(
        first_input,
        [(pos, 1)] + [(v, 0) for v in (keep1, other1, moved, zparts)],
        [((4 * BROWS, 128), BF16, 0)] * 4,
        flops=10**6,
    )
    f = [f[0]] + [first(f[k], k) for k in (1, 2, 3)]
    t = call(first_sum, [(v, 0) for v in f], [((BROWS, 128), BF16, 0)] * 4, flops=10**6)
    t = [t[0]] + [second(t[k], k) for k in (1, 2, 3)]
    spread = call(band_sum, [(v, 0) for v in t], [((NZ, BROWS, 128), BF16, 0)], flops=10**6)[0]
    over_z = lax.all_to_all(spread, "patch", split_axis=0, concat_axis=0, tiled=True)
    half_part = call(z_collect, [(over_z, 0)], [((448, 128), BF16, 0)], flops=10**6)[0]
    half_other = lax.ppermute(half_part, "rep", swap)

    def last(pos, mine, other, out):
        finish(pos, mine, other, out, grid_scale=grid_scale, mesh_scale=mesh_scale)

    weight_part = call(
        last, [(pos, 1), (half_part, 0), (half_other, 0)], [((7, 32, LAT), F32, 0)], flops=10**6
    )[0]
    return (grid_grad[None], gl_out[None], weight_part)


def solution(mesh):
    return jax.shard_map(
        body,
        mesh=mesh,
        in_specs=(
            P("rep", ("band", "patch"), None),
            P("rep", ("band", "patch"), None),
            P(),
            P(("band", "patch"), None),
            P(("band", "patch")),
            P(("band", "patch")),
            P(("band", "patch"), None),
            P("rep", ("band", "patch"), None),
        ),
        out_specs=(
            P("rep", ("band", "patch"), None),
            P("rep", ("band", "patch"), None),
            P(None, "band", None),
        ),
        check_vma=False,
    )
```

time: 181 us -> 147 us (0.81)
  local copies, waits for them, and re-layouts: 13.4 us -> 2.47 us
  waiting for transfers between devices: 70.2 us -> 61.2 us
  Pallas kernels: 29.6 us -> 22.4 us
  starting transfers between devices: 49 us -> 45.5 us
  other arithmetic: 3.16 us -> 0 us
    all_to_all x1 -> x0, waiting for transfers between devices: 20.1 us -> none  [body(): lax.all_to_all(spread, ('patch', 'rep'), split_axis=0, concat_axis=0, til...]
    ppermute x5 -> x7, waiting for transfers between devices: 8.32 us -> 24 us  [the longest x1 7.34 us: body(): lp = lax.ppermute(lat_up, ('band', 'patch'), up)]
    ppermute x6 -> x9, waiting for transfers between devices: 28.1 us -> 19.9 us  [first(): return lax.ppermute(v, ALL, shifts(k, False))]
    all_to_all x1 -> x0, starting transfers between devices: 8.17 us -> none  [body(): lax.all_to_all(spread, ('patch', 'rep'), split_axis=0, concat_axis=0, til...]
    pallas_call x13 -> x17, Pallas kernels: 29.6 us -> 22.4 us  [call(): pl.pallas_call(kernel, out_shape=out_shape, in_specs=specs_in, out_specs=...]
    unnamed x52 -> x22, local copies, waits for them, and re-layouts: 8.78 us -> 2.47 us
    ppermute x6 -> x9, waiting for transfers between devices: 6.87 us -> 11.5 us  [second(): return lax.ppermute(v, ALL, shifts(k, True))]
    ppermute x6 -> x9, starting transfers between devices: 7.35 us -> 10.9 us  [first(): return lax.ppermute(v, ALL, shifts(k, False))]
  transfers between devices with their start and end apart: 19 -> 26, of which waited for: 11 -> 16; matrix products, arithmetic and copies ran while one was open for 2% -> 0% of each run, Pallas kernels for 5% -> 5%
where the time goes in v2:
time: 147 us
  waiting for transfers between devices  61.2 us (42%)
  starting transfers between devices  45.5 us (31%)
  Pallas kernels  22.4 us (15%)
  blocking collectives  14.5 us (10%)
  local copies, waits for them, and re-layouts  2.47 us (2%)
    pallas_call x17, Pallas kernels, call(): pl.pallas_call(kernel, out_shape=out_shape, in_specs=specs_in, out_specs=...  22.4 us
    ppermute x9, waiting for transfers between devices, first(): return lax.ppermute(v, ALL, shifts(k, False))  19.9 us
    all_to_all x1, blocking collectives, body(): lax.all_to_all(spread, 'patch', split_axis=0, concat_axis=0, tiled=True)  14.5 us
    ppermute x9, waiting for transfers between devices, second(): return lax.ppermute(v, ALL, shifts(k, True))  11.5 us
    ppermute x9, starting transfers between devices, first(): return lax.ppermute(v, ALL, shifts(k, False))  10.9 us
    ppermute x1, starting transfers between devices, body(): cn = lax.ppermute(cot, ('band', 'patch'), down)  8.26 us
    ppermute x1, waiting for transfers between devices, body(): lp = lax.ppermute(lat_up, ('band', 'patch'), up)  7.34 us
    ppermute x1, waiting for transfers between devices, body(): cp = lax.ppermute(cot, ('band', 'patch'), up)  7.31 us
  transfers between devices with their start and end apart: 26, of which 16 were waited for; matrix products, arithmetic and copies ran while one was open for 0% of the time, Pallas kernels for 5%

profile of v2, /device:TPU:1, one launch (start us, length us, event | category | flops | bytes accessed | tf_op | source)
XLA Modules:
  0.0 147.0 jit_solution(2497220832320387470)
XLA Ops:
  0.7 3.4 %shard_map.103 = (bf16[528,512]{1,0:T(8,128)(2,1)}, bf16[512,512]{1,0:T(8,128)(2,1)}) custom-call(s32[4]{0:T(128)} %bitcast.21, s32[4]{0:T(128)} %tk.1, bf16[512,512]{1,0:T(8,128)(2,1)} %bitcast.10, bf16[7,512,512]{2,1,0:T(8,128)(2,1)} %w.11, s32[4,128]{1,0:T(4,128)} %bitcast.18), custom_call_target="tpu_custom_call" | custom-call | flops 268435456 | bytes 1000000 | tf_op jit(solution)/shard_map/pallas_call | solution.py:47
  4.1 2.1 %collective-permute-start = (bf16[528,512]{1,0:T(8,128)(2,1)}, bf16[528,512]{1,0:T(8,128)(2,1)S(1)}, u32[]{:S(2)}, u32[]{:S(2)}) collective-permute-start(bf16[528,512]{1,0:T(8,128)(2,1)} %get-tuple-element.57.p0), channel_id=1, source_target_pairs={{0,64},{1,17},{2,66},{3,19},{4,68},{5,21},{6,70},{7,23},{8,72},{9,... | collective-permute-start | bytes 1622024 | tf_op jit(solution)/shard_map/ppermute | solution.py:76
  6.2 1.4 collective-permute-start.4
  7.6 1.6 %collective-permute-start.3 = (bf16[528,512]{1,0:T(8,128)(2,1)}, bf16[528,512]{1,0:T(8,128)(2,1)S(1)}, u32[]{:S(2)}, u32[]{:S(2)}) collective-permute-start(bf16[528,512]{1,0:T(8,128)(2,1)} %get-tuple-element.57.p0), channel_id=1, source_target_pairs={{0,128},{1,33},{2,130},{3,35},{4,132},{5,37},{6,134},{7,39},{8,136... | collective-permute-start | bytes 1622024 | tf_op jit(solution)/shard_map/ppermute | solution.py:76
  9.3 8.3 %collective-permute-start.2 = (bf16[256,512]{1,0:T(8,128)(2,1)S(1)}, bf16[256,512]{1,0:T(8,128)(2,1)S(1)}, u32[]{:S(2)}, u32[]{:S(2)}) collective-permute-start(bf16[256,512]{1,0:T(8,128)(2,1)S(1)} %bitcast.13), channel_id=1, source_target_pairs={{2,0},{4,2},{6,4},{8,6},{10,8},{12,10},{14,12},{16,14},{18,16},{20... | collective-permute-start | bytes 786440 | tf_op jit(solution)/shard_map/ppermute | solution.py:386
  17.7 3.8 %collective-permute-done.2.cn = bf16[256,512]{1,0:T(8,128)(2,1)S(1)} collective-permute-done((bf16[256,512]{1,0:T(8,128)(2,1)S(1)}, bf16[256,512]{1,0:T(8,128)(2,1)S(1)}, u32[]{:S(2)}, u32[]{:S(2)}) %collective-permute-start.2) | collective-permute-done | bytes 262176 | tf_op jit(solution)/shard_map/ppermute | solution.py:386
  21.5 7.3 %collective-permute-done.1.cp = bf16[256,512]{1,0:T(8,128)(2,1)S(1)} collective-permute-done((bf16[256,512]{1,0:T(8,128)(2,1)S(1)}, bf16[256,512]{1,0:T(8,128)(2,1)S(1)}, u32[]{:S(2)}, u32[]{:S(2)}) %collective-permute-start.1) | collective-permute-done | bytes 262176 | tf_op jit(solution)/shard_map/ppermute | solution.py:385
  28.8 2.0 %copy-done = bf16[7,512,512]{2,1,0:T(8,128)(2,1)S(1)} copy-done((bf16[7,512,512]{2,1,0:T(8,128)(2,1)S(1)}, bf16[7,512,512]{2,1,0:T(8,128)(2,1)}, u32[]{:S(2)}) %copy-start) | copy-done | bytes 3670040
  33.3 2.4 %collective-permute-start.7 = (bf16[256,512]{1,0:T(8,128)(2,1)S(1)}, bf16[256,512]{1,0:T(8,128)(2,1)S(1)}, u32[]{:S(2)}, u32[]{:S(2)}) collective-permute-start(bf16[256,512]{1,0:T(8,128)(2,1)S(1)} %get-tuple-element.66), channel_id=1, source_target_pairs={{0,48},{1,193},{2,50},{3,195},{4,52},{5,197},{6,54},{7,199},{8,56}... | collective-permute-start | bytes 786440 | tf_op jit(solution)/shard_map/ppermute | solution.py:80
  35.7 6.9 %collective-permute-done.5.r1 = bf16[256,512]{1,0:T(8,128)(2,1)S(1)} collective-permute-done((bf16[256,512]{1,0:T(8,128)(2,1)S(1)}, bf16[256,512]{1,0:T(8,128)(2,1)S(1)}, u32[]{:S(2)}, u32[]{:S(2)}) %collective-permute-start.5) | collective-permute-done | bytes 262176 | tf_op jit(solution)/shard_map/ppermute | solution.py:80
  44.0 4.8 %collective-permute-start.9 = (bf16[272,512]{1,0:T(8,128)(2,1)S(1)}, bf16[272,512]{1,0:T(8,128)(2,1)S(1)}, u32[]{:S(2)}, u32[]{:S(2)}) collective-permute-start(bf16[272,512]{1,0:T(8,128)(2,1)S(1)} %get-tuple-element.70), channel_id=1, source_target_pairs={{2,0},{4,2},{6,4},{8,6},{10,8},{12,10},{14,12},{16,14},{18,16},{20... | collective-permute-start | bytes 835592 | tf_op jit(solution)/shard_map/ppermute | solution.py:430
  49.2 3.0 %collective-permute-done.9.ln = bf16[272,512]{1,0:T(8,128)(2,1)S(1)} collective-permute-done((bf16[272,512]{1,0:T(8,128)(2,1)S(1)}, bf16[272,512]{1,0:T(8,128)(2,1)S(1)}, u32[]{:S(2)}, u32[]{:S(2)}) %collective-permute-start.9) | collective-permute-done | bytes 278560 | tf_op jit(solution)/shard_map/ppermute | solution.py:430
  52.3 7.3 %collective-permute-done.8.lp = bf16[272,512]{1,0:T(8,128)(2,1)S(1)} collective-permute-done((bf16[272,512]{1,0:T(8,128)(2,1)S(1)}, bf16[272,512]{1,0:T(8,128)(2,1)S(1)}, u32[]{:S(2)}, u32[]{:S(2)}) %collective-permute-start.8) | collective-permute-done | bytes 278560 | tf_op jit(solution)/shard_map/ppermute | solution.py:429
  59.6 8.1 %shard_map.109 = (bf16[256,512]{1,0:T(8,128)(2,1)S(1)}, bf16[256,512]{1,0:T(8,128)(2,1)S(1)}, bf16[256,512]{1,0:T(8,128)(2,1)S(1)}, bf16[256,512]{1,0:T(8,128)(2...) custom-call(bf16[272,512]{1,0:T(8,128)(2,1)S(1)} %collective-permute, ...), custom_call_target="tpu_custom_call" | custom-call | flops 5000000000 | bytes 1000000 | tf_op jit(solution)/shard_map/pallas_call | solution.py:47
  68.7 3.8 %collective-permute-start.17 = (bf16[6144,128]{1,0:T(8,128)(2,1)S(1)}, bf16[6144,128]{1,0:T(8,128)(2,1)S(1)}, u32[]{:S(2)}, u32[]{:S(2)}) collective-permute-start(bf16[6144,128]{1,0:T(8,128)(2,1)S(1)} %get-tuple-element.100), channel_id=1, source_target_pairs={{0,1},{1,0},{2,3},{3,2},{4,5},{5,4},{6,7},{7,6},{8,9},{9,8},{10,11... | collective-permute-start | bytes 4718600 | tf_op jit(solution)/shard_map/ppermute | solution.py:462
  72.5 1.5 collective-permute-start.10
  74.0 1.6 %collective-permute-done.17.b = bf16[6144,128]{1,0:T(8,128)(2,1)S(1)} collective-permute-done((bf16[6144,128]{1,0:T(8,128)(2,1)S(1)}, bf16[6144,128]{1,0:T(8,128)(2,1)S(1)}, u32[]{:S(2)}, u32[]{:S(2)}) %collective-permute-start.17) | collective-permute-done | bytes 1572896 | tf_op jit(solution)/shard_map/ppermute | solution.py:462
  75.5 1.9 %shard_map.114 = (bf16[4096,128]{1,0:T(8,128)(2,1)}, bf16[2048,128]{1,0:T(8,128)(2,1)S(1)}) custom-call(bf16[6144,128]{1,0:T(8,128)(2,1)S(1)} %get-tuple-element.99.a, bf16[6144,128]{1,0:T(8,128)(2,1)S(1)} %collective-permute-done.17.b), custom_call_target="tpu_custom_call" | custom-call | flops 1000000 | bytes 1000000 | tf_op jit(solution)/shard_map/pallas_call | solution.py:47
  77.5 3.6 %all-to-all-start = ((bf16[8,512,128]{2,1,0:T(8,128)(2,1)}), bf16[8,512,128]{2,1,0:T(8,128)(2,1)S(1)}, u32[]{:S(2)}, u32[]{:S(2)}) async-start(bf16[8,512,128]{2,1,0:T(8,128)(2,1)} %bitcast.9), calls=%async_computation | async-start | bytes 2097152 | tf_op jit(solution)/shard_map/all_to_all | solution.py:476
  81.0 1.3 collective-permute-done.10.g1
  83.8 2.6 %collective-permute-start.15 = (bf16[512,512]{1,0:T(8,128)(2,1)S(1)}, bf16[512,512]{1,0:T(8,128)(2,1)S(1)}, u32[]{:S(2)}, u32[]{:S(2)}) collective-permute-start(bf16[512,512]{1,0:T(8,128)(2,1)S(1)} %get-tuple-element.82), channel_id=1, source_target_pairs={{0,192},{1,49},{2,194},{3,51},{4,196},{5,53},{6,198},{7,55},{8,200... | collective-permute-start | bytes 1572872 | tf_op jit(solution)/shard_map/ppermute | solution.py:76
  86.4 12.5 %collective-permute-done.13.r1 = bf16[512,512]{1,0:T(8,128)(2,1)S(1)} collective-permute-done((bf16[512,512]{1,0:T(8,128)(2,1)S(1)}, bf16[512,512]{1,0:T(8,128)(2,1)S(1)}, u32[]{:S(2)}, u32[]{:S(2)}) %collective-permute-start.13) | collective-permute-done | bytes 524320 | tf_op jit(solution)/shard_map/ppermute | solution.py:76
  99.5 1.4 shard_map.111
  100.9 2.2 %collective-permute-start.16 = (bf16[16,64,128]{2,1,0:T(8,128)(2,1)S(1)}, bf16[16,64,128]{2,1,0:T(8,128)(2,1)S(1)}, u32[]{:S(2)}, u32[]{:S(2)}) collective-permute-start(bf16[16,64,128]{2,1,0:T(8,128)(2,1)S(1)} %get-tuple-element.89), channel_id=1, source_target_pairs={{0,1},{1,0},{2,3},{3,2},{4,5},{5,4},{6,7},{7,6},{8,9},{9,8},{10,11... | collective-permute-start | bytes 786440 | tf_op jit(solution)/shard_map/ppermute | solution.py:485
  103.2 1.3 shard_map.112
  104.4 5.8 %all-to-all-done.zparts = bf16[8,512,128]{2,1,0:T(8,128)(2,1)S(1)} async-done(((bf16[8,512,128]{2,1,0:T(8,128)(2,1)}), bf16[8,512,128]{2,1,0:T(8,128)(2,1)S(1)}, u32[]{:S(2)}, u32[]{:S(2)}) %all-to-all-start) | async-done | bytes 1048608 | tf_op jit(solution)/shard_map/all_to_all | solution.py:476
  110.6 2.6 %collective-permute-start.20 = (bf16[896,128]{1,0:T(8,128)(2,1)S(1)}, bf16[896,128]{1,0:T(8,128)(2,1)S(1)}, u32[]{:S(2)}, u32[]{:S(2)}) collective-permute-start(bf16[896,128]{1,0:T(8,128)(2,1)S(1)} %get-tuple-element.106), channel_id=1, source_target_pairs={{0,192},{1,49},{2,194},{3,51},{4,196},{5,53},{6,198},{7,55},{8,200... | collective-permute-start | bytes 688136 | tf_op jit(solution)/shard_map/ppermute | solution.py:76
  113.2 6.2 %collective-permute-done.18.b = bf16[896,128]{1,0:T(8,128)(2,1)S(1)} collective-permute-done((bf16[896,128]{1,0:T(8,128)(2,1)S(1)}, bf16[896,128]{1,0:T(8,128)(2,1)S(1)}, u32[]{:S(2)}, u32[]{:S(2)}) %collective-permute-start.18) | collective-permute-done | bytes 229408 | tf_op jit(solution)/shard_map/ppermute | solution.py:76
  120.7 2.1 %collective-permute-start.23 = (bf16[224,128]{1,0:T(8,128)(2,1)S(1)}, bf16[224,128]{1,0:T(8,128)(2,1)S(1)}, u32[]{:S(2)}, u32[]{:S(2)}) collective-permute-start(bf16[224,128]{1,0:T(8,128)(2,1)S(1)} %get-tuple-element.110), channel_id=1, source_target_pairs={{0,48},{1,193},{2,50},{3,195},{4,52},{5,197},{6,54},{7,199},{8,56}... | collective-permute-start | bytes 172040 | tf_op jit(solution)/shard_map/ppermute | solution.py:80
  122.8 2.2 %collective-permute-done.21.b = bf16[224,128]{1,0:T(8,128)(2,1)S(1)} collective-permute-done((bf16[224,128]{1,0:T(8,128)(2,1)S(1)}, bf16[224,128]{1,0:T(8,128)(2,1)S(1)}, u32[]{:S(2)}, u32[]{:S(2)}) %collective-permute-start.21) | collective-permute-done | bytes 57376 | tf_op jit(solution)/shard_map/ppermute | solution.py:80
  125.6 14.5 %all_to_all.14.parts = bf16[8,224,128]{2,1,0:T(8,128)(2,1)S(1)} all-to-all(bf16[8,224,128]{2,1,0:T(8,128)(2,1)S(1)} %shard_map.117), channel_id=1, replica_groups=mesh['band'=16,'patch'=8,'rep'=2] {'patch'}, dimensions={0} | all-to-all | bytes 917504 | tf_op jit(solution)/shard_map/all_to_all | solution.py:503
  140.2 5.0 %collective-permute-start.24 = (bf16[448,128]{1,0:T(8,128)(2,1)S(1)}, bf16[448,128]{1,0:T(8,128)(2,1)S(1)}, u32[]{:S(2)}, u32[]{:S(2)}) collective-permute-start(bf16[448,128]{1,0:T(8,128)(2,1)S(1)} %shard_map.118.mine), channel_id=1, source_target_pairs={{0,1},{1,0},{2,3},{3,2},{4,5},{5,4},{6,7},{7,6},{8,9},{9,8},{10,11... | collective-permute-start | bytes 344072 | tf_op jit(solution)/shard_map/ppermute | solution.py:505
  (60 shorter events, 11.8 us)
Async XLA Ops:
  0.6 16.9 %copy-start.9 = (s32[256,6]{0,1:T(8,128)S(1)}, s32[256,6]{0,1:T(8,128)}, u32[]{:S(2)}) copy-start(s32[256,6]{0,1:T(8,128)} %param.14) | copy-start | bytes 18436
  4.1 27.4 %collective-permute-start = (bf16[528,512]{1,0:T(8,128)(2,1)}, bf16[528,512]{1,0:T(8,128)(2,1)S(1)}, u32[]{:S(2)}, u32[]{:S(2)}) collective-permute-start(bf16[528,512]{1,0:T(8,128)(2,1)} %get-tuple-element.57.p0), channel_id=1, source_target_pairs={{0,64},{1,17},{2,66},{3,19},{4,68},{5,21},{6,70},{7,23},{8,72},{9,... | collective-permute-start | bytes 1622024 | tf_op jit(solution)/shard_map/ppermute | solution.py:76
  6.2 25.3 %collective-permute-start.4 = (bf16[528,512]{1,0:T(8,128)(2,1)}, bf16[528,512]{1,0:T(8,128)(2,1)S(1)}, u32[]{:S(2)}, u32[]{:S(2)}) collective-permute-start(bf16[528,512]{1,0:T(8,128)(2,1)} %get-tuple-element.57.p0), channel_id=1, source_target_pairs={{0,192},{1,49},{2,194},{3,51},{4,196},{5,53},{6,198},{7,55},{8,200... | collective-permute-start | bytes 1622024 | tf_op jit(solution)/shard_map/ppermute | solution.py:76
  7.6 23.9 %collective-permute-start.3 = (bf16[528,512]{1,0:T(8,128)(2,1)}, bf16[528,512]{1,0:T(8,128)(2,1)S(1)}, u32[]{:S(2)}, u32[]{:S(2)}) collective-permute-start(bf16[528,512]{1,0:T(8,128)(2,1)} %get-tuple-element.57.p0), channel_id=1, source_target_pairs={{0,128},{1,33},{2,130},{3,35},{4,132},{5,37},{6,134},{7,39},{8,136... | collective-permute-start | bytes 1622024 | tf_op jit(solution)/shard_map/ppermute | solution.py:76
  9.3 12.2 %collective-permute-start.2 = (bf16[256,512]{1,0:T(8,128)(2,1)S(1)}, bf16[256,512]{1,0:T(8,128)(2,1)S(1)}, u32[]{:S(2)}, u32[]{:S(2)}) collective-permute-start(bf16[256,512]{1,0:T(8,128)(2,1)S(1)} %bitcast.13), channel_id=1, source_target_pairs={{2,0},{4,2},{6,4},{8,6},{10,8},{12,10},{14,12},{16,14},{18,16},{20... | collective-permute-start | bytes 786440 | tf_op jit(solution)/shard_map/ppermute | solution.py:386
  17.5 11.3 %collective-permute-start.1 = (bf16[256,512]{1,0:T(8,128)(2,1)S(1)}, bf16[256,512]{1,0:T(8,128)(2,1)S(1)}, u32[]{:S(2)}, u32[]{:S(2)}) collective-permute-start(bf16[256,512]{1,0:T(8,128)(2,1)S(1)} %bitcast.14), channel_id=1, source_target_pairs={{0,2},{2,4},{4,6},{6,8},{8,10},{10,12},{12,14},{14,16},{16,18},{18... | collective-permute-start | bytes 786440 | tf_op jit(solution)/shard_map/ppermute | solution.py:385
  33.0 9.6 %collective-permute-start.5 = (bf16[256,512]{1,0:T(8,128)(2,1)S(1)}, bf16[256,512]{1,0:T(8,128)(2,1)S(1)}, u32[]{:S(2)}, u32[]{:S(2)}) collective-permute-start(bf16[256,512]{1,0:T(8,128)(2,1)S(1)} %get-tuple-element.64), channel_id=1, source_target_pairs={{0,16},{1,65},{2,18},{3,67},{4,20},{5,69},{6,22},{7,71},{8,24},{9,... | collective-permute-start | bytes 786440 | tf_op jit(solution)/shard_map/ppermute | solution.py:80
  33.0 9.5 %collective-permute-start.6 = (bf16[256,512]{1,0:T(8,128)(2,1)S(1)}, bf16[256,512]{1,0:T(8,128)(2,1)S(1)}, u32[]{:S(2)}, u32[]{:S(2)}) collective-permute-start(bf16[256,512]{1,0:T(8,128)(2,1)S(1)} %get-tuple-element.65), channel_id=1, source_target_pairs={{0,32},{1,129},{2,34},{3,131},{4,36},{5,133},{6,38},{7,135},{8,40}... | collective-permute-start | bytes 786440 | tf_op jit(solution)/shard_map/ppermute | solution.py:80
  33.3 9.9 %collective-permute-start.7 = (bf16[256,512]{1,0:T(8,128)(2,1)S(1)}, bf16[256,512]{1,0:T(8,128)(2,1)S(1)}, u32[]{:S(2)}, u32[]{:S(2)}) collective-permute-start(bf16[256,512]{1,0:T(8,128)(2,1)S(1)} %get-tuple-element.66), channel_id=1, source_target_pairs={{0,48},{1,193},{2,50},{3,195},{4,52},{5,197},{6,54},{7,199},{8,56}... | collective-permute-start | bytes 786440 | tf_op jit(solution)/shard_map/ppermute | solution.py:80
  44.0 8.3 %collective-permute-start.9 = (bf16[272,512]{1,0:T(8,128)(2,1)S(1)}, bf16[272,512]{1,0:T(8,128)(2,1)S(1)}, u32[]{:S(2)}, u32[]{:S(2)}) collective-permute-start(bf16[272,512]{1,0:T(8,128)(2,1)S(1)} %get-tuple-element.70), channel_id=1, source_target_pairs={{2,0},{4,2},{6,4},{8,6},{10,8},{12,10},{14,12},{16,14},{18,16},{20... | collective-permute-start | bytes 835592 | tf_op jit(solution)/shard_map/ppermute | solution.py:430
  48.8 10.8 %collective-permute-start.8 = (bf16[272,512]{1,0:T(8,128)(2,1)S(1)}, bf16[272,512]{1,0:T(8,128)(2,1)S(1)}, u32[]{:S(2)}, u32[]{:S(2)}) collective-permute-start(bf16[272,512]{1,0:T(8,128)(2,1)S(1)} %get-tuple-element.69.lat), channel_id=1, source_target_pairs={{0,2},{2,4},{4,6},{6,8},{8,10},{10,12},{12,14},{14,16},{16,18},{18... | collective-permute-start | bytes 835592 | tf_op jit(solution)/shard_map/ppermute | solution.py:429
  68.7 6.8 %collective-permute-start.17 = (bf16[6144,128]{1,0:T(8,128)(2,1)S(1)}, bf16[6144,128]{1,0:T(8,128)(2,1)S(1)}, u32[]{:S(2)}, u32[]{:S(2)}) collective-permute-start(bf16[6144,128]{1,0:T(8,128)(2,1)S(1)} %get-tuple-element.100), channel_id=1, source_target_pairs={{0,1},{1,0},{2,3},{3,2},{4,5},{5,4},{6,7},{7,6},{8,9},{9,8},{10,11... | collective-permute-start | bytes 4718600 | tf_op jit(solution)/shard_map/ppermute | solution.py:462
  72.5 8.5 %collective-permute-start.12 = (bf16[256,512]{1,0:T(8,128)(2,1)S(1)}, bf16[256,512]{1,0:T(8,128)(2,1)S(1)}, u32[]{:S(2)}, u32[]{:S(2)}) collective-permute-start(bf16[256,512]{1,0:T(8,128)(2,1)S(1)} %get-tuple-element.78), channel_id=1, source_target_pairs={{0,48},{1,193},{2,50},{3,195},{4,52},{5,197},{6,54},{7,199},{8,56}... | collective-permute-start | bytes 786440 | tf_op jit(solution)/shard_map/ppermute | solution.py:80
  72.5 8.5 %collective-permute-start.11 = (bf16[256,512]{1,0:T(8,128)(2,1)S(1)}, bf16[256,512]{1,0:T(8,128)(2,1)S(1)}, u32[]{:S(2)}, u32[]{:S(2)}) collective-permute-start(bf16[256,512]{1,0:T(8,128)(2,1)S(1)} %get-tuple-element.78), channel_id=1, source_target_pairs={{0,32},{1,129},{2,34},{3,131},{4,36},{5,133},{6,38},{7,135},{8,40}... | collective-permute-start | bytes 786440 | tf_op jit(solution)/shard_map/ppermute | solution.py:80
  72.5 9.8 %collective-permute-start.10 = (bf16[256,512]{1,0:T(8,128)(2,1)S(1)}, bf16[256,512]{1,0:T(8,128)(2,1)S(1)}, u32[]{:S(2)}, u32[]{:S(2)}) collective-permute-start(bf16[256,512]{1,0:T(8,128)(2,1)S(1)} %get-tuple-element.78), channel_id=1, source_target_pairs={{0,16},{1,65},{2,18},{3,67},{4,20},{5,69},{6,22},{7,71},{8,24},{9,... | collective-permute-start | bytes 786440 | tf_op jit(solution)/shard_map/ppermute | solution.py:80
  77.5 32.8 %all-to-all-start = ((bf16[8,512,128]{2,1,0:T(8,128)(2,1)}), bf16[8,512,128]{2,1,0:T(8,128)(2,1)S(1)}, u32[]{:S(2)}, u32[]{:S(2)}) async-start(bf16[8,512,128]{2,1,0:T(8,128)(2,1)} %bitcast.9), calls=%async_computation | async-start | bytes 2097152 | tf_op jit(solution)/shard_map/all_to_all | solution.py:476
  82.3 17.2 %copy-start.3 = (bf16[1,512,512]{2,1,0:T(8,128)(2,1)S(1)}, bf16[1,512,512]{2,1,0:T(8,128)(2,1)}, u32[]{:S(2)}) copy-start(bf16[1,512,512]{2,1,0:T(8,128)(2,1)} %param.8) | copy-start | bytes 1572868
  82.3 17.2 %copy-start.5 = (bf16[512,512]{1,0:T(8,128)(2,1)S(1)}, bf16[512,512]{1,0:T(8,128)(2,1)}, u32[]{:S(2)}) copy-start(bf16[512,512]{1,0:T(8,128)(2,1)} %get-tuple-element.83.slope) | copy-start | bytes 1572868
  82.4 17.2 %copy-start.8 = (s32[512]{0:T(512)S(1)}, s32[512]{0:T(512)}, u32[]{:S(2)}) copy-start(s32[512]{0:T(512)} %param.13) | copy-start | bytes 6148
  82.4 17.2 %copy-start.10 = (s32[4,1]{0,1:T(1,128)S(1)}, s32[4,1]{0,1:T(1,128)}, u32[]{:S(2)}) copy-start(s32[4,1]{0,1:T(1,128)} %param.11) | copy-start | bytes 52
  82.4 20.8 %copy-start.2 = (bf16[7,512,512]{2,1,0:T(8,128)(2,1)S(1)}, bf16[7,512,512]{2,1,0:T(8,128)(2,1)}, u32[]{:S(2)}) copy-start(bf16[7,512,512]{2,1,0:T(8,128)(2,1)} %w.11) | copy-start | bytes 11010052
  83.4 15.5 %collective-permute-start.13 = (bf16[512,512]{1,0:T(8,128)(2,1)S(1)}, bf16[512,512]{1,0:T(8,128)(2,1)S(1)}, u32[]{:S(2)}, u32[]{:S(2)}) collective-permute-start(bf16[512,512]{1,0:T(8,128)(2,1)S(1)} %get-tuple-element.80), channel_id=1, source_target_pairs={{0,64},{1,17},{2,66},{3,19},{4,68},{5,21},{6,70},{7,23},{8,72},{9,... | collective-permute-start | bytes 1572872 | tf_op jit(solution)/shard_map/ppermute | solution.py:76
  83.7 15.1 %collective-permute-start.14 = (bf16[512,512]{1,0:T(8,128)(2,1)S(1)}, bf16[512,512]{1,0:T(8,128)(2,1)S(1)}, u32[]{:S(2)}, u32[]{:S(2)}) collective-permute-start(bf16[512,512]{1,0:T(8,128)(2,1)S(1)} %get-tuple-element.81), channel_id=1, source_target_pairs={{0,128},{1,33},{2,130},{3,35},{4,132},{5,37},{6,134},{7,39},{8,136... | collective-permute-start | bytes 1572872 | tf_op jit(solution)/shard_map/ppermute | solution.py:76
  83.8 15.7 %collective-permute-start.15 = (bf16[512,512]{1,0:T(8,128)(2,1)S(1)}, bf16[512,512]{1,0:T(8,128)(2,1)S(1)}, u32[]{:S(2)}, u32[]{:S(2)}) collective-permute-start(bf16[512,512]{1,0:T(8,128)(2,1)S(1)} %get-tuple-element.82), channel_id=1, source_target_pairs={{0,192},{1,49},{2,194},{3,51},{4,196},{5,53},{6,198},{7,55},{8,200... | collective-permute-start | bytes 1572872 | tf_op jit(solution)/shard_map/ppermute | solution.py:76
  100.9 3.5 %collective-permute-start.16 = (bf16[16,64,128]{2,1,0:T(8,128)(2,1)S(1)}, bf16[16,64,128]{2,1,0:T(8,128)(2,1)S(1)}, u32[]{:S(2)}, u32[]{:S(2)}) collective-permute-start(bf16[16,64,128]{2,1,0:T(8,128)(2,1)S(1)} %get-tuple-element.89), channel_id=1, source_target_pairs={{0,1},{1,0},{2,3},{3,2},{4,5},{5,4},{6,7},{7,6},{8,9},{9,8},{10,11... | collective-permute-start | bytes 786440 | tf_op jit(solution)/shard_map/ppermute | solution.py:485
  110.4 8.9 %collective-permute-start.18 = (bf16[896,128]{1,0:T(8,128)(2,1)S(1)}, bf16[896,128]{1,0:T(8,128)(2,1)S(1)}, u32[]{:S(2)}, u32[]{:S(2)}) collective-permute-start(bf16[896,128]{1,0:T(8,128)(2,1)S(1)} %get-tuple-element.104), channel_id=1, source_target_pairs={{0,64},{1,17},{2,66},{3,19},{4,68},{5,21},{6,70},{7,23},{8,72},{9,... | collective-permute-start | bytes 688136 | tf_op jit(solution)/shard_map/ppermute | solution.py:76
  110.5 8.8 %collective-permute-start.19 = (bf16[896,128]{1,0:T(8,128)(2,1)S(1)}, bf16[896,128]{1,0:T(8,128)(2,1)S(1)}, u32[]{:S(2)}, u32[]{:S(2)}) collective-permute-start(bf16[896,128]{1,0:T(8,128)(2,1)S(1)} %get-tuple-element.105), channel_id=1, source_target_pairs={{0,128},{1,33},{2,130},{3,35},{4,132},{5,37},{6,134},{7,39},{8,136... | collective-permute-start | bytes 688136 | tf_op jit(solution)/shard_map/ppermute | solution.py:76
  110.6 9.3 %collective-permute-start.20 = (bf16[896,128]{1,0:T(8,128)(2,1)S(1)}, bf16[896,128]{1,0:T(8,128)(2,1)S(1)}, u32[]{:S(2)}, u32[]{:S(2)}) collective-permute-start(bf16[896,128]{1,0:T(8,128)(2,1)S(1)} %get-tuple-element.106), channel_id=1, source_target_pairs={{0,192},{1,49},{2,194},{3,51},{4,196},{5,53},{6,198},{7,55},{8,200... | collective-permute-start | bytes 688136 | tf_op jit(solution)/shard_map/ppermute | solution.py:76
  120.1 4.9 %collective-permute-start.21 = (bf16[224,128]{1,0:T(8,128)(2,1)S(1)}, bf16[224,128]{1,0:T(8,128)(2,1)S(1)}, u32[]{:S(2)}, u32[]{:S(2)}) collective-permute-start(bf16[224,128]{1,0:T(8,128)(2,1)S(1)} %get-tuple-element.108), channel_id=1, source_target_pairs={{0,16},{1,65},{2,18},{3,67},{4,20},{5,69},{6,22},{7,71},{8,24},{9,... | collective-permute-start | bytes 172040 | tf_op jit(solution)/shard_map/ppermute | solution.py:80
  120.2 4.8 %collective-permute-start.22 = (bf16[224,128]{1,0:T(8,128)(2,1)S(1)}, bf16[224,128]{1,0:T(8,128)(2,1)S(1)}, u32[]{:S(2)}, u32[]{:S(2)}) collective-permute-start(bf16[224,128]{1,0:T(8,128)(2,1)S(1)} %get-tuple-element.109), channel_id=1, source_target_pairs={{0,32},{1,129},{2,34},{3,131},{4,36},{5,133},{6,38},{7,135},{8,40}... | collective-permute-start | bytes 172040 | tf_op jit(solution)/shard_map/ppermute | solution.py:80
  120.7 4.9 %collective-permute-start.23 = (bf16[224,128]{1,0:T(8,128)(2,1)S(1)}, bf16[224,128]{1,0:T(8,128)(2,1)S(1)}, u32[]{:S(2)}, u32[]{:S(2)}) collective-permute-start(bf16[224,128]{1,0:T(8,128)(2,1)S(1)} %get-tuple-element.110), channel_id=1, source_target_pairs={{0,48},{1,193},{2,50},{3,195},{4,52},{5,197},{6,54},{7,199},{8,56}... | collective-permute-start | bytes 172040 | tf_op jit(solution)/shard_map/ppermute | solution.py:80
  140.2 6.0 %collective-permute-start.24 = (bf16[448,128]{1,0:T(8,128)(2,1)S(1)}, bf16[448,128]{1,0:T(8,128)(2,1)S(1)}, u32[]{:S(2)}, u32[]{:S(2)}) collective-permute-start(bf16[448,128]{1,0:T(8,128)(2,1)S(1)} %shard_map.118.mine), channel_id=1, source_target_pairs={{0,1},{1,0},{2,3},{3,2},{4,5},{5,4},{6,7},{7,6},{8,9},{9,8},{10,11... | collective-permute-start | bytes 344072 | tf_op jit(solution)/shard_map/ppermute | solution.py:505
  (5 other events, 35.8 us)

commit v3 on v2

--- a/solution.py
+++ b/solution.py
@@ -1,3 +1,4 @@
+import functools
 import math
 
 import jax
@@ -162,33 +163,30 @@
         out[pl.ds(MESH, META), :] = ends[...]
 
 
+def cot_table(cot, w, gs):
+    gs[...] = nt(cot[...], w[6]) * 0.5
+
+
 def own_tables(lat, w, snd, rcv):
     rows = lat[pl.ds(0, MESH), :]
     snd[...] = (nn(rows, w[4]) * 0.5).astype(BF16)
     rcv[...] = nn(rows, w[5]) * 0.5
 
 
-def cot_tables(cot, cp, cn, w, gs):
-    for j, c in enumerate((cp, cot, cn)):
-        gs[pl.ds(j * MESH, MESH), :] = nt(c[...], w[6]) * 0.5
-
-
-def edges_backward(
-    lp, ln, snd, rcv, col, row, gs, cot, slope2, w,
-    summed_b, gsend_b, grecv_b, gl_b, gsec_b, ga_b, gm_b, gl_out, gm_own,
-    table, srcv, ecol, e, gsend,
-):
+HALF = 128
+
+
+def own_edges(lp, ln, snd, rcv, col, row, gs, w, summed_b, grecv_b, gsend, srcv, table, e):
     table[pl.ds(MESH, MESH), :] = snd[...]
     for j, c in enumerate((lp, ln)):
         rows = c[pl.ds(0, MESH), :]
         table[pl.ds(2 * j * MESH, MESH), :] = (nn(rows, w[4]) * 0.5).astype(BF16)
         srcv[pl.ds(j * MESH, MESH), :] = nn(rows, w[5]) * 0.5
-    half = 128
-    lane = lax.broadcasted_iota(I32, (half, 3 * MESH), 1).astype(F32)
+    lane = lax.broadcasted_iota(I32, (HALF, 3 * MESH), 1).astype(F32)
     for m in range(2):
-        rows = pl.ds(m * half, half)
-        total = jnp.zeros((half, LAT), F32)
-        recv = jnp.zeros((half, LAT), F32)
+        rows = pl.ds(m * HALF, HALF)
+        total = jnp.zeros((HALF, LAT), F32)
+        recv = jnp.zeros((HALF, LAT), F32)
         for k in range(K):
             pick = jnp.where(lane == col[rows, k : k + 1], 1.0, 0.0).astype(BF16)
             h = nn(pick, table[...]) + rcv[rows, :]
@@ -196,9 +194,9 @@
             u = 1.0 + t
             s = h * u
             total = total + s
-            eg = (gs[pl.ds(MESH + m * half, half), :] * (u + s * (1.0 - t))).astype(BF16)
+            eg = (gs[rows, :] * (u + s * (1.0 - t))).astype(BF16)
             recv = recv + eg.astype(F32)
-            e[pl.ds(k * MESH + m * half, half), :] = eg
+            e[pl.ds(k * MESH + m * HALF, HALF), :] = eg
         summed_b[rows, :] = total.astype(BF16)
         grecv_b[rows, :] = recv.astype(BF16)
     own = lax.broadcasted_iota(I32, (MESH, MESH), 0).astype(F32)
@@ -207,25 +205,36 @@
         pick = jnp.where(own + float(MESH) == row[k : k + 1, :], 1.0, 0.0).astype(BF16)
         acc = acc + nn(pick, e[pl.ds(k * MESH, MESH), :])
     gsend[...] = acc
-    lane2 = lax.broadcasted_iota(I32, (half, MESH), 1).astype(F32)
-    for side, c in enumerate((lp, ln)):
+
+
+def halo_edges(
+    lp, ln, cp, cn, snd, srcv, gsend, grecv_b, cot, slope2, w,
+    gsend_b, gl_b, gsec_b, ga_b, gm_b, gl_out, gm_own,
+    ecol, e, gs, total,
+):
+    own = lax.broadcasted_iota(I32, (MESH, MESH), 0).astype(F32)
+    lane = lax.broadcasted_iota(I32, (HALF, MESH), 1).astype(F32)
+    total[...] = gsend[...]
+    for side, (c, far) in enumerate(((lp, cp), (ln, cn))):
+        gs[...] = nt(far[...], w[6]) * 0.5
         codes = c[pl.ds(MESH, META), 0:MESH].astype(F32)
         ecol[...] = jnp.transpose(codes)
         for k in range(K):
             for m in range(2):
-                rows = pl.ds(m * half, half)
-                pick = jnp.where(lane2 == ecol[rows, k : k + 1], 1.0, 0.0).astype(BF16)
-                h = nn(pick, table[pl.ds(MESH, MESH), :]) + srcv[pl.ds(side * MESH + m * half, half), :]
+                rows = pl.ds(m * HALF, HALF)
+                pick = jnp.where(lane == ecol[rows, k : k + 1], 1.0, 0.0).astype(BF16)
+                h = nn(pick, snd[...]) + srcv[pl.ds(side * MESH + m * HALF, HALF), :]
                 t = jnp.tanh(h)
                 u = 1.0 + t
-                g = gs[pl.ds(2 * side * MESH + m * half, half), :]
-                e[pl.ds(k * MESH + m * half, half), :] = (g * (u + h * u * (1.0 - t))).astype(BF16)
-        acc = gsend[...]
+                e[pl.ds(k * MESH + m * HALF, HALF), :] = (
+                    gs[rows, :] * (u + h * u * (1.0 - t))
+                ).astype(BF16)
+        acc = total[...]
         for k in range(K):
             pick = jnp.where(own == codes[k : k + 1, :], 1.0, 0.0).astype(BF16)
             acc = acc + nn(pick, e[pl.ds(k * MESH, MESH), :])
-        gsend[...] = acc
-    gsend_b[...] = gsend[...].astype(BF16)
+        total[...] = acc
+    gsend_b[...] = total[...].astype(BF16)
     gl = cot[...].astype(F32) + nt(gsend_b[...], w[4]) + nt(grecv_b[...], w[5])
     gl_b[...] = gl.astype(BF16)
     gl_out[...] = gl_b[...]
@@ -239,20 +248,20 @@
 BROWS = 224
 
 
-def mesh_weights(pos, ah, agg, sq, lat, summed, ga, gsec, gl, gsend, grecv, cot, keep, give):
+def mesh_weights(pos, ah, agg, sq, lat, summed, ga, gsec, gl, gsend, grecv, cot, out, *, other):
     rep = place(pos)[2]
+    h = 1 - rep if other else rep
     pairs = ((ah, ga), (agg, gsec), (sq, gl), (lat, gsend), (lat, grecv), (summed, cot))
-    for out, h in ((give, 1 - rep), (keep, rep)):
-        cols = pl.ds(pl.multiple_of(h * 256, 256), 256)
-        for w, (left, right) in enumerate(pairs):
-            part = tn(left[pl.ds(0, MESH), :], right[:, cols]).astype(BF16)
-            for c in range(2):
-                for b in range(16):
-                    if w < 2:
-                        at = NZ * ZROWS + b * 128 + w * 64 + c * 32
-                    else:
-                        at = (c * 4 + w - 2) * ZROWS + b * 32
-                    out[pl.ds(at, 32), :] = part[b * 32 : b * 32 + 32, c * 128 : c * 128 + 128]
+    cols = pl.ds(pl.multiple_of(h * 256, 256), 256)
+    for w, (left, right) in enumerate(pairs):
+        part = tn(left[pl.ds(0, MESH), :], right[:, cols]).astype(BF16)
+        for c in range(2):
+            for b in range(16):
+                if w < 2:
+                    at = NZ * ZROWS + b * 128 + w * 64 + c * 32
+                else:
+                    at = (c * 4 + w - 2) * ZROWS + b * 32
+                out[pl.ds(at, 32), :] = part[b * 32 : b * 32 + 32, c * 128 : c * 128 + 128]
 
 
 def pair_sum(a, b, out, moved):
@@ -382,8 +391,6 @@
     down = [((i + 1) % ring, i) for i in range(ring)]
     tie = lax.optimization_barrier
 
-    cp = lax.ppermute(cot, ("band", "patch"), up)
-    cn = lax.ppermute(cot, ("band", "patch"), down)
     p0, slope1 = call(
         grid_forward,
         [(tb, 1), (tk, 1), (x, 0), (weights, 2), (slot, 0)],
@@ -405,12 +412,8 @@
     mesh_bf = ((MESH, LAT), BF16, 0)
     mesh_f = ((MESH, LAT), F32, 0)
     pay = ((MESH + META, LAT), BF16, 0)
-    gs = call(
-        cot_tables,
-        [(cot, 0), (cp, 0), (cn, 0), (weights, 0)],
-        [((3 * MESH, LAT), F32, 0)],
-        flops=6 * 256 * 512 * 512,
-    )[0]
+    near_cot, _ = tie((cot, p0))
+    gs = call(cot_table, [(near_cot, 0), (weights, 0)], [mesh_f], flops=2 * 256 * 512 * 512)[0]
     p[1], gs, row, col = tie((p[1], gs, row, col))
     q0, q1, q2, q3, table = call(
         route_sum,
@@ -428,35 +431,48 @@
     )
     lp = lax.ppermute(lat_up, ("band", "patch"), up)
     ln = lax.ppermute(lat_down, ("band", "patch"), down)
+    far, lat_down = tie((cot, lat_down))
+    cp = lax.ppermute(far, ("band", "patch"), up)
+    cn = lax.ppermute(far, ("band", "patch"), down)
     snd, rcv = call(
         own_tables,
         [(lat_up, 0), (weights, 0)],
         [mesh_bf, mesh_f],
-        flops=4 * 256 * 512 * 512
-    )
-    summed, gsend, grecv, gl, gsec, ga, gm, gl_out, gm_own = call(
-        edges_backward,
-        [(v, 0) for v in (lp, ln, snd, rcv, col, row, gs, cot, slope2)] + [(weights, 0)],
-        [mesh_bf] * 9,
+        flops=4 * 256 * 512 * 512,
+    )
+    summed, grecv, gsend_own, srcv = call(
+        own_edges,
+        [(v, 0) for v in (lp, ln, snd, rcv, col, row, gs, weights)],
+        [mesh_bf, mesh_bf, mesh_f, ((2 * MESH, LAT), F32, 0)],
+        scratch=[pltpu.VMEM((3 * MESH, LAT), BF16), pltpu.VMEM((K * MESH, LAT), BF16)],
+        flops=2 * 10**9,
+        limit=12,
+    )
+    gsend, gl, gsec, ga, gm, gl_out, gm_own = call(
+        halo_edges,
+        [(v, 0) for v in (lp, ln, cp, cn, snd, srcv, gsend_own, grecv, cot, slope2, weights)],
+        [mesh_bf] * 7,
         scratch=[
-            pltpu.VMEM((3 * MESH, LAT), BF16),
-            pltpu.VMEM((2 * MESH, LAT), F32),
             pltpu.VMEM((MESH, META), F32),
             pltpu.VMEM((K * MESH, LAT), BF16),
             pltpu.VMEM((MESH, LAT), F32),
+            pltpu.VMEM((MESH, LAT), F32),
         ],
-        flops=5 * 10**9,
-        limit=16,
+        flops=3 * 10**9,
+        limit=12,
     )
     g = [gm_own] + [second(gm, k) for k in (1, 2, 3)]
 
 
-    keep, give = call(
-        mesh_weights,
-        [(pos, 1)]
-        + [(v, 0) for v in (ah, agg, sq, lat_up, summed, ga, gsec, gl, gsend, grecv, cot)],
-        [((6144, 128), BF16, 0)] * 2,
-        flops=12 * 256 * 512 * 512,
+    give, keep = (
+        call(
+            functools.partial(mesh_weights, other=other),
+            [(pos, 1)]
+            + [(v, 0) for v in (ah, agg, sq, lat_up, summed, ga, gsec, gl, gsend, grecv, cot)],
+            [((6144, 128), BF16, 0)],
+            flops=6 * 256 * 512 * 512,
+        )[0]
+        for other in (True, False)
     )
     swap = [(0, 1), (1, 0)]
     other = lax.ppermute(give, "rep", swap)

time: 147 us -> 146 us (level)
  waiting for transfers between devices: 61.2 us -> 54.9 us
  starting transfers between devices: 45.5 us -> 51 us
    ppermute x9, waiting for transfers between devices: 19.9 us -> 29.9 us  [first(): return lax.ppermute(v, ALL, shifts(k, False))]
    ppermute x2, waiting for transfers between devices: 11.1 us -> 3.79 us  [the longest x1 3.78 us: body(): cp = lax.ppermute(far, ('band', 'patch'), up)]
    ppermute x1, waiting for transfers between devices: 7.34 us -> 3.48 us  [body(): lp = lax.ppermute(lat_up, ('band', 'patch'), up)]
    ppermute x1, starting transfers between devices: 4.78 us -> 8.58 us  [body(): ln = lax.ppermute(lat_down, ('band', 'patch'), down)]
    ppermute x1, waiting for transfers between devices: 3.05 us -> 0.01 us  [body(): ln = lax.ppermute(lat_down, ('band', 'patch'), down)]
    ppermute x9, starting transfers between devices: 6.97 us -> 8.8 us  [second(): return lax.ppermute(v, ALL, shifts(k, True))]
    ppermute x9, waiting for transfers between devices: 11.5 us -> 10 us  [second(): return lax.ppermute(v, ALL, shifts(k, True))]
    pallas_call x17 -> x19, Pallas kernels: 22.4 us -> 22.7 us  [call(): pl.pallas_call(kernel, out_shape=out_shape, in_specs=specs_in, out_specs=...]
  transfers between devices with their start and end apart: 26 -> 26, of which waited for: 16 -> 16; matrix products, arithmetic and copies ran while one was open for 0% -> 0% of each run, Pallas kernels for 5% -> 7%
where the time goes in v3:
time: 146 us
  waiting for transfers between devices  54.9 us (38%)
  starting transfers between devices  51 us (35%)
  Pallas kernels  22.7 us (16%)
  blocking collectives  14.5 us (10%)
  local copies, waits for them, and re-layouts  2.08 us (1%)
    ppermute x9, waiting for transfers between devices, first(): return lax.ppermute(v, ALL, shifts(k, False))  29.9 us
    pallas_call x19, Pallas kernels, call(): pl.pallas_call(kernel, out_shape=out_shape, in_specs=specs_in, out_specs=...  22.7 us
    all_to_all x1, blocking collectives, body(): lax.all_to_all(spread, 'patch', split_axis=0, concat_axis=0, tiled=True)  14.5 us
    ppermute x9, starting transfers between devices, first(): return lax.ppermute(v, ALL, shifts(k, False))  10.9 us
    ppermute x9, waiting for transfers between devices, second(): return lax.ppermute(v, ALL, shifts(k, True))  10 us
    ppermute x9, starting transfers between devices, second(): return lax.ppermute(v, ALL, shifts(k, True))  8.8 us
    ppermute x1, starting transfers between devices, body(): ln = lax.ppermute(lat_down, ('band', 'patch'), down)  8.58 us
    ppermute x1, starting transfers between devices, body(): cn = lax.ppermute(far, ('band', 'patch'), down)  6.89 us
  transfers between devices with their start and end apart: 26, of which 16 were waited for; matrix products, arithmetic and copies ran while one was open for 0% of the time, Pallas kernels for 7%

profile of v3, /device:TPU:1, one launch (start us, length us, event | category | flops | bytes accessed | tf_op | source)
XLA Modules:
  0.0 146.1 jit_solution(5246230430991782203)
XLA Ops:
  0.7 3.4 %shard_map.103 = (bf16[528,512]{1,0:T(8,128)(2,1)}, bf16[512,512]{1,0:T(8,128)(2,1)}) custom-call(s32[4]{0:T(128)} %bitcast.22, s32[4]{0:T(128)} %tk.1, bf16[512,512]{1,0:T(8,128)(2,1)} %bitcast.16, bf16[7,512,512]{2,1,0:T(8,128)(2,1)} %w.13, s32[4,128]{1,0:T(4,128)} %bitcast.19), custom_call_target="tpu_custom_call" | custom-call | flops 268435456 | bytes 1000000 | tf_op jit(solution)/shard_map/pallas_call | solution.py:48
  4.1 2.1 %collective-permute-start = (bf16[528,512]{1,0:T(8,128)(2,1)}, bf16[528,512]{1,0:T(8,128)(2,1)S(1)}, u32[]{:S(2)}, u32[]{:S(2)}) collective-permute-start(bf16[528,512]{1,0:T(8,128)(2,1)} %get-tuple-element.59.p0), channel_id=1, source_target_pairs={{0,64},{1,17},{2,66},{3,19},{4,68},{5,21},{6,70},{7,23},{8,72},{9,... | collective-permute-start | bytes 1622024 | tf_op jit(solution)/shard_map/ppermute | solution.py:77
  6.2 1.4 collective-permute-start.2
  7.6 1.6 %collective-permute-start.1 = (bf16[528,512]{1,0:T(8,128)(2,1)}, bf16[528,512]{1,0:T(8,128)(2,1)S(1)}, u32[]{:S(2)}, u32[]{:S(2)}) collective-permute-start(bf16[528,512]{1,0:T(8,128)(2,1)} %get-tuple-element.59.p0), channel_id=1, source_target_pairs={{0,128},{1,33},{2,130},{3,35},{4,132},{5,37},{6,134},{7,39},{8,136... | collective-permute-start | bytes 1622024 | tf_op jit(solution)/shard_map/ppermute | solution.py:77
  9.4 2.0 %copy-done = bf16[7,512,512]{2,1,0:T(8,128)(2,1)S(1)} copy-done((bf16[7,512,512]{2,1,0:T(8,128)(2,1)S(1)}, bf16[7,512,512]{2,1,0:T(8,128)(2,1)}, u32[]{:S(2)}) %copy-start) | copy-done | bytes 3670040
  11.8 3.1 %collective-permute-done.p1 = bf16[528,512]{1,0:T(8,128)(2,1)S(1)} collective-permute-done((bf16[528,512]{1,0:T(8,128)(2,1)}, bf16[528,512]{1,0:T(8,128)(2,1)S(1)}, u32[]{:S(2)}, u32[]{:S(2)}) %collective-permute-start) | collective-permute-done | bytes 540704 | tf_op jit(solution)/shard_map/ppermute | solution.py:77
  14.9 6.9 %collective-permute-done.1.p2 = bf16[528,512]{1,0:T(8,128)(2,1)S(1)} collective-permute-done((bf16[528,512]{1,0:T(8,128)(2,1)}, bf16[528,512]{1,0:T(8,128)(2,1)S(1)}, u32[]{:S(2)}, u32[]{:S(2)}) %collective-permute-start.1) | collective-permute-done | bytes 540704 | tf_op jit(solution)/shard_map/ppermute | solution.py:77
  23.8 2.7 %collective-permute-start.4 = (bf16[256,512]{1,0:T(8,128)(2,1)S(1)}, bf16[256,512]{1,0:T(8,128)(2,1)S(1)}, u32[]{:S(2)}, u32[]{:S(2)}) collective-permute-start(bf16[256,512]{1,0:T(8,128)(2,1)S(1)} %get-tuple-element.68), channel_id=1, source_target_pairs={{0,32},{1,129},{2,34},{3,131},{4,36},{5,133},{6,38},{7,135},{8,40}... | collective-permute-start | bytes 786440 | tf_op jit(solution)/shard_map/ppermute | solution.py:81
  27.4 2.2 %collective-permute-done.3.r1 = bf16[256,512]{1,0:T(8,128)(2,1)S(1)} collective-permute-done((bf16[256,512]{1,0:T(8,128)(2,1)S(1)}, bf16[256,512]{1,0:T(8,128)(2,1)S(1)}, u32[]{:S(2)}, u32[]{:S(2)}) %collective-permute-start.3) | collective-permute-done | bytes 262176 | tf_op jit(solution)/shard_map/ppermute | solution.py:81
  29.7 3.8 %collective-permute-done.4.r2 = bf16[256,512]{1,0:T(8,128)(2,1)S(1)} collective-permute-done((bf16[256,512]{1,0:T(8,128)(2,1)S(1)}, bf16[256,512]{1,0:T(8,128)(2,1)S(1)}, u32[]{:S(2)}, u32[]{:S(2)}) %collective-permute-start.4) | collective-permute-done | bytes 262176 | tf_op jit(solution)/shard_map/ppermute | solution.py:81
  34.3 8.6 %collective-permute-start.7 = (bf16[272,512]{1,0:T(8,128)(2,1)S(1)}, bf16[272,512]{1,0:T(8,128)(2,1)S(1)}, u32[]{:S(2)}, u32[]{:S(2)}) collective-permute-start(bf16[272,512]{1,0:T(8,128)(2,1)S(1)} %get-tuple-element.73), channel_id=1, source_target_pairs={{2,0},{4,2},{6,4},{8,6},{10,8},{12,10},{14,12},{16,14},{18,16},{20... | collective-permute-start | bytes 835592 | tf_op jit(solution)/shard_map/ppermute | solution.py:433
  42.9 6.9 %collective-permute-start.9 = (bf16[256,512]{1,0:T(8,128)(2,1)S(1)}, bf16[256,512]{1,0:T(8,128)(2,1)S(1)}, u32[]{:S(2)}, u32[]{:S(2)}) collective-permute-start(bf16[256,512]{1,0:T(8,128)(2,1)S(1)} %bitcast.11), channel_id=1, source_target_pairs={{2,0},{4,2},{6,4},{8,6},{10,8},{12,10},{14,12},{16,14},{18,16},{20... | collective-permute-start | bytes 786440 | tf_op jit(solution)/shard_map/ppermute | solution.py:436
  50.2 3.5 %collective-permute-done.6.lp = bf16[272,512]{1,0:T(8,128)(2,1)S(1)} collective-permute-done((bf16[272,512]{1,0:T(8,128)(2,1)S(1)}, bf16[272,512]{1,0:T(8,128)(2,1)S(1)}, u32[]{:S(2)}, u32[]{:S(2)}) %collective-permute-start.6) | collective-permute-done | bytes 278560 | tf_op jit(solution)/shard_map/ppermute | solution.py:432
  53.7 2.9 %shard_map.109 = (bf16[256,512]{1,0:T(8,128)(2,1)S(1)}, bf16[256,512]{1,0:T(8,128)(2,1)S(1)}, f32[256,512]{1,0:T(8,128)S(1)}, f32[512,512]{1,0:T(8,128)S(1)}) custom-call(bf16[272,512]{1,0:T(8,128)(2,1)S(1)} %collective-permute-done.6.lp, bf16[272,512]{1,0:T(8,128)(2,1)S(1)} %collective-permute-done.7.ln, bf16[256,512]{1,0:T(8,128)(2,1)S(1)} %get-tuple-element.75.snd, ...), custom_call_target="tpu_custom_call" | custom-call | flops 2000000000 | bytes 1000000 | tf_op jit(solution)/shard_map/pallas_call | solution.py:48
  56.6 3.8 %collective-permute-done.8.cp = bf16[256,512]{1,0:T(8,128)(2,1)S(1)} collective-permute-done((bf16[256,512]{1,0:T(8,128)(2,1)S(1)}, bf16[256,512]{1,0:T(8,128)(2,1)S(1)}, u32[]{:S(2)}, u32[]{:S(2)}) %collective-permute-start.8) | collective-permute-done | bytes 262176 | tf_op jit(solution)/shard_map/ppermute | solution.py:435
  60.4 5.6 %shard_map.110 = (bf16[256,512]{1,0:T(8,128)(2,1)S(1)}, bf16[256,512]{1,0:T(8,128)(2,1)S(1)}, bf16[256,512]{1,0:T(8,128)(2,1)S(1)}, bf16[256,512]{1,0:T(8,128)(2...) custom-call(bf16[272,512]{1,0:T(8,128)(2,1)S(1)} %collective-permute-done.6.lp, ...), custom_call_target="tpu_custom_call" | custom-call | flops 3000000000 | bytes 1000000 | tf_op jit(solution)/shard_map/pallas_call | solution.py:48
  66.6 5.0 %collective-permute-start.17 = (bf16[6144,128]{1,0:T(8,128)(2,1)S(1)}, bf16[6144,128]{1,0:T(8,128)(2,1)S(1)}, u32[]{:S(2)}, u32[]{:S(2)}) collective-permute-start(bf16[6144,128]{1,0:T(8,128)(2,1)S(1)} %shard_map.115), channel_id=1, source_target_pairs={{0,1},{1,0},{2,3},{3,2},{4,5},{5,4},{6,7},{7,6},{8,9},{9,8},{10,11... | collective-permute-start | bytes 4718600 | tf_op jit(solution)/shard_map/ppermute | solution.py:478
  71.6 1.5 %collective-permute-start.10 = (bf16[256,512]{1,0:T(8,128)(2,1)S(1)}, bf16[256,512]{1,0:T(8,128)(2,1)S(1)}, u32[]{:S(2)}, u32[]{:S(2)}) collective-permute-start(bf16[256,512]{1,0:T(8,128)(2,1)S(1)} %get-tuple-element.85), channel_id=1, source_target_pairs={{0,16},{1,65},{2,18},{3,67},{4,20},{5,69},{6,22},{7,71},{8,24},{9,... | collective-permute-start | bytes 786440 | tf_op jit(solution)/shard_map/ppermute | solution.py:81
  74.7 1.9 %shard_map.116 = (bf16[4096,128]{1,0:T(8,128)(2,1)}, bf16[2048,128]{1,0:T(8,128)(2,1)S(1)}) custom-call(bf16[6144,128]{1,0:T(8,128)(2,1)S(1)} %shard_map.114.a, bf16[6144,128]{1,0:T(8,128)(2,1)S(1)} %collective-permute-done.17.b), custom_call_target="tpu_custom_call" | custom-call | flops 1000000 | bytes 1000000 | tf_op jit(solution)/shard_map/pallas_call | solution.py:48
  76.6 3.6 %all-to-all-start = ((bf16[8,512,128]{2,1,0:T(8,128)(2,1)}), bf16[8,512,128]{2,1,0:T(8,128)(2,1)S(1)}, u32[]{:S(2)}, u32[]{:S(2)}) async-start(bf16[8,512,128]{2,1,0:T(8,128)(2,1)} %bitcast.9), calls=%async_computation | async-start | bytes 2097152 | tf_op jit(solution)/shard_map/all_to_all | solution.py:492
  80.2 1.3 collective-permute-done.10.g1
  82.9 2.6 %collective-permute-start.15 = (bf16[512,512]{1,0:T(8,128)(2,1)S(1)}, bf16[512,512]{1,0:T(8,128)(2,1)S(1)}, u32[]{:S(2)}, u32[]{:S(2)}) collective-permute-start(bf16[512,512]{1,0:T(8,128)(2,1)S(1)} %get-tuple-element.89), channel_id=1, source_target_pairs={{0,192},{1,49},{2,194},{3,51},{4,196},{5,53},{6,198},{7,55},{8,200... | collective-permute-start | bytes 1572872 | tf_op jit(solution)/shard_map/ppermute | solution.py:77
  85.5 12.5 %collective-permute-done.13.r1 = bf16[512,512]{1,0:T(8,128)(2,1)S(1)} collective-permute-done((bf16[512,512]{1,0:T(8,128)(2,1)S(1)}, bf16[512,512]{1,0:T(8,128)(2,1)S(1)}, u32[]{:S(2)}, u32[]{:S(2)}) %collective-permute-start.13) | collective-permute-done | bytes 524320 | tf_op jit(solution)/shard_map/ppermute | solution.py:77
  98.6 1.4 shard_map.112
  100.0 2.3 %collective-permute-start.16 = (bf16[16,64,128]{2,1,0:T(8,128)(2,1)S(1)}, bf16[16,64,128]{2,1,0:T(8,128)(2,1)S(1)}, u32[]{:S(2)}, u32[]{:S(2)}) collective-permute-start(bf16[16,64,128]{2,1,0:T(8,128)(2,1)S(1)} %get-tuple-element.96), channel_id=1, source_target_pairs={{0,1},{1,0},{2,3},{3,2},{4,5},{5,4},{6,7},{7,6},{8,9},{9,8},{10,11... | collective-permute-start | bytes 786440 | tf_op jit(solution)/shard_map/ppermute | solution.py:501
  103.6 5.8 %all-to-all-done.zparts = bf16[8,512,128]{2,1,0:T(8,128)(2,1)S(1)} async-done(((bf16[8,512,128]{2,1,0:T(8,128)(2,1)}), bf16[8,512,128]{2,1,0:T(8,128)(2,1)S(1)}, u32[]{:S(2)}, u32[]{:S(2)}) %all-to-all-start) | async-done | bytes 1048608 | tf_op jit(solution)/shard_map/all_to_all | solution.py:492
  109.7 2.6 %collective-permute-start.20 = (bf16[896,128]{1,0:T(8,128)(2,1)S(1)}, bf16[896,128]{1,0:T(8,128)(2,1)S(1)}, u32[]{:S(2)}, u32[]{:S(2)}) collective-permute-start(bf16[896,128]{1,0:T(8,128)(2,1)S(1)} %get-tuple-element.110), channel_id=1, source_target_pairs={{0,192},{1,49},{2,194},{3,51},{4,196},{5,53},{6,198},{7,55},{8,200... | collective-permute-start | bytes 688136 | tf_op jit(solution)/shard_map/ppermute | solution.py:77
  112.3 6.2 %collective-permute-done.18.b = bf16[896,128]{1,0:T(8,128)(2,1)S(1)} collective-permute-done((bf16[896,128]{1,0:T(8,128)(2,1)S(1)}, bf16[896,128]{1,0:T(8,128)(2,1)S(1)}, u32[]{:S(2)}, u32[]{:S(2)}) %collective-permute-start.18) | collective-permute-done | bytes 229408 | tf_op jit(solution)/shard_map/ppermute | solution.py:77
  119.4 2.6 %collective-permute-start.23 = (bf16[224,128]{1,0:T(8,128)(2,1)S(1)}, bf16[224,128]{1,0:T(8,128)(2,1)S(1)}, u32[]{:S(2)}, u32[]{:S(2)}) collective-permute-start(bf16[224,128]{1,0:T(8,128)(2,1)S(1)} %get-tuple-element.114), channel_id=1, source_target_pairs={{0,48},{1,193},{2,50},{3,195},{4,52},{5,197},{6,54},{7,199},{8,56}... | collective-permute-start | bytes 172040 | tf_op jit(solution)/shard_map/ppermute | solution.py:81
  122.0 2.2 %collective-permute-done.21.b = bf16[224,128]{1,0:T(8,128)(2,1)S(1)} collective-permute-done((bf16[224,128]{1,0:T(8,128)(2,1)S(1)}, bf16[224,128]{1,0:T(8,128)(2,1)S(1)}, u32[]{:S(2)}, u32[]{:S(2)}) %collective-permute-start.21) | collective-permute-done | bytes 57376 | tf_op jit(solution)/shard_map/ppermute | solution.py:81
  124.8 14.5 %all_to_all.14.parts = bf16[8,224,128]{2,1,0:T(8,128)(2,1)S(1)} all-to-all(bf16[8,224,128]{2,1,0:T(8,128)(2,1)S(1)} %shard_map.119), channel_id=1, replica_groups=mesh['band'=16,'patch'=8,'rep'=2] {'patch'}, dimensions={0} | all-to-all | bytes 917504 | tf_op jit(solution)/shard_map/all_to_all | solution.py:519
  139.3 5.0 %collective-permute-start.24 = (bf16[448,128]{1,0:T(8,128)(2,1)S(1)}, bf16[448,128]{1,0:T(8,128)(2,1)S(1)}, u32[]{:S(2)}, u32[]{:S(2)}) collective-permute-start(bf16[448,128]{1,0:T(8,128)(2,1)S(1)} %shard_map.120.mine), channel_id=1, source_target_pairs={{0,1},{1,0},{2,3},{3,2},{4,5},{5,4},{6,7},{7,6},{8,9},{9,8},{10,11... | collective-permute-start | bytes 344072 | tf_op jit(solution)/shard_map/ppermute | solution.py:521
  (62 shorter events, 13.9 us)
Async XLA Ops:
  4.1 10.8 %collective-permute-start = (bf16[528,512]{1,0:T(8,128)(2,1)}, bf16[528,512]{1,0:T(8,128)(2,1)S(1)}, u32[]{:S(2)}, u32[]{:S(2)}) collective-permute-start(bf16[528,512]{1,0:T(8,128)(2,1)} %get-tuple-element.59.p0), channel_id=1, source_target_pairs={{0,64},{1,17},{2,66},{3,19},{4,68},{5,21},{6,70},{7,23},{8,72},{9,... | collective-permute-start | bytes 1622024 | tf_op jit(solution)/shard_map/ppermute | solution.py:77
  6.2 8.7 %collective-permute-start.2 = (bf16[528,512]{1,0:T(8,128)(2,1)}, bf16[528,512]{1,0:T(8,128)(2,1)S(1)}, u32[]{:S(2)}, u32[]{:S(2)}) collective-permute-start(bf16[528,512]{1,0:T(8,128)(2,1)} %get-tuple-element.59.p0), channel_id=1, source_target_pairs={{0,192},{1,49},{2,194},{3,51},{4,196},{5,53},{6,198},{7,55},{8,200... | collective-permute-start | bytes 1622024 | tf_op jit(solution)/shard_map/ppermute | solution.py:77
  7.6 14.2 %collective-permute-start.1 = (bf16[528,512]{1,0:T(8,128)(2,1)}, bf16[528,512]{1,0:T(8,128)(2,1)S(1)}, u32[]{:S(2)}, u32[]{:S(2)}) collective-permute-start(bf16[528,512]{1,0:T(8,128)(2,1)} %get-tuple-element.59.p0), channel_id=1, source_target_pairs={{0,128},{1,33},{2,130},{3,35},{4,132},{5,37},{6,134},{7,39},{8,136... | collective-permute-start | bytes 1622024 | tf_op jit(solution)/shard_map/ppermute | solution.py:77
  11.5 22.0 %copy-start.1 = (bf16[7,512,512]{2,1,0:T(8,128)(2,1)S(1)}, bf16[7,512,512]{2,1,0:T(8,128)(2,1)}, u32[]{:S(2)}) copy-start(bf16[7,512,512]{2,1,0:T(8,128)(2,1)} %w.13) | copy-start | bytes 11010052
  11.8 21.6 %copy-start.7 = (bf16[1,256,512]{2,1,0:T(8,128)(2,1)S(1)}, bf16[1,256,512]{2,1,0:T(8,128)(2,1)}, u32[]{:S(2)}) copy-start(bf16[1,256,512]{2,1,0:T(8,128)(2,1)} %param.9) | copy-start | bytes 786436
  22.9 6.8 %collective-permute-start.3 = (bf16[256,512]{1,0:T(8,128)(2,1)S(1)}, bf16[256,512]{1,0:T(8,128)(2,1)S(1)}, u32[]{:S(2)}, u32[]{:S(2)}) collective-permute-start(bf16[256,512]{1,0:T(8,128)(2,1)S(1)} %get-tuple-element.67), channel_id=1, source_target_pairs={{0,16},{1,65},{2,18},{3,67},{4,20},{5,69},{6,22},{7,71},{8,24},{9,... | collective-permute-start | bytes 786440 | tf_op jit(solution)/shard_map/ppermute | solution.py:81
  23.8 9.6 %collective-permute-start.4 = (bf16[256,512]{1,0:T(8,128)(2,1)S(1)}, bf16[256,512]{1,0:T(8,128)(2,1)S(1)}, u32[]{:S(2)}, u32[]{:S(2)}) collective-permute-start(bf16[256,512]{1,0:T(8,128)(2,1)S(1)} %get-tuple-element.68), channel_id=1, source_target_pairs={{0,32},{1,129},{2,34},{3,131},{4,36},{5,133},{6,38},{7,135},{8,40}... | collective-permute-start | bytes 786440 | tf_op jit(solution)/shard_map/ppermute | solution.py:81
  26.6 6.9 %collective-permute-start.5 = (bf16[256,512]{1,0:T(8,128)(2,1)S(1)}, bf16[256,512]{1,0:T(8,128)(2,1)S(1)}, u32[]{:S(2)}, u32[]{:S(2)}) collective-permute-start(bf16[256,512]{1,0:T(8,128)(2,1)S(1)} %get-tuple-element.69), channel_id=1, source_target_pairs={{0,48},{1,193},{2,50},{3,195},{4,52},{5,197},{6,54},{7,199},{8,56}... | collective-permute-start | bytes 786440 | tf_op jit(solution)/shard_map/ppermute | solution.py:81
  34.3 15.9 %collective-permute-start.7 = (bf16[272,512]{1,0:T(8,128)(2,1)S(1)}, bf16[272,512]{1,0:T(8,128)(2,1)S(1)}, u32[]{:S(2)}, u32[]{:S(2)}) collective-permute-start(bf16[272,512]{1,0:T(8,128)(2,1)S(1)} %get-tuple-element.73), channel_id=1, source_target_pairs={{2,0},{4,2},{6,4},{8,6},{10,8},{12,10},{14,12},{16,14},{18,16},{20... | collective-permute-start | bytes 835592 | tf_op jit(solution)/shard_map/ppermute | solution.py:433
  42.9 10.8 %collective-permute-start.6 = (bf16[272,512]{1,0:T(8,128)(2,1)S(1)}, bf16[272,512]{1,0:T(8,128)(2,1)S(1)}, u32[]{:S(2)}, u32[]{:S(2)}) collective-permute-start(bf16[272,512]{1,0:T(8,128)(2,1)S(1)} %get-tuple-element.72.lat), channel_id=1, source_target_pairs={{0,2},{2,4},{4,6},{6,8},{8,10},{10,12},{12,14},{14,16},{16,18},{18... | collective-permute-start | bytes 835592 | tf_op jit(solution)/shard_map/ppermute | solution.py:432
  42.9 13.8 %collective-permute-start.9 = (bf16[256,512]{1,0:T(8,128)(2,1)S(1)}, bf16[256,512]{1,0:T(8,128)(2,1)S(1)}, u32[]{:S(2)}, u32[]{:S(2)}) collective-permute-start(bf16[256,512]{1,0:T(8,128)(2,1)S(1)} %bitcast.11), channel_id=1, source_target_pairs={{2,0},{4,2},{6,4},{8,6},{10,8},{12,10},{14,12},{16,14},{18,16},{20... | collective-permute-start | bytes 786440 | tf_op jit(solution)/shard_map/ppermute | solution.py:436
  49.8 10.7 %collective-permute-start.8 = (bf16[256,512]{1,0:T(8,128)(2,1)S(1)}, bf16[256,512]{1,0:T(8,128)(2,1)S(1)}, u32[]{:S(2)}, u32[]{:S(2)}) collective-permute-start(bf16[256,512]{1,0:T(8,128)(2,1)S(1)} %bitcast.12), channel_id=1, source_target_pairs={{0,2},{2,4},{4,6},{6,8},{8,10},{10,12},{12,14},{14,16},{16,18},{18... | collective-permute-start | bytes 786440 | tf_op jit(solution)/shard_map/ppermute | solution.py:435
  66.6 8.0 %collective-permute-start.17 = (bf16[6144,128]{1,0:T(8,128)(2,1)S(1)}, bf16[6144,128]{1,0:T(8,128)(2,1)S(1)}, u32[]{:S(2)}, u32[]{:S(2)}) collective-permute-start(bf16[6144,128]{1,0:T(8,128)(2,1)S(1)} %shard_map.115), channel_id=1, source_target_pairs={{0,1},{1,0},{2,3},{3,2},{4,5},{5,4},{6,7},{7,6},{8,9},{9,8},{10,11... | collective-permute-start | bytes 4718600 | tf_op jit(solution)/shard_map/ppermute | solution.py:478
  71.6 8.5 %collective-permute-start.12 = (bf16[256,512]{1,0:T(8,128)(2,1)S(1)}, bf16[256,512]{1,0:T(8,128)(2,1)S(1)}, u32[]{:S(2)}, u32[]{:S(2)}) collective-permute-start(bf16[256,512]{1,0:T(8,128)(2,1)S(1)} %get-tuple-element.85), channel_id=1, source_target_pairs={{0,48},{1,193},{2,50},{3,195},{4,52},{5,197},{6,54},{7,199},{8,56}... | collective-permute-start | bytes 786440 | tf_op jit(solution)/shard_map/ppermute | solution.py:81
  71.6 8.5 %collective-permute-start.11 = (bf16[256,512]{1,0:T(8,128)(2,1)S(1)}, bf16[256,512]{1,0:T(8,128)(2,1)S(1)}, u32[]{:S(2)}, u32[]{:S(2)}) collective-permute-start(bf16[256,512]{1,0:T(8,128)(2,1)S(1)} %get-tuple-element.85), channel_id=1, source_target_pairs={{0,32},{1,129},{2,34},{3,131},{4,36},{5,133},{6,38},{7,135},{8,40}... | collective-permute-start | bytes 786440 | tf_op jit(solution)/shard_map/ppermute | solution.py:81
  71.6 9.8 %collective-permute-start.10 = (bf16[256,512]{1,0:T(8,128)(2,1)S(1)}, bf16[256,512]{1,0:T(8,128)(2,1)S(1)}, u32[]{:S(2)}, u32[]{:S(2)}) collective-permute-start(bf16[256,512]{1,0:T(8,128)(2,1)S(1)} %get-tuple-element.85), channel_id=1, source_target_pairs={{0,16},{1,65},{2,18},{3,67},{4,20},{5,69},{6,22},{7,71},{8,24},{9,... | collective-permute-start | bytes 786440 | tf_op jit(solution)/shard_map/ppermute | solution.py:81
  76.6 32.8 %all-to-all-start = ((bf16[8,512,128]{2,1,0:T(8,128)(2,1)}), bf16[8,512,128]{2,1,0:T(8,128)(2,1)S(1)}, u32[]{:S(2)}, u32[]{:S(2)}) async-start(bf16[8,512,128]{2,1,0:T(8,128)(2,1)} %bitcast.9), calls=%async_computation | async-start | bytes 2097152 | tf_op jit(solution)/shard_map/all_to_all | solution.py:492
  81.5 17.1 %copy-start.6 = (bf16[512,512]{1,0:T(8,128)(2,1)S(1)}, bf16[512,512]{1,0:T(8,128)(2,1)}, u32[]{:S(2)}) copy-start(bf16[512,512]{1,0:T(8,128)(2,1)} %get-tuple-element.90.slope) | copy-start | bytes 1572868
  81.5 17.1 %copy-start.8 = (s32[512]{0:T(512)S(1)}, s32[512]{0:T(512)}, u32[]{:S(2)}) copy-start(s32[512]{0:T(512)} %param.13) | copy-start | bytes 6148
  81.5 17.1 %copy-start.10 = (s32[4,1]{0,1:T(1,128)S(1)}, s32[4,1]{0,1:T(1,128)}, u32[]{:S(2)}) copy-start(s32[4,1]{0,1:T(1,128)} %param.11) | copy-start | bytes 52
  81.5 20.8 %copy-start.2 = (bf16[7,512,512]{2,1,0:T(8,128)(2,1)S(1)}, bf16[7,512,512]{2,1,0:T(8,128)(2,1)}, u32[]{:S(2)}) copy-start(bf16[7,512,512]{2,1,0:T(8,128)(2,1)} %w.13) | copy-start | bytes 11010052
  82.5 15.5 %collective-permute-start.13 = (bf16[512,512]{1,0:T(8,128)(2,1)S(1)}, bf16[512,512]{1,0:T(8,128)(2,1)S(1)}, u32[]{:S(2)}, u32[]{:S(2)}) collective-permute-start(bf16[512,512]{1,0:T(8,128)(2,1)S(1)} %get-tuple-element.87), channel_id=1, source_target_pairs={{0,64},{1,17},{2,66},{3,19},{4,68},{5,21},{6,70},{7,23},{8,72},{9,... | collective-permute-start | bytes 1572872 | tf_op jit(solution)/shard_map/ppermute | solution.py:77
  82.8 15.1 %collective-permute-start.14 = (bf16[512,512]{1,0:T(8,128)(2,1)S(1)}, bf16[512,512]{1,0:T(8,128)(2,1)S(1)}, u32[]{:S(2)}, u32[]{:S(2)}) collective-permute-start(bf16[512,512]{1,0:T(8,128)(2,1)S(1)} %get-tuple-element.88), channel_id=1, source_target_pairs={{0,128},{1,33},{2,130},{3,35},{4,132},{5,37},{6,134},{7,39},{8,136... | collective-permute-start | bytes 1572872 | tf_op jit(solution)/shard_map/ppermute | solution.py:77
  82.9 15.7 %collective-permute-start.15 = (bf16[512,512]{1,0:T(8,128)(2,1)S(1)}, bf16[512,512]{1,0:T(8,128)(2,1)S(1)}, u32[]{:S(2)}, u32[]{:S(2)}) collective-permute-start(bf16[512,512]{1,0:T(8,128)(2,1)S(1)} %get-tuple-element.89), channel_id=1, source_target_pairs={{0,192},{1,49},{2,194},{3,51},{4,196},{5,53},{6,198},{7,55},{8,200... | collective-permute-start | bytes 1572872 | tf_op jit(solution)/shard_map/ppermute | solution.py:77
  100.0 3.5 %collective-permute-start.16 = (bf16[16,64,128]{2,1,0:T(8,128)(2,1)S(1)}, bf16[16,64,128]{2,1,0:T(8,128)(2,1)S(1)}, u32[]{:S(2)}, u32[]{:S(2)}) collective-permute-start(bf16[16,64,128]{2,1,0:T(8,128)(2,1)S(1)} %get-tuple-element.96), channel_id=1, source_target_pairs={{0,1},{1,0},{2,3},{3,2},{4,5},{5,4},{6,7},{7,6},{8,9},{9,8},{10,11... | collective-permute-start | bytes 786440 | tf_op jit(solution)/shard_map/ppermute | solution.py:501
  109.5 8.9 %collective-permute-start.18 = (bf16[896,128]{1,0:T(8,128)(2,1)S(1)}, bf16[896,128]{1,0:T(8,128)(2,1)S(1)}, u32[]{:S(2)}, u32[]{:S(2)}) collective-permute-start(bf16[896,128]{1,0:T(8,128)(2,1)S(1)} %get-tuple-element.108), channel_id=1, source_target_pairs={{0,64},{1,17},{2,66},{3,19},{4,68},{5,21},{6,70},{7,23},{8,72},{9,... | collective-permute-start | bytes 688136 | tf_op jit(solution)/shard_map/ppermute | solution.py:77
  109.6 8.8 %collective-permute-start.19 = (bf16[896,128]{1,0:T(8,128)(2,1)S(1)}, bf16[896,128]{1,0:T(8,128)(2,1)S(1)}, u32[]{:S(2)}, u32[]{:S(2)}) collective-permute-start(bf16[896,128]{1,0:T(8,128)(2,1)S(1)} %get-tuple-element.109), channel_id=1, source_target_pairs={{0,128},{1,33},{2,130},{3,35},{4,132},{5,37},{6,134},{7,39},{8,136... | collective-permute-start | bytes 688136 | tf_op jit(solution)/shard_map/ppermute | solution.py:77
  109.7 9.3 %collective-permute-start.20 = (bf16[896,128]{1,0:T(8,128)(2,1)S(1)}, bf16[896,128]{1,0:T(8,128)(2,1)S(1)}, u32[]{:S(2)}, u32[]{:S(2)}) collective-permute-start(bf16[896,128]{1,0:T(8,128)(2,1)S(1)} %get-tuple-element.110), channel_id=1, source_target_pairs={{0,192},{1,49},{2,194},{3,51},{4,196},{5,53},{6,198},{7,55},{8,200... | collective-permute-start | bytes 688136 | tf_op jit(solution)/shard_map/ppermute | solution.py:77
  119.2 4.9 %collective-permute-start.21 = (bf16[224,128]{1,0:T(8,128)(2,1)S(1)}, bf16[224,128]{1,0:T(8,128)(2,1)S(1)}, u32[]{:S(2)}, u32[]{:S(2)}) collective-permute-start(bf16[224,128]{1,0:T(8,128)(2,1)S(1)} %get-tuple-element.112), channel_id=1, source_target_pairs={{0,16},{1,65},{2,18},{3,67},{4,20},{5,69},{6,22},{7,71},{8,24},{9,... | collective-permute-start | bytes 172040 | tf_op jit(solution)/shard_map/ppermute | solution.py:81
  119.3 4.8 %collective-permute-start.22 = (bf16[224,128]{1,0:T(8,128)(2,1)S(1)}, bf16[224,128]{1,0:T(8,128)(2,1)S(1)}, u32[]{:S(2)}, u32[]{:S(2)}) collective-permute-start(bf16[224,128]{1,0:T(8,128)(2,1)S(1)} %get-tuple-element.113), channel_id=1, source_target_pairs={{0,32},{1,129},{2,34},{3,131},{4,36},{5,133},{6,38},{7,135},{8,40}... | collective-permute-start | bytes 172040 | tf_op jit(solution)/shard_map/ppermute | solution.py:81
  119.4 5.3 %collective-permute-start.23 = (bf16[224,128]{1,0:T(8,128)(2,1)S(1)}, bf16[224,128]{1,0:T(8,128)(2,1)S(1)}, u32[]{:S(2)}, u32[]{:S(2)}) collective-permute-start(bf16[224,128]{1,0:T(8,128)(2,1)S(1)} %get-tuple-element.114), channel_id=1, source_target_pairs={{0,48},{1,193},{2,50},{3,195},{4,52},{5,197},{6,54},{7,199},{8,56}... | collective-permute-start | bytes 172040 | tf_op jit(solution)/shard_map/ppermute | solution.py:81
  139.3 6.0 %collective-permute-start.24 = (bf16[448,128]{1,0:T(8,128)(2,1)S(1)}, bf16[448,128]{1,0:T(8,128)(2,1)S(1)}, u32[]{:S(2)}, u32[]{:S(2)}) collective-permute-start(bf16[448,128]{1,0:T(8,128)(2,1)S(1)} %shard_map.120.mine), channel_id=1, source_target_pairs={{0,1},{1,0},{2,3},{3,2},{4,5},{5,4},{6,7},{7,6},{8,9},{9,8},{10,11... | collective-permute-start | bytes 344072 | tf_op jit(solution)/shard_map/ppermute | solution.py:521
  (5 other events, 47.0 us)

commit v4 on v3

--- a/solution.py
+++ b/solution.py
@@ -267,11 +267,11 @@
 def pair_sum(a, b, out, moved):
     for dst, base in ((out, 0), (moved, NZ * ZROWS)):
 
-        @pl.loop(0, dst.shape[0], step=64)
+        @pl.loop(0, dst.shape[0], step=256)
         def _(at):
-            at = pl.multiple_of(at, 64)
-            rows = pl.ds(base + at, 64)
-            dst[pl.ds(at, 64), :] = (a[rows, :].astype(F32) + b[rows, :].astype(F32)).astype(BF16)
+            at = pl.multiple_of(at, 256)
+            rows = pl.ds(base + at, 256)
+            dst[pl.ds(at, 256), :] = (a[rows, :].astype(F32) + b[rows, :].astype(F32)).astype(BF16)
 
 
 def return_pick(pos, table, g0, g1, g2, g3, r0, r1, r2, r3):

time: 146 us -> 146 us (level)
  no operation moved by 1% of the time
where the time goes in v4:
time: 146 us
  waiting for transfers between devices  54.9 us (38%)
  starting transfers between devices  51 us (35%)
  Pallas kernels  22.4 us (15%)
  blocking collectives  14.5 us (10%)
  local copies, waits for them, and re-layouts  2.08 us (1%)
    ppermute x9, waiting for transfers between devices, first(): return lax.ppermute(v, ALL, shifts(k, False))  29.9 us
    pallas_call x19, Pallas kernels, call(): pl.pallas_call(kernel, out_shape=out_shape, in_specs=specs_in, out_specs=...  22.4 us
    all_to_all x1, blocking collectives, body(): lax.all_to_all(spread, 'patch', split_axis=0, concat_axis=0, tiled=True)  14.5 us
    ppermute x9, starting transfers between devices, first(): return lax.ppermute(v, ALL, shifts(k, False))  10.9 us
    ppermute x9, waiting for transfers between devices, second(): return lax.ppermute(v, ALL, shifts(k, True))  10.5 us
    ppermute x9, starting transfers between devices, second(): return lax.ppermute(v, ALL, shifts(k, True))  8.82 us
    ppermute x1, starting transfers between devices, body(): ln = lax.ppermute(lat_down, ('band', 'patch'), down)  8.46 us
    ppermute x1, starting transfers between devices, body(): cn = lax.ppermute(far, ('band', 'patch'), down)  6.89 us
  transfers between devices with their start and end apart: 26, of which 16 were waited for; matrix products, arithmetic and copies ran while one was open for 0% of the time, Pallas kernels for 7%

profile of v4, /device:TPU:1, one launch (start us, length us, event | category | flops | bytes accessed | tf_op | source)
XLA Modules:
  0.0 145.8 jit_solution(3693030356368723024)
XLA Ops:
  0.7 3.4 %shard_map.103 = (bf16[528,512]{1,0:T(8,128)(2,1)}, bf16[512,512]{1,0:T(8,128)(2,1)}) custom-call(s32[4]{0:T(128)} %bitcast.22, s32[4]{0:T(128)} %tk.1, bf16[512,512]{1,0:T(8,128)(2,1)} %bitcast.16, bf16[7,512,512]{2,1,0:T(8,128)(2,1)} %w.13, s32[4,128]{1,0:T(4,128)} %bitcast.19), custom_call_target="tpu_custom_call" | custom-call | flops 268435456 | bytes 1000000 | tf_op jit(solution)/shard_map/pallas_call | solution.py:48
  4.1 2.1 %collective-permute-start = (bf16[528,512]{1,0:T(8,128)(2,1)}, bf16[528,512]{1,0:T(8,128)(2,1)S(1)}, u32[]{:S(2)}, u32[]{:S(2)}) collective-permute-start(bf16[528,512]{1,0:T(8,128)(2,1)} %get-tuple-element.59.p0), channel_id=1, source_target_pairs={{0,64},{1,17},{2,66},{3,19},{4,68},{5,21},{6,70},{7,23},{8,72},{9,... | collective-permute-start | bytes 1622024 | tf_op jit(solution)/shard_map/ppermute | solution.py:77
  6.2 1.4 collective-permute-start.2
  7.6 1.6 %collective-permute-start.1 = (bf16[528,512]{1,0:T(8,128)(2,1)}, bf16[528,512]{1,0:T(8,128)(2,1)S(1)}, u32[]{:S(2)}, u32[]{:S(2)}) collective-permute-start(bf16[528,512]{1,0:T(8,128)(2,1)} %get-tuple-element.59.p0), channel_id=1, source_target_pairs={{0,128},{1,33},{2,130},{3,35},{4,132},{5,37},{6,134},{7,39},{8,136... | collective-permute-start | bytes 1622024 | tf_op jit(solution)/shard_map/ppermute | solution.py:77
  9.4 2.0 %copy-done = bf16[7,512,512]{2,1,0:T(8,128)(2,1)S(1)} copy-done((bf16[7,512,512]{2,1,0:T(8,128)(2,1)S(1)}, bf16[7,512,512]{2,1,0:T(8,128)(2,1)}, u32[]{:S(2)}) %copy-start) | copy-done | bytes 3670040
  11.8 3.1 %collective-permute-done.p1 = bf16[528,512]{1,0:T(8,128)(2,1)S(1)} collective-permute-done((bf16[528,512]{1,0:T(8,128)(2,1)}, bf16[528,512]{1,0:T(8,128)(2,1)S(1)}, u32[]{:S(2)}, u32[]{:S(2)}) %collective-permute-start) | collective-permute-done | bytes 540704 | tf_op jit(solution)/shard_map/ppermute | solution.py:77
  14.9 6.9 %collective-permute-done.1.p2 = bf16[528,512]{1,0:T(8,128)(2,1)S(1)} collective-permute-done((bf16[528,512]{1,0:T(8,128)(2,1)}, bf16[528,512]{1,0:T(8,128)(2,1)S(1)}, u32[]{:S(2)}, u32[]{:S(2)}) %collective-permute-start.1) | collective-permute-done | bytes 540704 | tf_op jit(solution)/shard_map/ppermute | solution.py:77
  23.9 2.8 %collective-permute-start.4 = (bf16[256,512]{1,0:T(8,128)(2,1)S(1)}, bf16[256,512]{1,0:T(8,128)(2,1)S(1)}, u32[]{:S(2)}, u32[]{:S(2)}) collective-permute-start(bf16[256,512]{1,0:T(8,128)(2,1)S(1)} %get-tuple-element.68), channel_id=1, source_target_pairs={{0,32},{1,129},{2,34},{3,131},{4,36},{5,133},{6,38},{7,135},{8,40}... | collective-permute-start | bytes 786440 | tf_op jit(solution)/shard_map/ppermute | solution.py:81
  27.5 2.2 %collective-permute-done.3.r1 = bf16[256,512]{1,0:T(8,128)(2,1)S(1)} collective-permute-done((bf16[256,512]{1,0:T(8,128)(2,1)S(1)}, bf16[256,512]{1,0:T(8,128)(2,1)S(1)}, u32[]{:S(2)}, u32[]{:S(2)}) %collective-permute-start.3) | collective-permute-done | bytes 262176 | tf_op jit(solution)/shard_map/ppermute | solution.py:81
  29.7 3.8 %collective-permute-done.4.r2 = bf16[256,512]{1,0:T(8,128)(2,1)S(1)} collective-permute-done((bf16[256,512]{1,0:T(8,128)(2,1)S(1)}, bf16[256,512]{1,0:T(8,128)(2,1)S(1)}, u32[]{:S(2)}, u32[]{:S(2)}) %collective-permute-start.4) | collective-permute-done | bytes 262176 | tf_op jit(solution)/shard_map/ppermute | solution.py:81
  34.4 8.5 %collective-permute-start.7 = (bf16[272,512]{1,0:T(8,128)(2,1)S(1)}, bf16[272,512]{1,0:T(8,128)(2,1)S(1)}, u32[]{:S(2)}, u32[]{:S(2)}) collective-permute-start(bf16[272,512]{1,0:T(8,128)(2,1)S(1)} %get-tuple-element.73), channel_id=1, source_target_pairs={{2,0},{4,2},{6,4},{8,6},{10,8},{12,10},{14,12},{16,14},{18,16},{20... | collective-permute-start | bytes 835592 | tf_op jit(solution)/shard_map/ppermute | solution.py:433
  42.9 6.9 %collective-permute-start.9 = (bf16[256,512]{1,0:T(8,128)(2,1)S(1)}, bf16[256,512]{1,0:T(8,128)(2,1)S(1)}, u32[]{:S(2)}, u32[]{:S(2)}) collective-permute-start(bf16[256,512]{1,0:T(8,128)(2,1)S(1)} %bitcast.11), channel_id=1, source_target_pairs={{2,0},{4,2},{6,4},{8,6},{10,8},{12,10},{14,12},{16,14},{18,16},{20... | collective-permute-start | bytes 786440 | tf_op jit(solution)/shard_map/ppermute | solution.py:436
  50.2 3.5 %collective-permute-done.6.lp = bf16[272,512]{1,0:T(8,128)(2,1)S(1)} collective-permute-done((bf16[272,512]{1,0:T(8,128)(2,1)S(1)}, bf16[272,512]{1,0:T(8,128)(2,1)S(1)}, u32[]{:S(2)}, u32[]{:S(2)}) %collective-permute-start.6) | collective-permute-done | bytes 278560 | tf_op jit(solution)/shard_map/ppermute | solution.py:432
  53.7 2.9 %shard_map.109 = (bf16[256,512]{1,0:T(8,128)(2,1)S(1)}, bf16[256,512]{1,0:T(8,128)(2,1)S(1)}, f32[256,512]{1,0:T(8,128)S(1)}, f32[512,512]{1,0:T(8,128)S(1)}) custom-call(bf16[272,512]{1,0:T(8,128)(2,1)S(1)} %collective-permute-done.6.lp, bf16[272,512]{1,0:T(8,128)(2,1)S(1)} %collective-permute-done.7.ln, bf16[256,512]{1,0:T(8,128)(2,1)S(1)} %get-tuple-element.75.snd, ...), custom_call_target="tpu_custom_call" | custom-call | flops 2000000000 | bytes 1000000 | tf_op jit(solution)/shard_map/pallas_call | solution.py:48
  56.6 3.8 %collective-permute-done.8.cp = bf16[256,512]{1,0:T(8,128)(2,1)S(1)} collective-permute-done((bf16[256,512]{1,0:T(8,128)(2,1)S(1)}, bf16[256,512]{1,0:T(8,128)(2,1)S(1)}, u32[]{:S(2)}, u32[]{:S(2)}) %collective-permute-start.8) | collective-permute-done | bytes 262176 | tf_op jit(solution)/shard_map/ppermute | solution.py:435
  60.4 5.6 %shard_map.110 = (bf16[256,512]{1,0:T(8,128)(2,1)S(1)}, bf16[256,512]{1,0:T(8,128)(2,1)S(1)}, bf16[256,512]{1,0:T(8,128)(2,1)S(1)}, bf16[256,512]{1,0:T(8,128)(2...) custom-call(bf16[272,512]{1,0:T(8,128)(2,1)S(1)} %collective-permute-done.6.lp, ...), custom_call_target="tpu_custom_call" | custom-call | flops 3000000000 | bytes 1000000 | tf_op jit(solution)/shard_map/pallas_call | solution.py:48
  66.6 5.1 %collective-permute-start.17 = (bf16[6144,128]{1,0:T(8,128)(2,1)S(1)}, bf16[6144,128]{1,0:T(8,128)(2,1)S(1)}, u32[]{:S(2)}, u32[]{:S(2)}) collective-permute-start(bf16[6144,128]{1,0:T(8,128)(2,1)S(1)} %shard_map.115), channel_id=1, source_target_pairs={{0,1},{1,0},{2,3},{3,2},{4,5},{5,4},{6,7},{7,6},{8,9},{9,8},{10,11... | collective-permute-start | bytes 4718600 | tf_op jit(solution)/shard_map/ppermute | solution.py:478
  71.7 1.5 %collective-permute-start.10 = (bf16[256,512]{1,0:T(8,128)(2,1)S(1)}, bf16[256,512]{1,0:T(8,128)(2,1)S(1)}, u32[]{:S(2)}, u32[]{:S(2)}) collective-permute-start(bf16[256,512]{1,0:T(8,128)(2,1)S(1)} %get-tuple-element.85), channel_id=1, source_target_pairs={{0,16},{1,65},{2,18},{3,67},{4,20},{5,69},{6,22},{7,71},{8,24},{9,... | collective-permute-start | bytes 786440 | tf_op jit(solution)/shard_map/ppermute | solution.py:81
  74.8 1.5 %shard_map.116 = (bf16[4096,128]{1,0:T(8,128)(2,1)}, bf16[2048,128]{1,0:T(8,128)(2,1)S(1)}) custom-call(bf16[6144,128]{1,0:T(8,128)(2,1)S(1)} %shard_map.114.a, bf16[6144,128]{1,0:T(8,128)(2,1)S(1)} %collective-permute-done.17.b), custom_call_target="tpu_custom_call" | custom-call | flops 1000000 | bytes 1000000 | tf_op jit(solution)/shard_map/pallas_call | solution.py:48
  76.2 3.6 %all-to-all-start = ((bf16[8,512,128]{2,1,0:T(8,128)(2,1)}), bf16[8,512,128]{2,1,0:T(8,128)(2,1)S(1)}, u32[]{:S(2)}, u32[]{:S(2)}) async-start(bf16[8,512,128]{2,1,0:T(8,128)(2,1)} %bitcast.9), calls=%async_computation | async-start | bytes 2097152 | tf_op jit(solution)/shard_map/all_to_all | solution.py:492
  79.8 1.7 %collective-permute-done.10.g1 = bf16[256,512]{1,0:T(8,128)(2,1)S(1)} collective-permute-done((bf16[256,512]{1,0:T(8,128)(2,1)S(1)}, bf16[256,512]{1,0:T(8,128)(2,1)S(1)}, u32[]{:S(2)}, u32[]{:S(2)}) %collective-permute-start.10) | collective-permute-done | bytes 262176 | tf_op jit(solution)/shard_map/ppermute | solution.py:81
  83.1 2.6 %collective-permute-start.15 = (bf16[512,512]{1,0:T(8,128)(2,1)S(1)}, bf16[512,512]{1,0:T(8,128)(2,1)S(1)}, u32[]{:S(2)}, u32[]{:S(2)}) collective-permute-start(bf16[512,512]{1,0:T(8,128)(2,1)S(1)} %get-tuple-element.89), channel_id=1, source_target_pairs={{0,192},{1,49},{2,194},{3,51},{4,196},{5,53},{6,198},{7,55},{8,200... | collective-permute-start | bytes 1572872 | tf_op jit(solution)/shard_map/ppermute | solution.py:77
  85.6 12.5 %collective-permute-done.13.r1 = bf16[512,512]{1,0:T(8,128)(2,1)S(1)} collective-permute-done((bf16[512,512]{1,0:T(8,128)(2,1)S(1)}, bf16[512,512]{1,0:T(8,128)(2,1)S(1)}, u32[]{:S(2)}, u32[]{:S(2)}) %collective-permute-start.13) | collective-permute-done | bytes 524320 | tf_op jit(solution)/shard_map/ppermute | solution.py:77
  98.7 1.4 shard_map.112
  100.1 2.2 %collective-permute-start.16 = (bf16[16,64,128]{2,1,0:T(8,128)(2,1)S(1)}, bf16[16,64,128]{2,1,0:T(8,128)(2,1)S(1)}, u32[]{:S(2)}, u32[]{:S(2)}) collective-permute-start(bf16[16,64,128]{2,1,0:T(8,128)(2,1)S(1)} %get-tuple-element.96), channel_id=1, source_target_pairs={{0,1},{1,0},{2,3},{3,2},{4,5},{5,4},{6,7},{7,6},{8,9},{9,8},{10,11... | collective-permute-start | bytes 786440 | tf_op jit(solution)/shard_map/ppermute | solution.py:501
  103.6 5.4 %all-to-all-done.zparts = bf16[8,512,128]{2,1,0:T(8,128)(2,1)S(1)} async-done(((bf16[8,512,128]{2,1,0:T(8,128)(2,1)}), bf16[8,512,128]{2,1,0:T(8,128)(2,1)S(1)}, u32[]{:S(2)}, u32[]{:S(2)}) %all-to-all-start) | async-done | bytes 1048608 | tf_op jit(solution)/shard_map/all_to_all | solution.py:492
  109.4 2.6 %collective-permute-start.20 = (bf16[896,128]{1,0:T(8,128)(2,1)S(1)}, bf16[896,128]{1,0:T(8,128)(2,1)S(1)}, u32[]{:S(2)}, u32[]{:S(2)}) collective-permute-start(bf16[896,128]{1,0:T(8,128)(2,1)S(1)} %get-tuple-element.110), channel_id=1, source_target_pairs={{0,192},{1,49},{2,194},{3,51},{4,196},{5,53},{6,198},{7,55},{8,200... | collective-permute-start | bytes 688136 | tf_op jit(solution)/shard_map/ppermute | solution.py:77
  112.0 6.2 %collective-permute-done.18.b = bf16[896,128]{1,0:T(8,128)(2,1)S(1)} collective-permute-done((bf16[896,128]{1,0:T(8,128)(2,1)S(1)}, bf16[896,128]{1,0:T(8,128)(2,1)S(1)}, u32[]{:S(2)}, u32[]{:S(2)}) %collective-permute-start.18) | collective-permute-done | bytes 229408 | tf_op jit(solution)/shard_map/ppermute | solution.py:77
  119.1 2.6 %collective-permute-start.23 = (bf16[224,128]{1,0:T(8,128)(2,1)S(1)}, bf16[224,128]{1,0:T(8,128)(2,1)S(1)}, u32[]{:S(2)}, u32[]{:S(2)}) collective-permute-start(bf16[224,128]{1,0:T(8,128)(2,1)S(1)} %get-tuple-element.114), channel_id=1, source_target_pairs={{0,48},{1,193},{2,50},{3,195},{4,52},{5,197},{6,54},{7,199},{8,56}... | collective-permute-start | bytes 172040 | tf_op jit(solution)/shard_map/ppermute | solution.py:81
  121.6 2.2 %collective-permute-done.21.b = bf16[224,128]{1,0:T(8,128)(2,1)S(1)} collective-permute-done((bf16[224,128]{1,0:T(8,128)(2,1)S(1)}, bf16[224,128]{1,0:T(8,128)(2,1)S(1)}, u32[]{:S(2)}, u32[]{:S(2)}) %collective-permute-start.21) | collective-permute-done | bytes 57376 | tf_op jit(solution)/shard_map/ppermute | solution.py:81
  124.4 14.5 %all_to_all.14.parts = bf16[8,224,128]{2,1,0:T(8,128)(2,1)S(1)} all-to-all(bf16[8,224,128]{2,1,0:T(8,128)(2,1)S(1)} %shard_map.119), channel_id=1, replica_groups=mesh['band'=16,'patch'=8,'rep'=2] {'patch'}, dimensions={0} | all-to-all | bytes 917504 | tf_op jit(solution)/shard_map/all_to_all | solution.py:519
  139.0 5.0 %collective-permute-start.24 = (bf16[448,128]{1,0:T(8,128)(2,1)S(1)}, bf16[448,128]{1,0:T(8,128)(2,1)S(1)}, u32[]{:S(2)}, u32[]{:S(2)}) collective-permute-start(bf16[448,128]{1,0:T(8,128)(2,1)S(1)} %shard_map.120.mine), channel_id=1, source_target_pairs={{0,1},{1,0},{2,3},{3,2},{4,5},{5,4},{6,7},{7,6},{8,9},{9,8},{10,11... | collective-permute-start | bytes 344072 | tf_op jit(solution)/shard_map/ppermute | solution.py:521
  (62 shorter events, 13.9 us)
Async XLA Ops:
  4.1 10.8 %collective-permute-start = (bf16[528,512]{1,0:T(8,128)(2,1)}, bf16[528,512]{1,0:T(8,128)(2,1)S(1)}, u32[]{:S(2)}, u32[]{:S(2)}) collective-permute-start(bf16[528,512]{1,0:T(8,128)(2,1)} %get-tuple-element.59.p0), channel_id=1, source_target_pairs={{0,64},{1,17},{2,66},{3,19},{4,68},{5,21},{6,70},{7,23},{8,72},{9,... | collective-permute-start | bytes 1622024 | tf_op jit(solution)/shard_map/ppermute | solution.py:77
  6.2 8.7 %collective-permute-start.2 = (bf16[528,512]{1,0:T(8,128)(2,1)}, bf16[528,512]{1,0:T(8,128)(2,1)S(1)}, u32[]{:S(2)}, u32[]{:S(2)}) collective-permute-start(bf16[528,512]{1,0:T(8,128)(2,1)} %get-tuple-element.59.p0), channel_id=1, source_target_pairs={{0,192},{1,49},{2,194},{3,51},{4,196},{5,53},{6,198},{7,55},{8,200... | collective-permute-start | bytes 1622024 | tf_op jit(solution)/shard_map/ppermute | solution.py:77
  7.6 14.2 %collective-permute-start.1 = (bf16[528,512]{1,0:T(8,128)(2,1)}, bf16[528,512]{1,0:T(8,128)(2,1)S(1)}, u32[]{:S(2)}, u32[]{:S(2)}) collective-permute-start(bf16[528,512]{1,0:T(8,128)(2,1)} %get-tuple-element.59.p0), channel_id=1, source_target_pairs={{0,128},{1,33},{2,130},{3,35},{4,132},{5,37},{6,134},{7,39},{8,136... | collective-permute-start | bytes 1622024 | tf_op jit(solution)/shard_map/ppermute | solution.py:77
  11.5 22.1 %copy-start.1 = (bf16[7,512,512]{2,1,0:T(8,128)(2,1)S(1)}, bf16[7,512,512]{2,1,0:T(8,128)(2,1)}, u32[]{:S(2)}) copy-start(bf16[7,512,512]{2,1,0:T(8,128)(2,1)} %w.13) | copy-start | bytes 11010052
  11.8 21.7 %copy-start.7 = (bf16[1,256,512]{2,1,0:T(8,128)(2,1)S(1)}, bf16[1,256,512]{2,1,0:T(8,128)(2,1)}, u32[]{:S(2)}) copy-start(bf16[1,256,512]{2,1,0:T(8,128)(2,1)} %param.9) | copy-start | bytes 786436
  22.9 6.8 %collective-permute-start.3 = (bf16[256,512]{1,0:T(8,128)(2,1)S(1)}, bf16[256,512]{1,0:T(8,128)(2,1)S(1)}, u32[]{:S(2)}, u32[]{:S(2)}) collective-permute-start(bf16[256,512]{1,0:T(8,128)(2,1)S(1)} %get-tuple-element.67), channel_id=1, source_target_pairs={{0,16},{1,65},{2,18},{3,67},{4,20},{5,69},{6,22},{7,71},{8,24},{9,... | collective-permute-start | bytes 786440 | tf_op jit(solution)/shard_map/ppermute | solution.py:81
  23.9 9.6 %collective-permute-start.4 = (bf16[256,512]{1,0:T(8,128)(2,1)S(1)}, bf16[256,512]{1,0:T(8,128)(2,1)S(1)}, u32[]{:S(2)}, u32[]{:S(2)}) collective-permute-start(bf16[256,512]{1,0:T(8,128)(2,1)S(1)} %get-tuple-element.68), channel_id=1, source_target_pairs={{0,32},{1,129},{2,34},{3,131},{4,36},{5,133},{6,38},{7,135},{8,40}... | collective-permute-start | bytes 786440 | tf_op jit(solution)/shard_map/ppermute | solution.py:81
  26.7 6.9 %collective-permute-start.5 = (bf16[256,512]{1,0:T(8,128)(2,1)S(1)}, bf16[256,512]{1,0:T(8,128)(2,1)S(1)}, u32[]{:S(2)}, u32[]{:S(2)}) collective-permute-start(bf16[256,512]{1,0:T(8,128)(2,1)S(1)} %get-tuple-element.69), channel_id=1, source_target_pairs={{0,48},{1,193},{2,50},{3,195},{4,52},{5,197},{6,54},{7,199},{8,56}... | collective-permute-start | bytes 786440 | tf_op jit(solution)/shard_map/ppermute | solution.py:81
  34.4 15.8 %collective-permute-start.7 = (bf16[272,512]{1,0:T(8,128)(2,1)S(1)}, bf16[272,512]{1,0:T(8,128)(2,1)S(1)}, u32[]{:S(2)}, u32[]{:S(2)}) collective-permute-start(bf16[272,512]{1,0:T(8,128)(2,1)S(1)} %get-tuple-element.73), channel_id=1, source_target_pairs={{2,0},{4,2},{6,4},{8,6},{10,8},{12,10},{14,12},{16,14},{18,16},{20... | collective-permute-start | bytes 835592 | tf_op jit(solution)/shard_map/ppermute | solution.py:433
  42.9 10.8 %collective-permute-start.6 = (bf16[272,512]{1,0:T(8,128)(2,1)S(1)}, bf16[272,512]{1,0:T(8,128)(2,1)S(1)}, u32[]{:S(2)}, u32[]{:S(2)}) collective-permute-start(bf16[272,512]{1,0:T(8,128)(2,1)S(1)} %get-tuple-element.72.lat), channel_id=1, source_target_pairs={{0,2},{2,4},{4,6},{6,8},{8,10},{10,12},{12,14},{14,16},{16,18},{18... | collective-permute-start | bytes 835592 | tf_op jit(solution)/shard_map/ppermute | solution.py:432
  42.9 13.8 %collective-permute-start.9 = (bf16[256,512]{1,0:T(8,128)(2,1)S(1)}, bf16[256,512]{1,0:T(8,128)(2,1)S(1)}, u32[]{:S(2)}, u32[]{:S(2)}) collective-permute-start(bf16[256,512]{1,0:T(8,128)(2,1)S(1)} %bitcast.11), channel_id=1, source_target_pairs={{2,0},{4,2},{6,4},{8,6},{10,8},{12,10},{14,12},{16,14},{18,16},{20... | collective-permute-start | bytes 786440 | tf_op jit(solution)/shard_map/ppermute | solution.py:436
  49.8 10.7 %collective-permute-start.8 = (bf16[256,512]{1,0:T(8,128)(2,1)S(1)}, bf16[256,512]{1,0:T(8,128)(2,1)S(1)}, u32[]{:S(2)}, u32[]{:S(2)}) collective-permute-start(bf16[256,512]{1,0:T(8,128)(2,1)S(1)} %bitcast.12), channel_id=1, source_target_pairs={{0,2},{2,4},{4,6},{6,8},{8,10},{10,12},{12,14},{14,16},{16,18},{18... | collective-permute-start | bytes 786440 | tf_op jit(solution)/shard_map/ppermute | solution.py:435
  66.6 8.1 %collective-permute-start.17 = (bf16[6144,128]{1,0:T(8,128)(2,1)S(1)}, bf16[6144,128]{1,0:T(8,128)(2,1)S(1)}, u32[]{:S(2)}, u32[]{:S(2)}) collective-permute-start(bf16[6144,128]{1,0:T(8,128)(2,1)S(1)} %shard_map.115), channel_id=1, source_target_pairs={{0,1},{1,0},{2,3},{3,2},{4,5},{5,4},{6,7},{7,6},{8,9},{9,8},{10,11... | collective-permute-start | bytes 4718600 | tf_op jit(solution)/shard_map/ppermute | solution.py:478
  71.7 8.1 %collective-permute-start.12 = (bf16[256,512]{1,0:T(8,128)(2,1)S(1)}, bf16[256,512]{1,0:T(8,128)(2,1)S(1)}, u32[]{:S(2)}, u32[]{:S(2)}) collective-permute-start(bf16[256,512]{1,0:T(8,128)(2,1)S(1)} %get-tuple-element.85), channel_id=1, source_target_pairs={{0,48},{1,193},{2,50},{3,195},{4,52},{5,197},{6,54},{7,199},{8,56}... | collective-permute-start | bytes 786440 | tf_op jit(solution)/shard_map/ppermute | solution.py:81
  71.7 8.1 %collective-permute-start.11 = (bf16[256,512]{1,0:T(8,128)(2,1)S(1)}, bf16[256,512]{1,0:T(8,128)(2,1)S(1)}, u32[]{:S(2)}, u32[]{:S(2)}) collective-permute-start(bf16[256,512]{1,0:T(8,128)(2,1)S(1)} %get-tuple-element.85), channel_id=1, source_target_pairs={{0,32},{1,129},{2,34},{3,131},{4,36},{5,133},{6,38},{7,135},{8,40}... | collective-permute-start | bytes 786440 | tf_op jit(solution)/shard_map/ppermute | solution.py:81
  71.7 9.8 %collective-permute-start.10 = (bf16[256,512]{1,0:T(8,128)(2,1)S(1)}, bf16[256,512]{1,0:T(8,128)(2,1)S(1)}, u32[]{:S(2)}, u32[]{:S(2)}) collective-permute-start(bf16[256,512]{1,0:T(8,128)(2,1)S(1)} %get-tuple-element.85), channel_id=1, source_target_pairs={{0,16},{1,65},{2,18},{3,67},{4,20},{5,69},{6,22},{7,71},{8,24},{9,... | collective-permute-start | bytes 786440 | tf_op jit(solution)/shard_map/ppermute | solution.py:81
  76.2 32.8 %all-to-all-start = ((bf16[8,512,128]{2,1,0:T(8,128)(2,1)}), bf16[8,512,128]{2,1,0:T(8,128)(2,1)S(1)}, u32[]{:S(2)}, u32[]{:S(2)}) async-start(bf16[8,512,128]{2,1,0:T(8,128)(2,1)} %bitcast.9), calls=%async_computation | async-start | bytes 2097152 | tf_op jit(solution)/shard_map/all_to_all | solution.py:492
  81.6 17.2 %copy-start.6 = (bf16[512,512]{1,0:T(8,128)(2,1)S(1)}, bf16[512,512]{1,0:T(8,128)(2,1)}, u32[]{:S(2)}) copy-start(bf16[512,512]{1,0:T(8,128)(2,1)} %get-tuple-element.90.slope) | copy-start | bytes 1572868
  81.6 17.2 %copy-start.8 = (s32[512]{0:T(512)S(1)}, s32[512]{0:T(512)}, u32[]{:S(2)}) copy-start(s32[512]{0:T(512)} %param.13) | copy-start | bytes 6148
  81.6 17.2 %copy-start.10 = (s32[4,1]{0,1:T(1,128)S(1)}, s32[4,1]{0,1:T(1,128)}, u32[]{:S(2)}) copy-start(s32[4,1]{0,1:T(1,128)} %param.11) | copy-start | bytes 52
  81.6 20.8 %copy-start.2 = (bf16[7,512,512]{2,1,0:T(8,128)(2,1)S(1)}, bf16[7,512,512]{2,1,0:T(8,128)(2,1)}, u32[]{:S(2)}) copy-start(bf16[7,512,512]{2,1,0:T(8,128)(2,1)} %w.13) | copy-start | bytes 11010052
  82.6 15.5 %collective-permute-start.13 = (bf16[512,512]{1,0:T(8,128)(2,1)S(1)}, bf16[512,512]{1,0:T(8,128)(2,1)S(1)}, u32[]{:S(2)}, u32[]{:S(2)}) collective-permute-start(bf16[512,512]{1,0:T(8,128)(2,1)S(1)} %get-tuple-element.87), channel_id=1, source_target_pairs={{0,64},{1,17},{2,66},{3,19},{4,68},{5,21},{6,70},{7,23},{8,72},{9,... | collective-permute-start | bytes 1572872 | tf_op jit(solution)/shard_map/ppermute | solution.py:77
  83.0 15.1 %collective-permute-start.14 = (bf16[512,512]{1,0:T(8,128)(2,1)S(1)}, bf16[512,512]{1,0:T(8,128)(2,1)S(1)}, u32[]{:S(2)}, u32[]{:S(2)}) collective-permute-start(bf16[512,512]{1,0:T(8,128)(2,1)S(1)} %get-tuple-element.88), channel_id=1, source_target_pairs={{0,128},{1,33},{2,130},{3,35},{4,132},{5,37},{6,134},{7,39},{8,136... | collective-permute-start | bytes 1572872 | tf_op jit(solution)/shard_map/ppermute | solution.py:77
  83.1 15.7 %collective-permute-start.15 = (bf16[512,512]{1,0:T(8,128)(2,1)S(1)}, bf16[512,512]{1,0:T(8,128)(2,1)S(1)}, u32[]{:S(2)}, u32[]{:S(2)}) collective-permute-start(bf16[512,512]{1,0:T(8,128)(2,1)S(1)} %get-tuple-element.89), channel_id=1, source_target_pairs={{0,192},{1,49},{2,194},{3,51},{4,196},{5,53},{6,198},{7,55},{8,200... | collective-permute-start | bytes 1572872 | tf_op jit(solution)/shard_map/ppermute | solution.py:77
  100.1 3.5 %collective-permute-start.16 = (bf16[16,64,128]{2,1,0:T(8,128)(2,1)S(1)}, bf16[16,64,128]{2,1,0:T(8,128)(2,1)S(1)}, u32[]{:S(2)}, u32[]{:S(2)}) collective-permute-start(bf16[16,64,128]{2,1,0:T(8,128)(2,1)S(1)} %get-tuple-element.96), channel_id=1, source_target_pairs={{0,1},{1,0},{2,3},{3,2},{4,5},{5,4},{6,7},{7,6},{8,9},{9,8},{10,11... | collective-permute-start | bytes 786440 | tf_op jit(solution)/shard_map/ppermute | solution.py:501
  109.2 8.9 %collective-permute-start.18 = (bf16[896,128]{1,0:T(8,128)(2,1)S(1)}, bf16[896,128]{1,0:T(8,128)(2,1)S(1)}, u32[]{:S(2)}, u32[]{:S(2)}) collective-permute-start(bf16[896,128]{1,0:T(8,128)(2,1)S(1)} %get-tuple-element.108), channel_id=1, source_target_pairs={{0,64},{1,17},{2,66},{3,19},{4,68},{5,21},{6,70},{7,23},{8,72},{9,... | collective-permute-start | bytes 688136 | tf_op jit(solution)/shard_map/ppermute | solution.py:77
  109.3 8.8 %collective-permute-start.19 = (bf16[896,128]{1,0:T(8,128)(2,1)S(1)}, bf16[896,128]{1,0:T(8,128)(2,1)S(1)}, u32[]{:S(2)}, u32[]{:S(2)}) collective-permute-start(bf16[896,128]{1,0:T(8,128)(2,1)S(1)} %get-tuple-element.109), channel_id=1, source_target_pairs={{0,128},{1,33},{2,130},{3,35},{4,132},{5,37},{6,134},{7,39},{8,136... | collective-permute-start | bytes 688136 | tf_op jit(solution)/shard_map/ppermute | solution.py:77
  109.4 9.3 %collective-permute-start.20 = (bf16[896,128]{1,0:T(8,128)(2,1)S(1)}, bf16[896,128]{1,0:T(8,128)(2,1)S(1)}, u32[]{:S(2)}, u32[]{:S(2)}) collective-permute-start(bf16[896,128]{1,0:T(8,128)(2,1)S(1)} %get-tuple-element.110), channel_id=1, source_target_pairs={{0,192},{1,49},{2,194},{3,51},{4,196},{5,53},{6,198},{7,55},{8,200... | collective-permute-start | bytes 688136 | tf_op jit(solution)/shard_map/ppermute | solution.py:77
  118.9 4.9 %collective-permute-start.21 = (bf16[224,128]{1,0:T(8,128)(2,1)S(1)}, bf16[224,128]{1,0:T(8,128)(2,1)S(1)}, u32[]{:S(2)}, u32[]{:S(2)}) collective-permute-start(bf16[224,128]{1,0:T(8,128)(2,1)S(1)} %get-tuple-element.112), channel_id=1, source_target_pairs={{0,16},{1,65},{2,18},{3,67},{4,20},{5,69},{6,22},{7,71},{8,24},{9,... | collective-permute-start | bytes 172040 | tf_op jit(solution)/shard_map/ppermute | solution.py:81
  119.0 4.8 %collective-permute-start.22 = (bf16[224,128]{1,0:T(8,128)(2,1)S(1)}, bf16[224,128]{1,0:T(8,128)(2,1)S(1)}, u32[]{:S(2)}, u32[]{:S(2)}) collective-permute-start(bf16[224,128]{1,0:T(8,128)(2,1)S(1)} %get-tuple-element.113), channel_id=1, source_target_pairs={{0,32},{1,129},{2,34},{3,131},{4,36},{5,133},{6,38},{7,135},{8,40}... | collective-permute-start | bytes 172040 | tf_op jit(solution)/shard_map/ppermute | solution.py:81
  119.1 5.3 %collective-permute-start.23 = (bf16[224,128]{1,0:T(8,128)(2,1)S(1)}, bf16[224,128]{1,0:T(8,128)(2,1)S(1)}, u32[]{:S(2)}, u32[]{:S(2)}) collective-permute-start(bf16[224,128]{1,0:T(8,128)(2,1)S(1)} %get-tuple-element.114), channel_id=1, source_target_pairs={{0,48},{1,193},{2,50},{3,195},{4,52},{5,197},{6,54},{7,199},{8,56}... | collective-permute-start | bytes 172040 | tf_op jit(solution)/shard_map/ppermute | solution.py:81
  139.0 6.0 %collective-permute-start.24 = (bf16[448,128]{1,0:T(8,128)(2,1)S(1)}, bf16[448,128]{1,0:T(8,128)(2,1)S(1)}, u32[]{:S(2)}, u32[]{:S(2)}) collective-permute-start(bf16[448,128]{1,0:T(8,128)(2,1)S(1)} %shard_map.120.mine), channel_id=1, source_target_pairs={{0,1},{1,0},{2,3},{3,2},{4,5},{5,4},{6,7},{7,6},{8,9},{9,8},{10,11... | collective-permute-start | bytes 344072 | tf_op jit(solution)/shard_map/ppermute | solution.py:521
  (5 other events, 47.0 us)
